TPU v7x, 128 devices: a whole 4x4x4 slice. The times are simulated.
128 devices in a mesh: seq: 16 (over x_hi, z, core), head: 8 (over y, x_lo).
Axes of the slice: x: 4 (x_hi: 2, x_lo: 2; x = x_hi * 2 + x_lo), y: 4, z: 4, core: 2. Of those that a mesh axis runs over, the one named last changes fastest.
Arguments:
- hidden_low: bfloat16 [2048, 4096], P('seq'), may hold values from -2 to 2
- query_low: bfloat16 [2048, 4096], P('seq', 'head'), may hold values from -48 to 48
- key_low: bfloat16 [2048, 4096], P('seq', 'head'), may hold values from -10 to 10
- value_low: bfloat16 [2048, 4096], P('seq', 'head'), may hold values from -6 to 6
- out_weight: bfloat16 [4096, 4096], P('head'), may hold values from -0.09375 to 0.09375
- latent_weight: bfloat16 [4096, 128], replicated, may hold values from -0.09375 to 0.09375
- conv_first: bfloat16 [3, 3, 3, 128, 512], replicated, may hold values from -0.109375 to 0.109375
- bias_first: float32 [512], replicated, may hold values from -3 to 3
- conv_second: bfloat16 [512, 512], replicated, may hold values from -0.25 to 0.25
- bias_second: float32 [512], replicated, may hold values from -3 to 3
- query_weight: bfloat16 [128, 4096], replicated, may hold values from -0.36 to 0.36
- key_weight: bfloat16 [128, 4096], replicated, may hold values from -0.36 to 0.36
- value_weight: bfloat16 [128, 4096], replicated, may hold values from -0.5 to 0.5
- query_gain: float32 [4096], replicated, may hold values from 0.1 to 6.3
- key_gain: float32 [4096], replicated, may hold values from 0.1 to 6.3
Outputs:
- hires_attention: bfloat16 [8192, 4096], P('seq', 'head')
- upsampled: bfloat16 [8192, 128], P(('seq', 'head'))
All inputs are finite; a program needn't handle non-finite values.
Results may differ from a plain program's by a relative error of at most 0.04.
Values may be sent and summed in bfloat16 or wider, within the bound.
No kernel may reach another device: no remote copies, remote signals or barrier semaphores. Data moves between devices by JAX's collectives and lax.ppermute only.
A program may use at most 192 MiB of HBM per device.

v0:
```python
import math

import jax
import jax.numpy as jnp
from jax import lax
from jax.sharding import PartitionSpec as P

HD = 128
H_LO = 4
W_LO = 32


def with_halo(block, sides, width):
    for axis, dim in sides:
        count = lax.axis_size(axis)
        forward = [(i, i + 1) for i in range(count - 1)]
        backward = [(target, source) for source, target in forward]
        low = lax.ppermute(
            lax.slice_in_dim(block, block.shape[dim] - width, None, axis=dim), axis, forward
        )
        high = lax.ppermute(lax.slice_in_dim(block, 0, width, axis=dim), axis, backward)
        block = jnp.concatenate([low, block, high], axis=dim)
    return block


def start_carry(row_count, head_count):
    return (
        jnp.full((head_count, row_count), -1e30, jnp.float32),
        jnp.zeros((head_count, row_count), jnp.float32),
        jnp.zeros((head_count, row_count, HD), jnp.float32),
    )


def attend_step(running, queries, key_block, value_block):
    running_max, totals, numerator = running
    query_count = queries.shape[0]
    key_count = key_block.shape[0]
    head_count = queries.shape[1] // HD
    query_heads = queries.reshape(query_count, head_count, HD)
    key_heads = key_block.reshape(key_count, head_count, HD)
    value_heads = value_block.reshape(key_count, head_count, HD)
    scores = jnp.einsum(
        "qhd,khd->hqk", query_heads, key_heads, preferred_element_type=jnp.float32
    ) * (1.0 / math.sqrt(HD))
    newest = jnp.maximum(running_max, jnp.max(scores, axis=2))
    weights = jnp.exp(scores - newest[:, :, None])
    totals = jnp.sum(weights, axis=2)
    numerator = jnp.einsum(
        "hqk,khd->hqd",
        weights.astype(jnp.bfloat16),
        value_heads,
        preferred_element_type=jnp.float32,
    )
    return (newest, totals, numerator)


def attend_finish(running):
    running_max, totals, numerator = running
    result = numerator / totals[:, :, None]
    head_count, row_count = totals.shape
    return result.transpose(1, 0, 2).reshape(row_count, head_count * HD).astype(jnp.bfloat16)


def normed(projected, gain):
    return (
        projected * lax.rsqrt(jnp.mean(projected * projected, axis=1, keepdims=True) + 1e-06) * gain
    )


def upsample_frame(window, frame_low, conv_first, bias_first, conv_second, bias_second):
    rows_low = frame_low.shape[0]
    cols_low = frame_low.shape[1]
    channels = frame_low.shape[2]
    padded = jnp.pad(window, ((0, 0), (1, 1), (1, 1), (0, 0)))
    patches = []
    for frame_off in range(3):
        for row_off in range(3):
            for col_off in range(3):
                patches.append(
                    padded[frame_off, row_off : row_off + rows_low, col_off : col_off + cols_low, :]
                )
    stacked = jnp.concatenate(patches, axis=2).reshape(rows_low * cols_low, 27 * channels)
    kernel = conv_first.reshape(27 * channels, conv_first.shape[4])
    middle = jax.nn.silu(
        jnp.dot(stacked, kernel, preferred_element_type=jnp.float32) + bias_first
    ).astype(jnp.bfloat16)
    sub_pixels = jnp.dot(middle, conv_second, preferred_element_type=jnp.float32) + bias_second
    sub_pixels = sub_pixels.reshape(rows_low, cols_low, 2, 2, channels).transpose(0, 2, 1, 3, 4)
    sub_pixels = sub_pixels.reshape(2 * rows_low, 2 * cols_low, channels)
    nearest = jnp.repeat(jnp.repeat(frame_low.astype(jnp.float32), 2, axis=0), 2, axis=1)
    return (sub_pixels + nearest).astype(jnp.bfloat16)


def local(
    hidden_low,
    query_low,
    key_low,
    value_low,
    out_weight,
    latent_weight,
    conv_first,
    bias_first,
    conv_second,
    bias_second,
    query_weight,
    key_weight,
    value_weight,
    query_gain,
    key_gain,
):
    head_total = lax.axis_size("head")
    head_index = lax.axis_index("head")
    local_width = query_low.shape[1]
    channels = latent_weight.shape[1]
    blocks = (
        lax.all_gather(key_low, "seq", axis=0, tiled=True),
        lax.all_gather(value_low, "seq", axis=0, tiled=True),
    )
    low_state = attend_step(
        start_carry(query_low.shape[0], local_width // HD), query_low, blocks[0], blocks[1]
    )
    attn_low = attend_finish(low_state)
    partial_value = jnp.dot(attn_low, out_weight, preferred_element_type=jnp.float32)
    summed = lax.psum(partial_value.astype(jnp.bfloat16), "head").astype(jnp.float32)
    mixture = (hidden_low.astype(jnp.float32) + summed).astype(jnp.bfloat16)
    latent = jnp.dot(mixture, latent_weight, preferred_element_type=jnp.float32).astype(
        jnp.bfloat16
    )
    frame_low = latent.reshape(1, H_LO, W_LO, channels)
    window = with_halo(frame_low, (("seq", 0),), 1)
    high_frame = upsample_frame(
        window, frame_low[0], conv_first, bias_first, conv_second, bias_second
    )
    high_rows = 2 * H_LO // head_total
    tile_latent = lax.dynamic_slice_in_dim(
        high_frame, head_index * high_rows, high_rows, 0
    ).reshape(high_rows * 2 * W_LO, channels)
    hi_query = normed(
        jnp.dot(tile_latent, query_weight, preferred_element_type=jnp.float32), query_gain
    ).astype(jnp.bfloat16)
    hi_key = normed(
        jnp.dot(tile_latent, key_weight, preferred_element_type=jnp.float32), key_gain
    ).astype(jnp.bfloat16)
    hi_value = jnp.dot(tile_latent, value_weight, preferred_element_type=jnp.float32).astype(
        jnp.bfloat16
    )
    head_query, head_key, head_value = (
        lax.all_to_all(hi_query, "head", split_axis=1, concat_axis=0, tiled=True),
        lax.all_to_all(hi_key, "head", split_axis=1, concat_axis=0, tiled=True),
        lax.all_to_all(hi_value, "head", split_axis=1, concat_axis=0, tiled=True),
    )
    blocks = (
        lax.all_gather(head_key, "seq", axis=0, tiled=True),
        lax.all_gather(head_value, "seq", axis=0, tiled=True),
    )
    high_state = attend_step(
        start_carry(head_query.shape[0], local_width // HD), head_query, blocks[0], blocks[1]
    )
    return (attend_finish(high_state), tile_latent)


def solution(mesh):
    placed = (
        P("seq", None),
        P("seq", "head"),
        P("seq", "head"),
        P("seq", "head"),
        P("head", None),
        P(),
        P(),
        P(),
        P(),
        P(),
        P(),
        P(),
        P(),
        P(),
        P(),
    )
    return jax.shard_map(
        local,
        mesh=mesh,
        in_specs=placed,
        out_specs=(P("seq", "head"), P(("seq", "head"), None)),
        check_vma=False,
    )
```

profile of v0, /device:TPU:1, one launch (start us, length us, event | category | flops | bytes accessed | tf_op | source)
XLA Modules:
  0.0 432.0 jit_solution(15380311760030277334)
XLA Ops:
  7.2 0.0 copy-start
  7.2 0.0 all-gather.5.cloned.1.call-start
  7.2 1.8 copy.20
  9.0 0.0 all-gather.5.cloned.1.call-update
  9.1 0.0 all-gather.7.cloned.1.call-start
  9.1 0.7 all-gather.7.cloned.1.call-update
  9.8 0.0 all-reduce.3.cloned.1.call-start
  9.9 51.8 %all-gather.5.cloned.1.call-done = bf16[2048,512]{0,1:T(8,128)(2,1)} async-done(((bf16[128,512]{0,1:T(8,128)(2,1)}), bf16[2048,512]{0,1:T(8,128)(2,1)}) %all-gather.5.cloned.1.call-update) | async-done | bytes 2097168 | tf_op jit(solution)/shard_map/all_gather | solution.py:116
  61.7 2.5 multiply_reduce_fusion.1
  64.2 1.9 copy-done.2
  66.1 0.8 fusion.4
  66.9 42.9 %all-gather.7.cloned.1.call-done = bf16[2048,512]{1,0:T(8,128)(2,1)} async-done(((bf16[128,512]{1,0:T(8,128)(2,1)}), bf16[2048,512]{1,0:T(8,128)(2,1)}) %all-gather.7.cloned.1.call-update) | async-done | bytes 2097168 | tf_op jit(solution)/shard_map/all_gather | solution.py:117
  109.9 4.0 copy.23
  113.8 4.0 fusion.25
  117.9 0.0 copy-done.3
  117.9 1.7 convolution_convert_fusion
  119.6 0.0 all-reduce.3.cloned.1.call-update
  119.6 0.0 all-gather.9.cloned.1.call-start
  119.7 74.7 %all-reduce.3.cloned.1.call-done = bf16[128,4096]{1,0:T(8,128)(2,1)} async-done(((bf16[128,4096]{1,0:T(8,128)(2,1)}), bf16[128,4096]{1,0:T(8,128)(2,1)}) %all-reduce.3.cloned.1.call-update) | async-done | bytes 1048592 | tf_op jit(solution)/shard_map/psum | solution.py:124
  194.4 2.9 convolution_convert_fusion.2
  197.3 8.1 %collective-permute-start = (bf16[1,4,32,128]{3,2,1,0:T(8,128)(2,1)}, bf16[1,4,32,128]{3,2,1,0:T(8,128)(2,1)}, u32[]{:S(2)}, u32[]{:S(2)}) collective-permute-start(bf16[1,4,32,128]{3,2,1,0:T(8,128)(2,1)} %bitcast.5), channel_id=1, source_target_pairs={{0,8},{8,16},{16,24},{24,32},{32,40},{40,48},{48,56},{56,64},{64,7... | collective-permute-start | bytes 98312 | tf_op jit(solution)/shard_map/ppermute | solution.py:18
  205.4 1.9 collective-permute-start.1
  207.3 0.0 collective-permute-done
  207.3 3.6 collective-permute-done.1
  211.0 0.8 select_maximum_fusion
  211.8 0.1 fusion.46
  212.0 0.8 constant_dynamic-update-slice_fusion.22
  212.9 0.8 constant_dynamic-update-slice_fusion.13
  213.8 0.8 constant_dynamic-update-slice_fusion.4
  214.7 0.0 copy-start.8
  214.7 0.9 copy-done.8
  215.6 0.0 copy-done
  215.6 2.9 convolution_add_fusion
  218.5 1.1 reshape.148
  219.6 0.1 copy.24
  219.7 0.8 broadcast_in_dim.9
  220.5 0.1 broadcast_in_dim.10
  220.6 0.0 copy-start.5
  220.6 1.6 multiply_reduce_fusion.2
  222.3 0.0 copy-done.6
  222.3 0.0 copy-start.4
  222.3 0.2 multiply_convert_fusion
  222.5 0.0 copy-start.7
  222.5 12.3 %all_to_all.54 = bf16[64,8,512]{2,0,1:T(8,128)(2,1)} all-to-all(bf16[64,8,512]{2,0,1:T(8,128)(2,1)S(1)} %bitcast.112), channel_id=1, replica_groups=mesh['seq'=16,'head'=8] {'head'}, dimensions={1} | all-to-all | bytes 1048576 | tf_op jit(solution)/shard_map/all_to_all | solution.py:149
  234.8 0.0 all-gather.9.cloned.1.call-update
  234.9 0.0 all-gather.11.cloned.1.call-start
  234.9 1.5 convolution_convert_fusion.1
  236.5 13.9 %all_to_all.55 = bf16[64,8,512]{2,0,1:T(8,128)(2,1)} all-to-all(bf16[64,8,512]{2,0,1:T(8,128)(2,1)S(1)} %bitcast.113), channel_id=1, replica_groups=mesh['seq'=16,'head'=8] {'head'}, dimensions={1} | all-to-all | bytes 1048576 | tf_op jit(solution)/shard_map/all_to_all | solution.py:150
  250.4 0.0 all-gather.11.cloned.1.call-update
  250.4 0.0 copy-done.5
  250.4 0.0 copy-done.4
  250.4 0.4 multiply_reduce_fusion.3
  250.8 0.0 copy-done.7
  250.8 0.2 multiply_convert_fusion.1
  251.1 12.4 %all_to_all.56 = bf16[64,8,512]{2,0,1:T(8,128)(2,1)S(1)} all-to-all(bf16[64,8,512]{2,0,1:T(8,128)(2,1)S(1)} %bitcast.114), channel_id=1, replica_groups=mesh['seq'=16,'head'=8] {'head'}, dimensions={1} | all-to-all | bytes 1048576 | tf_op jit(solution)/shard_map/all_to_all | solution.py:148
  263.5 0.1 reshape.153
  263.6 47.6 %all-gather.9.cloned.1.call-done = bf16[8192,512]{1,0:T(8,128)(2,1)} async-done(((bf16[512,512]{1,0:T(8,128)(2,1)}), bf16[8192,512]{1,0:T(8,128)(2,1)}) %all-gather.9.cloned.1.call-update) | async-done | bytes 8388624 | tf_op jit(solution)/shard_map/all_gather | solution.py:153
  311.2 12.0 %copy.27 = bf16[8192,512]{0,1:T(8,128)(2,1)} copy(bf16[8192,512]{1,0:T(8,128)(2,1)} %all-gather.9.cloned.1.call-done) | data formatting | bytes 16777216 | tf_op jit(solution)/shard_map/all_gather | solution.py:153
  323.2 27.7 %multiply_reduce_fusion = (f32[4,512]{1,0:T(4,128)S(1)}, f32[4,512,8192]{2,1,0:T(8,128)}) fusion(bf16[8192,4,128]{0,2,1:T(8,128)(2,1)} %bitcast.102, bf16[512,4,128]{2,1,0:T(4,128)(2,1)S(1)} %reshape.153), kind=kOutput, calls=%fused_computation.1 | convolution fusion | flops 4328519680 | bytes 76029952 | tf_op jit(solution)/shard_map/qhd,khd->hqk/dot_general | solution.py:42
  350.8 21.6 %fusion = f32[4,512]{1,0:T(4,128)S(1)} fusion(f32[4,512,8192]{2,1,0:T(8,128)} %get-tuple-element.37, f32[4,512]{1,0:T(4,128)S(1)} %broadcast_maximum_fusion), kind=kLoop, calls=%fused_computation.2 | loop fusion | flops 50329600 | bytes 67125248 | tf_op jit(solution)/shard_map/reduce_sum | solution.py:47
  372.4 11.9 %all-gather.11.cloned.1.call-done = bf16[8192,512]{1,0:T(8,128)(2,1)} async-done(((bf16[512,512]{1,0:T(8,128)(2,1)}), bf16[8192,512]{1,0:T(8,128)(2,1)}) %all-gather.11.cloned.1.call-update) | async-done | bytes 8388624 | tf_op jit(solution)/shard_map/all_gather | solution.py:154
  384.4 12.0 %copy.31 = bf16[8192,512]{0,1:T(8,128)(2,1)} copy(bf16[8192,512]{1,0:T(8,128)(2,1)} %all-gather.11.cloned.1.call-done) | data formatting | bytes 16777216 | tf_op jit(solution)/shard_map/all_gather | solution.py:154
  396.4 27.0 %fusion.16 = bf16[512,4,128]{0,2,1:T(8,128)(2,1)} fusion(bf16[8192,4,128]{0,2,1:T(8,128)(2,1)} %bitcast.103, f32[4,512,8192]{2,1,0:T(8,128)} %get-tuple-element.37, f32[4,512]{1,0:T(4,128)S(1)} %broadcast_maximum_fusion, f32[512,4]{0,1:T(4,128)S(1)} %bitcast.119), kind=kOutput, calls=%fused_computation.17 | convolution fusion | flops 4345823232 | bytes 76038144 | tf_op jit(solution)/shard_map/hqk,khd->hqd/dot_general | solution.py:48
  423.4 2.0 copy.32
  (38 shorter events, 0.5 us)
Async XLA Ops:
  7.2 208.4 %copy-start = (bf16[3,3,3,128,512]{4,3,2,1,0:T(8,128)(2,1)S(1)}, bf16[3,3,3,128,512]{4,3,2,1,0:T(8,128)(2,1)}, u32[]{:S(2)}) copy-start(bf16[3,3,3,128,512]{4,3,2,1,0:T(8,128)(2,1)} %param.21) | copy-start | bytes 10616836
  7.2 54.5 %all-gather.5.cloned.1.call-start = ((), (), s32[]{:S(2)}) async-start(), calls=%async_computation.3 | async-start | bytes 2228224 | tf_op jit(solution)/shard_map/all_gather | solution.py:116
  9.1 100.8 %all-gather.7.cloned.1.call-start = ((), (), s32[]{:S(2)}) async-start(), calls=%async_computation.4 | async-start | bytes 2228224 | tf_op jit(solution)/shard_map/all_gather | solution.py:117
  9.8 184.6 %all-reduce.3.cloned.1.call-start = ((), (), s32[]{:S(2)}) async-start(), calls=%async_computation.5 | async-start | bytes 2097152 | tf_op jit(solution)/shard_map/psum | solution.py:124
  64.1 2.0 copy-start.2
  113.8 4.1 copy-start.3
  119.6 191.6 %all-gather.9.cloned.1.call-start = ((), (), s32[]{:S(2)}) async-start(), calls=%async_computation.6 | async-start | bytes 8912896 | tf_op jit(solution)/shard_map/all_gather | solution.py:153
  197.3 10.1 %collective-permute-start = (bf16[1,4,32,128]{3,2,1,0:T(8,128)(2,1)}, bf16[1,4,32,128]{3,2,1,0:T(8,128)(2,1)}, u32[]{:S(2)}, u32[]{:S(2)}) collective-permute-start(bf16[1,4,32,128]{3,2,1,0:T(8,128)(2,1)} %bitcast.5), channel_id=1, source_target_pairs={{0,8},{8,16},{16,24},{24,32},{32,40},{40,48},{48,56},{56,64},{64,7... | collective-permute-start | bytes 98312 | tf_op jit(solution)/shard_map/ppermute | solution.py:18
  205.4 5.6 %collective-permute-start.1 = (bf16[1,4,32,128]{3,2,1,0:T(8,128)(2,1)}, bf16[1,4,32,128]{3,2,1,0:T(8,128)(2,1)}, u32[]{:S(2)}, u32[]{:S(2)}) collective-permute-start(bf16[1,4,32,128]{3,2,1,0:T(8,128)(2,1)} %bitcast.5), channel_id=1, source_target_pairs={{8,0},{16,8},{24,16},{32,24},{40,32},{48,40},{56,48},{64,56},{72,6... | collective-permute-start | bytes 98312 | tf_op jit(solution)/shard_map/ppermute | solution.py:21
  214.7 0.9 copy-start.8
  215.6 6.7 %copy-start.6 = (f32[4096]{0:T(1024)S(1)}, f32[4096]{0:T(1024)}, u32[]{:S(2)}) copy-start(f32[4096]{0:T(1024)} %param.29) | copy-start | bytes 49156
  220.6 29.8 %copy-start.5 = (bf16[64,128]{1,0:T(8,128)(2,1)}, bf16[64,128]{1,0:T(8,128)(2,1)S(1)}, u32[]{:S(2)}) copy-start(bf16[64,128]{1,0:T(8,128)(2,1)S(1)} %fusion.42) | copy-start | bytes 49156
  222.3 28.1 %copy-start.4 = (bf16[128,4096]{1,0:T(8,128)(2,1)S(1)}, bf16[128,4096]{1,0:T(8,128)(2,1)}, u32[]{:S(2)}) copy-start(bf16[128,4096]{1,0:T(8,128)(2,1)} %param.25) | copy-start | bytes 3145732
  222.5 28.3 %copy-start.7 = (f32[4096]{0:T(1024)S(1)}, f32[4096]{0:T(1024)}, u32[]{:S(2)}) copy-start(f32[4096]{0:T(1024)} %param.28) | copy-start | bytes 49156
  234.9 149.5 %all-gather.11.cloned.1.call-start = ((), (), s32[]{:S(2)}) async-start(), calls=%async_computation.7 | async-start | bytes 8912896 | tf_op jit(solution)/shard_map/all_gather | solution.py:154
  396.4 29.1 %copy-start.1 = (bf16[3,3,3,128,512]{4,3,2,1,0:T(8,128)(2,1)S(1)}, bf16[3,3,3,128,512]{4,3,2,1,0:T(8,128)(2,1)}, u32[]{:S(2)}) copy-start(bf16[3,3,3,128,512]{4,3,2,1,0:T(8,128)(2,1)} %param.21) | copy-start | bytes 10616836
Sparse Core Ops, SparseCore 0:
  10.9 50.7 all-gather.4
  64.1 45.6 all-gather.6
  119.8 74.5 all-reduce.2
  235.0 76.1 all-gather.8
  313.5 70.7 all-gather.10
where the time goes:
time: 433 us; the launch traced here: 432 us
  waiting for transfers between devices  233 us (54%)
  matrix products  72.3 us (17%)
  local copies, waits for them, and re-layouts  39.7 us (9%)
  blocking collectives  38.6 us (9%)
  other arithmetic  23.6 us (5%)
  between operations  14.1 us (3%)
  starting transfers between devices  10.3 us (2%)
    psum x1, waiting for transfers between devices, local(): lax.psum(partial_value.astype(jnp.bfloat16), 'head').astype(jnp.float32)  74.7 us
    all_gather x1, waiting for transfers between devices, local(): lax.all_gather(key_low, 'seq', axis=0, tiled=True)  51.8 us
    all_gather x1, waiting for transfers between devices, local(): lax.all_gather(head_key, 'seq', axis=0, tiled=True)  47.6 us
    all_gather x1, waiting for transfers between devices, local(): lax.all_gather(value_low, 'seq', axis=0, tiled=True)  42.9 us
    dot_general x2, matrix products, attend_step(): jnp.einsum('hqk,khd->hqd', weights.astype(jnp.bfloat16), value_heads, pre...  31.1 us
    dot_general x2, matrix products, attend_step(): jnp.einsum('qhd,khd->hqk', query_heads, key_heads, preferred_element_type...  30.1 us
    reduce_sum x2, other arithmetic, attend_step(): totals = jnp.sum(weights, axis=2)  22.4 us
    all_to_all x1, blocking collectives, local(): lax.all_to_all(hi_value, 'head', split_axis=1, concat_axis=0, tiled=True)  13.9 us
  transfers between devices with their start and end apart: 7, of which 6 were waited for; matrix products, arithmetic and copies ran while one was open for 15% of the time, Pallas kernels for 0%

commit v1 on v0

v1 whole, which is shorter than its diff:
```python
import functools
import math

import jax
import jax.numpy as jnp
from jax import lax
from jax.experimental import pallas as pl
from jax.experimental.pallas import tpu as pltpu
from jax.sharding import PartitionSpec as P

HD = 128
H_LO = 4
W_LO = 32
FRAMES = 16
TOK = H_LO * W_LO
KEYS = 4 * FRAMES * TOK
LOG2E = 1.4426950408889634
SCALE = LOG2E / math.sqrt(HD)
BF = jnp.bfloat16
F32 = jnp.float32
NT = (((1,), (1,)), ((), ()))


def dot(a, b):
    return jnp.dot(a, b, preferred_element_type=F32)


def dot_nt(a, b):
    return lax.dot_general(a, b, NT, preferred_element_type=F32)


def split2(x):
    high = x.astype(BF)
    low = (x - high.astype(F32)).astype(BF)
    return jnp.concatenate([high, low], axis=1)


def dot2(a, b2):
    both = dot(a, b2)
    half = both.shape[1] // 2
    return both[:, :half] + both[:, half:]


def whole(shape):
    return pl.BlockSpec(shape, lambda *_: (0,) * len(shape))


def pack_kernel(pos, q_ref, k_ref, v_ref, *outs):
    for shift, out in enumerate(outs):
        head = lax.rem(pos[1] + shift, 4)
        columns = pl.ds(pl.multiple_of(head * HD, HD), HD)
        out[:, 0:HD] = q_ref[:, columns]
        out[:, HD : 2 * HD] = k_ref[:, columns]
        out[:, 2 * HD : 3 * HD] = v_ref[:, columns]


def pack(pos, q, k, v):
    piece = jax.ShapeDtypeStruct((TOK, 3 * HD), BF)
    return pl.pallas_call(
        pack_kernel,
        grid_spec=pltpu.PrefetchScalarGridSpec(
            num_scalar_prefetch=1,
            grid=(1,),
            in_specs=[whole(q.shape)] * 3,
            out_specs=[whole(piece.shape)] * 4,
        ),
        out_shape=[piece] * 4,
        name="pack",
    )(pos, q, k, v)


def prep_kernel(pos, ow, lw, hid, wqh, wkh, gq, gk, wq, wk, w2_out, hl_out, m_out, gq_out, gk_out):
    del pos
    w2_out[...] = split2(dot(ow[...], lw[...]))
    hl_out[...] = dot(hid[...], lw[...])
    gain = gq[...] * gk[...]
    for head in range(4):
        cols = slice(head * HD, (head + 1) * HD)
        left = split2(wqh[:, cols].astype(F32) * gain[:, cols])
        right = wkh[:, cols]
        m_out[head] = split2(dot_nt(left[:, :HD], right) + dot_nt(left[:, HD:], right))
    gq_out[...] = split2(dot_nt(wq[...], wq[...]))
    gk_out[...] = split2(dot_nt(wk[...], wk[...]))


def prep(pos, out_weight, latent_weight, hidden, query_weight, key_weight, query_gain, key_gain):
    width = hidden.shape[1]
    share = TOK // 8
    group = 4 * HD
    return pl.pallas_call(
        prep_kernel,
        grid_spec=pltpu.PrefetchScalarGridSpec(
            num_scalar_prefetch=1,
            grid=(1,),
            in_specs=[
                pl.BlockSpec((HD, width), lambda i, pos: (pos[1], 0)),
                whole(latent_weight.shape),
                pl.BlockSpec((share, width), lambda i, pos: (pos[3], 0)),
                pl.BlockSpec((HD, group), lambda i, pos: (0, pos[3])),
                pl.BlockSpec((HD, group), lambda i, pos: (0, pos[3])),
                pl.BlockSpec((1, group), lambda i, pos: (0, pos[3])),
                pl.BlockSpec((1, group), lambda i, pos: (0, pos[3])),
                whole(query_weight.shape),
                whole(key_weight.shape),
            ],
            out_specs=[
                whole((HD, 2 * HD)),
                whole((share, HD)),
                whole((4, HD, 2 * HD)),
                whole((HD, 2 * HD)),
                whole((HD, 2 * HD)),
            ],
        ),
        out_shape=[
            jax.ShapeDtypeStruct((HD, 2 * HD), BF),
            jax.ShapeDtypeStruct((share, HD), F32),
            jax.ShapeDtypeStruct((4, HD, 2 * HD), BF),
            jax.ShapeDtypeStruct((HD, 2 * HD), BF),
            jax.ShapeDtypeStruct((HD, 2 * HD), BF),
        ],
        compiler_params=pltpu.CompilerParams(vmem_limit_bytes=24 * 2**20),
        cost_estimate=pl.CostEstimate(flops=900_000_000, bytes_accessed=5_000_000, transcendentals=0),
        name="prep",
    )(
        pos,
        out_weight,
        latent_weight,
        hidden,
        query_weight,
        key_weight,
        query_gain.reshape(1, -1),
        key_gain.reshape(1, -1),
        query_weight,
        key_weight,
    )


def low_kernel(pos, p0, p1, p2, p3, kv0, kv1, kv2, kv3, w2, hl, out, q_s, part_s):
    z = pos[1]
    for shift, piece in enumerate((p0, p1, p2, p3)):
        q_s[lax.rem(z + 4 - shift, 4)] = piece[:, 0:HD]
    for half in range(2):
        q = q_s[2 * half : 2 * half + 2].reshape(2 * TOK, HD)
        blocks = (kv0, kv1, kv2, kv3)
        scores = [dot_nt(q, kv[:, 0:HD]) * SCALE for kv in blocks]
        top = functools.reduce(jnp.maximum, [jnp.max(s, axis=1, keepdims=True) for s in scores])
        total = jnp.zeros((2 * TOK, 1), F32)
        numerator = jnp.zeros((2 * TOK, HD), F32)
        for s, kv in zip(scores, blocks):
            e = jnp.exp2(s - top)
            total = total + jnp.sum(e, axis=1, keepdims=True)
            numerator = numerator + dot(e.astype(BF), kv[:, HD : 2 * HD])
        attn = (numerator / total).astype(BF)
        part_s[2 * half * TOK : (2 * half + 2) * TOK, :] = dot2(attn, w2[...])
    share = TOK // 8
    rows = pl.ds(pl.multiple_of(z * TOK + pos[3] * share, share), share)
    part_s[rows, :] = part_s[rows, :] + hl[...]
    out[...] = part_s[...].astype(BF)


def low_attention(pos, pieces, kvs, w2, hl):
    args = (*pieces, *kvs, w2, hl)
    return pl.pallas_call(
        low_kernel,
        grid_spec=pltpu.PrefetchScalarGridSpec(
            num_scalar_prefetch=1,
            grid=(1,),
            in_specs=[whole(a.shape) for a in args],
            out_specs=whole((4 * TOK, HD)),
            scratch_shapes=[pltpu.VMEM((4, TOK, HD), BF), pltpu.VMEM((4 * TOK, HD), F32)],
        ),
        out_shape=jax.ShapeDtypeStruct((4 * TOK, HD), BF),
        compiler_params=pltpu.CompilerParams(vmem_limit_bytes=32 * 2**20),
        name="low",
    )(pos, *args)


CHUNK = 4
BLOCK = 2048
TINY = 2.0**-90


def hi_kernel(
    pos,
    lat0,
    lat1,
    lat2,
    lat3,
    conv,
    b1,
    second,
    b2,
    gq,
    gk,
    m,
    wv,
    attn_out,
    up_out,
    grid_s,
    lat_s,
    key_s,
    val_s,
    q_s,
    nat_s,
    acc_s,
    max_s,
):
    x, z, c, g = pos[0], pos[1], pos[2], pos[3]
    for dx, dc, piece in ((0, 0, lat0), (0, 1, lat1), (1, 0, lat2), (1, 1, lat3)):
        px = lax.bitwise_xor(x, dx)
        pc = lax.bitwise_xor(c, dc)
        for pz in range(4):
            lat_s[px * 8 + pz * 2 + pc] = piece[pz * TOK : (pz + 1) * TOK, :]
    grid_s[...] = jnp.zeros_like(grid_s)
    lat = lat_s[...].reshape(FRAMES * TOK, HD).astype(F32)
    column = lax.rem(lax.broadcasted_iota(jnp.int32, (FRAMES * TOK, HD), 0), W_LO)
    left = jnp.where(column == 0, 0.0, pltpu.roll(lat, 1, 0))
    right = jnp.where(column == W_LO - 1, 0.0, pltpu.roll(lat, FRAMES * TOK - 1, 0))
    for index, shifted in enumerate((left, lat, right)):
        grid_s[index, 1 : FRAMES + 1, 1 : H_LO + 1] = shifted.astype(BF).reshape(FRAMES, H_LO, W_LO, HD)

    val_s[:, HD : 2 * HD] = jnp.ones((KEYS, HD), BF)
    biggest = jnp.zeros((1, 1), F32)
    rows = CHUNK * TOK
    for first in range(0, FRAMES, CHUNK):
        taps = []
        for a in range(3):
            for b in range(3):
                for t in range(3):
                    taps.append(grid_s[t, first + a : first + a + CHUNK, b : b + H_LO].reshape(rows, HD))
        middle = dot(jnp.concatenate(taps, axis=1), conv[...]) + b1[...]
        middle = (middle / (1.0 + jnp.exp(-middle))).astype(BF)
        sub = dot(middle, second[...]) + b2[...]
        base = lat_s[first : first + CHUNK].reshape(rows, HD).astype(F32)
        for s in range(4):
            up = (sub[:, s * HD : (s + 1) * HD] + base).astype(BF)
            upf = up.astype(F32)
            square = jnp.sum(dot2(up, gk[...]) * upf, axis=1, keepdims=True)
            inverse = lax.rsqrt(jnp.maximum(square, 0.0) * (1.0 / 4096.0) + 1e-6)
            key = (upf * inverse).astype(BF)
            where = pl.ds(s * FRAMES * TOK + first * TOK, rows)
            val_s[where, 0:HD] = up
            key_s[where, :] = key
            keyf = key.astype(F32)
            length = jnp.sum(keyf * keyf, axis=1, keepdims=True)
            biggest = jnp.maximum(biggest, jnp.max(length, axis=0, keepdims=True))

    frame = x * 8 + z * 2 + c
    own = jnp.concatenate(
        [val_s[pl.ds(pl.multiple_of(s * FRAMES * TOK + frame * TOK, TOK), TOK), 0:HD] for s in range(4)], axis=0
    )
    to = lax.broadcasted_iota(jnp.int32, (4 * TOK, 4 * TOK), 0)
    source = lax.broadcasted_iota(jnp.int32, (4 * TOK, 4 * TOK), 1)
    row, col = to // (2 * W_LO), lax.rem(to, 2 * W_LO)
    wanted = (lax.rem(row, 2) * 2 + lax.rem(col, 2)) * TOK + (row // 2) * W_LO + col // 2
    natural = dot(jnp.where(source == wanted, 1.0, 0.0).astype(BF), own)
    nat_s[...] = natural
    up_out[...] = nat_s[pl.ds(pl.multiple_of(g * 2 * W_LO, 2 * W_LO), 2 * W_LO), :].astype(BF)
    mine = natural.astype(BF)
    square = jnp.sum(dot2(mine, gq[...]) * natural, axis=1, keepdims=True)
    inverse = lax.rsqrt(jnp.maximum(square, 0.0) * (1.0 / 4096.0) + 1e-6) * SCALE
    for head in range(4):
        q_s[head] = (dot2(mine, m[head]) * inverse).astype(BF)

    def one_head(head, carry):
        q = q_s[head]
        qf = q.astype(F32)
        bound = jnp.sqrt(jnp.sum(qf * qf, axis=1, keepdims=True) * biggest)

        def step(j, acc):
            keys = pl.ds(pl.multiple_of(j * BLOCK, BLOCK), BLOCK)
            scores = dot_nt(q, key_s[keys, :])
            return acc + dot(jnp.exp2(scores - bound).astype(BF), val_s[keys, :])

        acc = lax.fori_loop(0, KEYS // BLOCK, step, jnp.zeros((4 * TOK, 2 * HD), F32), unroll=2)
        acc_s[...] = acc
        weakest = jnp.min(acc[:, HD:])

        @pl.when(jnp.logical_not(weakest > TINY))
        def _():
            acc_s[...] = jnp.zeros_like(acc_s)
            max_s[...] = jnp.full_like(max_s, -1e30)

            def careful(j, carry):
                keys = pl.ds(pl.multiple_of(j * 512, 512), 512)
                scores = dot_nt(q_s[head], key_s[keys, :])
                before = max_s[:, 0:1]
                top = jnp.maximum(before, jnp.max(scores, axis=1, keepdims=True))
                weights = jnp.exp2(scores - top).astype(BF)
                acc_s[...] = acc_s[...] * jnp.exp2(before - top) + dot(weights, val_s[keys, :])
                max_s[...] = jnp.broadcast_to(top, max_s.shape)
                return carry

            lax.fori_loop(0, KEYS // 512, careful, 0)

        mixed = (acc_s[:, :HD] / acc_s[:, HD:]).astype(BF)
        columns = pl.ds(pl.multiple_of(head * HD, HD), HD)
        attn_out[:, columns] = dot(mixed, wv[:, columns]).astype(BF)
        return carry

    lax.fori_loop(0, 4, one_head, 0)


def hi_attention(pos, lats, conv_first, bias_first, conv_second, bias_second, gq, gk, m, value_weight):
    mid = conv_second.shape[0]
    conv = conv_first.reshape(27 * HD, mid)
    args = (*lats, conv, bias_first.reshape(1, -1), conv_second, bias_second.reshape(1, -1), gq, gk, m, value_weight)
    in_specs = [whole(a.shape) for a in args]
    in_specs[-1] = pl.BlockSpec((HD, 4 * HD), lambda i, pos: (0, pos[3]))
    return pl.pallas_call(
        hi_kernel,
        grid_spec=pltpu.PrefetchScalarGridSpec(
            num_scalar_prefetch=1,
            grid=(1,),
            in_specs=in_specs,
            out_specs=[whole((4 * TOK, 4 * HD)), whole((2 * W_LO, HD))],
            scratch_shapes=[
                pltpu.VMEM((3, FRAMES + 2, H_LO + 2, W_LO, HD), BF),
                pltpu.VMEM((FRAMES, TOK, HD), BF),
                pltpu.VMEM((KEYS, HD), BF),
                pltpu.VMEM((KEYS, 2 * HD), BF),
                pltpu.VMEM((4, 4 * TOK, HD), BF),
                pltpu.VMEM((4 * TOK, HD), F32),
                pltpu.VMEM((4 * TOK, 2 * HD), F32),
                pltpu.VMEM((4 * TOK, HD), F32),
            ],
        ),
        out_shape=[
            jax.ShapeDtypeStruct((4 * TOK, 4 * HD), BF),
            jax.ShapeDtypeStruct((2 * W_LO, HD), BF),
        ],
        compiler_params=pltpu.CompilerParams(vmem_limit_bytes=56 * 2**20),
        name="hi",
    )(pos, *args)


def swap(axis, bit):
    return [(i, i ^ bit) for i in range(16 if axis == "seq" else 8)]


def z_shift(step):
    return [(i, (i & 9) | ((((i >> 1) + step) & 3) << 1)) for i in range(16)]


CORE, X_HI = ("seq", 1), ("seq", 8)


def send(value, link):
    axis, bit = link
    return lax.ppermute(value, axis, swap(axis, bit))


def local(
    hidden_low,
    query_low,
    key_low,
    value_low,
    out_weight,
    latent_weight,
    conv_first,
    bias_first,
    conv_second,
    bias_second,
    query_weight,
    key_weight,
    value_weight,
    query_gain,
    key_gain,
):
    seq, head = lax.axis_index("seq"), lax.axis_index("head")
    pos = jnp.stack([seq // 8, (seq // 2) % 4, seq % 2, head]).astype(jnp.int32)
    pieces = pack(pos, query_low, key_low, value_low)
    pieces = [pieces[0]] + [
        lax.ppermute(pieces[step], "seq", z_shift(step)) for step in (1, 2, 3)
    ]
    w2, hl, m, gq, gk = prep(
        pos, out_weight, latent_weight, hidden_low, query_weight, key_weight, query_gain, key_gain
    )
    kv = jnp.concatenate([piece[:, HD:] for piece in pieces], axis=0)
    kv_x = send(kv, X_HI)
    kv_c = send(kv, CORE)
    kv_xc = send(kv_x, CORE)
    latent = low_attention(pos, pieces, (kv, kv_c, kv_x, kv_xc), w2, hl)
    for link in (("head", 1), ("head", 2), ("head", 4), ("seq", 2), ("seq", 4)):
        latent = (latent.astype(F32) + send(latent, link).astype(F32)).astype(BF)
    lat_x = send(latent, X_HI)
    lat_c = send(latent, CORE)
    lat_xc = send(lat_x, CORE)
    attn, up = hi_attention(
        pos,
        (latent, lat_c, lat_x, lat_xc),
        conv_first,
        bias_first,
        conv_second,
        bias_second,
        gq,
        gk,
        m,
        value_weight,
    )
    return attn, up


def solution(mesh):
    placed = (
        P("seq", None),
        P("seq", "head"),
        P("seq", "head"),
        P("seq", "head"),
        P("head", None),
    ) + (P(),) * 10
    return jax.shard_map(
        local,
        mesh=mesh,
        in_specs=placed,
        out_specs=(P("seq", "head"), P(("seq", "head"), None)),
        check_vma=False,
    )
```

time: 433 us -> 134 us (0.31)
  waiting for transfers between devices: 233 us -> 22.3 us
  matrix products: 72.3 us -> 0 us
  Pallas kernels: 0 us -> 64.4 us
  blocking collectives: 38.6 us -> 0 us
  local copies, waits for them, and re-layouts: 39.7 us -> 11.4 us
  starting transfers between devices: 10.3 us -> 34 us
  other arithmetic: 23.6 us -> 0.87 us
  between operations: 14.1 us -> 0.8 us
    all_gather x4 -> x0, waiting for transfers between devices: 154 us -> none  [the longest x1 51.8 us: local(): lax.all_gather(key_low, 'seq', axis=0, tiled=True)]
    psum x1 -> x0, waiting for transfers between devices: 74.7 us -> none  [local(): lax.psum(partial_value.astype(jnp.bfloat16), 'head').astype(jnp.float32)]
    dot_general x10 -> x0, matrix products: 72.3 us -> none  [the longest x2 31.1 us: attend_step(): jnp.einsum('hqk,khd->hqd', weights.astype(jnp.bfloat16), value_heads, pre...]
    pallas_call x0 -> x4, Pallas kernels: none -> 64.4 us  [the longest x1 57.3 us: hi_attention(): pl.pallas_call(hi_kernel, grid_spec=pltpu.PrefetchScalarGridSpec(num_scal...]
    all_to_all x3 -> x0, blocking collectives: 38.6 us -> none  [the longest x1 13.9 us: local(): lax.all_to_all(hi_value, 'head', split_axis=1, concat_axis=0, tiled=True)]
    all_gather x3 -> x0, local copies, waits for them, and re-layouts: 27.9 us -> none  [the longest x1 12 us: local(): lax.all_gather(head_value, 'seq', axis=0, tiled=True)]
    ppermute x2 -> x14, starting transfers between devices: 10.1 us -> 34 us  [the longest x11 27.5 us: send(): return lax.ppermute(value, axis, swap(axis, bit))]
    reduce_sum x2 -> x0, other arithmetic: 22.4 us -> none  [attend_step(): totals = jnp.sum(weights, axis=2)]
  transfers between devices with their start and end apart: 7 -> 14, of which waited for: 6 -> 8; matrix products, arithmetic and copies ran while one was open for 15% -> 1% of each run, Pallas kernels for 0% -> 1%
where the time goes in v1:
time: 134 us
  Pallas kernels  64.4 us (48%)
  starting transfers between devices  34 us (25%)
  waiting for transfers between devices  22.3 us (17%)
  local copies, waits for them, and re-layouts  11.4 us (9%)
    pallas_call x1, Pallas kernels, hi_attention(): pl.pallas_call(hi_kernel, grid_spec=pltpu.PrefetchScalarGridSpec(num_scal...  57.3 us
    ppermute x11, starting transfers between devices, send(): return lax.ppermute(value, axis, swap(axis, bit))  27.5 us
    ppermute x11, waiting for transfers between devices, send(): return lax.ppermute(value, axis, swap(axis, bit))  19.7 us
    unnamed x34, local copies, waits for them, and re-layouts  10.5 us
    ppermute x3, starting transfers between devices, local(): lax.ppermute(pieces[step], 'seq', z_shift(step))  6.5 us
    pallas_call x1, Pallas kernels, low_attention(): pl.pallas_call(low_kernel, grid_spec=pltpu.PrefetchScalarGridSpec(num_sca...  2.78 us
  transfers between devices with their start and end apart: 14, of which 8 were waited for; matrix products, arithmetic and copies ran while one was open for 1% of the time, Pallas kernels for 1%

profile of v1, /device:TPU:1, one launch (start us, length us, event | category | flops | bytes accessed | tf_op | source)
XLA Modules:
  0.0 133.8 jit_solution(1829362439047798463)
XLA Ops:
  0.7 0.7 pad_add_fusion.pos
  1.3 2.5 %pack.1 = (bf16[128,384]{1,0:T(8,128)(2,1)}, bf16[128,384]{1,0:T(8,128)(2,1)}, bf16[128,384]{1,0:T(8,128)(2,1)}, bf16[128,384]{1,0:T(8,128)(2,1)}) custom-call(s32[4]{0:T(128)} %pad_add_fusion.pos, bf16[128,512]{1,0:T(8,128)(2,1)} %q_ref.1, bf16[128,512]{1,0:T(8,128)(2,1)} %k_ref.1, bf16[128,512]{1,0:T(8,128)(2,1)} %v_ref.1), custom_call_target="tpu_custom_call" | custom-call | tf_op jit(solution)/shard_map/pack/pallas_call | solution.py:59
  3.8 2.5 %collective-permute-start = (bf16[128,384]{1,0:T(8,128)(2,1)}, bf16[128,384]{1,0:T(8,128)(2,1)S(1)}, u32[]{:S(2)}, u32[]{:S(2)}) collective-permute-start(bf16[128,384]{1,0:T(8,128)(2,1)} %get-tuple-element.12), channel_id=1, source_target_pairs={{0,16},{8,24},{16,32},{24,40},{32,48},{40,56},{48,0},{56,8},{64,80... | collective-permute-start | bytes 294920 | tf_op jit(solution)/shard_map/ppermute | solution.py:374
  6.3 3.3 %collective-permute-start.1 = (bf16[128,384]{1,0:T(8,128)(2,1)}, bf16[128,384]{1,0:T(8,128)(2,1)S(1)}, u32[]{:S(2)}, u32[]{:S(2)}) collective-permute-start(bf16[128,384]{1,0:T(8,128)(2,1)} %get-tuple-element.13), channel_id=1, source_target_pairs={{0,32},{8,40},{16,48},{24,56},{32,0},{40,8},{48,16},{56,24},{64,96... | collective-permute-start | bytes 294920 | tf_op jit(solution)/shard_map/ppermute | solution.py:374
  9.6 0.7 collective-permute-start.2
  10.3 0.8 slice.12
  11.1 0.0 collective-permute-done.p1
  11.2 2.6 %collective-permute-done.1.p2 = bf16[128,384]{1,0:T(8,128)(2,1)S(1)} collective-permute-done((bf16[128,384]{1,0:T(8,128)(2,1)}, bf16[128,384]{1,0:T(8,128)(2,1)S(1)}, u32[]{:S(2)}, u32[]{:S(2)}) %collective-permute-start.1) | collective-permute-done | bytes 98336 | tf_op jit(solution)/shard_map/ppermute | solution.py:374
  13.8 0.0 collective-permute-done.2.p3
  13.8 2.8 %collective-permute-start.4 = (bf16[512,256]{1,0:T(8,128)(2,1)S(1)}, bf16[512,256]{1,0:T(8,128)(2,1)S(1)}, u32[]{:S(2)}, u32[]{:S(2)}) collective-permute-start(bf16[512,256]{1,0:T(8,128)(2,1)S(1)} %pad_maximum_fusion.kv0), channel_id=1, source_target_pairs={{0,64},{8,72},{16,80},{24,88},{32,96},{40,104},{48,112},{56,120},{... | collective-permute-start | bytes 786440 | tf_op jit(solution)/shard_map/ppermute | solution.py:350
  16.7 2.1 %collective-permute-start.3 = (bf16[512,256]{1,0:T(8,128)(2,1)S(1)}, bf16[512,256]{1,0:T(8,128)(2,1)S(1)}, u32[]{:S(2)}, u32[]{:S(2)}) collective-permute-start(bf16[512,256]{1,0:T(8,128)(2,1)S(1)} %pad_maximum_fusion.kv0), channel_id=1, source_target_pairs={{0,8},{8,0},{16,24},{24,16},{32,40},{40,32},{48,56},{56,48},{64,72... | collective-permute-start | bytes 786440 | tf_op jit(solution)/shard_map/ppermute | solution.py:350
  18.8 2.6 %collective-permute-done.4.kv2 = bf16[512,256]{1,0:T(8,128)(2,1)S(1)} collective-permute-done((bf16[512,256]{1,0:T(8,128)(2,1)S(1)}, bf16[512,256]{1,0:T(8,128)(2,1)S(1)}, u32[]{:S(2)}, u32[]{:S(2)}) %collective-permute-start.4) | collective-permute-done | bytes 262176 | tf_op jit(solution)/shard_map/ppermute | solution.py:350
  21.4 2.8 %collective-permute-start.5 = (bf16[512,256]{1,0:T(8,128)(2,1)S(1)}, bf16[512,256]{1,0:T(8,128)(2,1)S(1)}, u32[]{:S(2)}, u32[]{:S(2)}) collective-permute-start(bf16[512,256]{1,0:T(8,128)(2,1)S(1)} %collective-permute-done.4.kv2), channel_id=1, source_target_pairs={{0,8},{8,0},{16,24},{24,16},{32,40},{40,32},{48,56},{56,48},{64,72... | collective-permute-start | bytes 786440 | tf_op jit(solution)/shard_map/ppermute | solution.py:350
  24.1 0.0 copy-start
  24.1 2.2 %copy-done = bf16[512,4096]{1,0:T(8,128)(2,1)S(1)} copy-done((bf16[512,4096]{1,0:T(8,128)(2,1)S(1)}, bf16[512,4096]{1,0:T(8,128)(2,1)}, u32[]{:S(2)}) %copy-start) | copy-done | bytes 4194328
  26.3 0.0 copy-start.1
  26.3 1.2 copy-done.1
  27.6 0.0 copy-start.2
  27.6 1.2 copy-done.2
  28.8 0.0 copy-start.3
  28.8 1.2 copy-done.3
  30.0 0.0 copy-start.4
  30.0 1.2 copy-done.4
  31.2 0.0 copy-start.9
  31.2 0.7 copy-done.9
  32.0 0.0 copy-start.10
  32.0 0.7 copy-done.10
  32.7 0.0 copy-start.11
  32.7 0.7 copy-done.11
  33.3 0.0 copy-start.5
  33.3 1.9 %prep.1 = (bf16[128,256]{1,0:T(8,128)(2,1)S(1)}, f32[16,128]{1,0:T(8,128)S(1)}, bf16[4,128,256]{2,1,0:T(8,128)(2,1)S(1)}, bf16[128,256]{1,0:T(8,128)(2,1)S(1)}, bf16[128,256]{1,0:T(8,128)(2,1)S(1)}) custom-call(s32[4]{0:T(128)S(1)} %copy-done.11, bf16[512,4096]{1,0:T(8,128)(2,1)S(1)} %copy-done, bf16[4096,128]{1,0:T(8,128)(2,1)S(1)} %copy-done.3, ...), custom_call_target="tpu_custom_call" | custom-call | flops 900000000 | bytes 5000000 | tf_op jit(solution)/shard_map/prep/pallas_call | solution.py:90
  35.2 0.0 copy-start.6
  35.2 0.7 copy-done.6
  35.9 0.0 copy-start.7
  35.9 0.0 collective-permute-done.3.kv1
  35.9 0.0 collective-permute-done.5.kv3
  35.9 0.0 copy-done.5
  35.9 0.0 copy-done.12
  35.9 2.8 %low.1 = bf16[512,128]{1,0:T(8,128)(2,1)S(1)} custom-call(s32[4]{0:T(128)S(1)} %copy-done.12, bf16[128,384]{1,0:T(8,128)(2,1)S(1)} %copy-done.5, bf16[128,384]{1,0:T(8,128)(2,1)S(1)} %collective-permute-done.p1, bf16[128,384]{1,0:T(8,128)(2,1)S(1)} %collective-permute-done.1.p2, bf16[128,384]{1,0:T(8,128)(2,1)S(1)} %collective-permute-done.2.p3, ...), custom_call_target="tpu_custom_call" | custom-call | tf_op jit(solution)/shard_map/low/pallas_call | solution.py:163
  38.7 1.3 collective-permute-start.6
  40.0 3.9 %collective-permute-done.6 = bf16[512,128]{1,0:T(8,128)(2,1)S(1)} collective-permute-done((bf16[512,128]{1,0:T(8,128)(2,1)S(1)}, bf16[512,128]{1,0:T(8,128)(2,1)S(1)}, u32[]{:S(2)}, u32[]{:S(2)}) %collective-permute-start.6) | collective-permute-done | bytes 131104 | tf_op jit(solution)/shard_map/ppermute | solution.py:350
  44.0 0.0 copy-done.7
  44.0 1.4 %collective-permute-start.7 = (bf16[512,128]{1,0:T(8,128)(2,1)S(1)}, bf16[512,128]{1,0:T(8,128)(2,1)S(1)}, u32[]{:S(2)}, u32[]{:S(2)}) collective-permute-start(bf16[512,128]{1,0:T(8,128)(2,1)S(1)} %add_convert_fusion.4), channel_id=1, source_target_pairs={{0,2},{1,3},{2,0},{3,1},{4,6},{5,7},{6,4},{7,5},{8,10},{9,11},{10,... | collective-permute-start | bytes 393224 | tf_op jit(solution)/shard_map/ppermute | solution.py:350
  45.4 0.0 copy-done.8
  45.4 2.9 %collective-permute-done.7 = bf16[512,128]{1,0:T(8,128)(2,1)S(1)} collective-permute-done((bf16[512,128]{1,0:T(8,128)(2,1)S(1)}, bf16[512,128]{1,0:T(8,128)(2,1)S(1)}, u32[]{:S(2)}, u32[]{:S(2)}) %collective-permute-start.7) | collective-permute-done | bytes 131104 | tf_op jit(solution)/shard_map/ppermute | solution.py:350
  48.4 3.0 %collective-permute-start.8 = (bf16[512,128]{1,0:T(8,128)(2,1)S(1)}, bf16[512,128]{1,0:T(8,128)(2,1)S(1)}, u32[]{:S(2)}, u32[]{:S(2)}) collective-permute-start(bf16[512,128]{1,0:T(8,128)(2,1)S(1)} %add_convert_fusion.3), channel_id=1, source_target_pairs={{0,4},{1,5},{2,6},{3,7},{4,0},{5,1},{6,2},{7,3},{8,12},{9,13},{10,... | collective-permute-start | bytes 393224 | tf_op jit(solution)/shard_map/ppermute | solution.py:350
  51.3 2.4 %collective-permute-done.8 = bf16[512,128]{1,0:T(8,128)(2,1)S(1)} collective-permute-done((bf16[512,128]{1,0:T(8,128)(2,1)S(1)}, bf16[512,128]{1,0:T(8,128)(2,1)S(1)}, u32[]{:S(2)}, u32[]{:S(2)}) %collective-permute-start.8) | collective-permute-done | bytes 131104 | tf_op jit(solution)/shard_map/ppermute | solution.py:350
  53.8 1.4 %collective-permute-start.9 = (bf16[512,128]{1,0:T(8,128)(2,1)S(1)}, bf16[512,128]{1,0:T(8,128)(2,1)S(1)}, u32[]{:S(2)}, u32[]{:S(2)}) collective-permute-start(bf16[512,128]{1,0:T(8,128)(2,1)S(1)} %add_convert_fusion.2), channel_id=1, source_target_pairs={{0,16},{8,24},{16,0},{24,8},{32,48},{40,56},{48,32},{56,40},{64,80... | collective-permute-start | bytes 393224 | tf_op jit(solution)/shard_map/ppermute | solution.py:350
  55.2 2.5 %collective-permute-done.9 = bf16[512,128]{1,0:T(8,128)(2,1)S(1)} collective-permute-done((bf16[512,128]{1,0:T(8,128)(2,1)S(1)}, bf16[512,128]{1,0:T(8,128)(2,1)S(1)}, u32[]{:S(2)}, u32[]{:S(2)}) %collective-permute-start.9) | collective-permute-done | bytes 131104 | tf_op jit(solution)/shard_map/ppermute | solution.py:350
  57.7 2.0 %collective-permute-start.10 = (bf16[512,128]{1,0:T(8,128)(2,1)S(1)}, bf16[512,128]{1,0:T(8,128)(2,1)S(1)}, u32[]{:S(2)}, u32[]{:S(2)}) collective-permute-start(bf16[512,128]{1,0:T(8,128)(2,1)S(1)} %add_convert_fusion.1), channel_id=1, source_target_pairs={{0,32},{8,40},{16,48},{24,56},{32,0},{40,8},{48,16},{56,24},{64,96... | collective-permute-start | bytes 393224 | tf_op jit(solution)/shard_map/ppermute | solution.py:350
  59.8 4.3 %collective-permute-done.10 = bf16[512,128]{1,0:T(8,128)(2,1)S(1)} collective-permute-done((bf16[512,128]{1,0:T(8,128)(2,1)S(1)}, bf16[512,128]{1,0:T(8,128)(2,1)S(1)}, u32[]{:S(2)}, u32[]{:S(2)}) %collective-permute-start.10) | collective-permute-done | bytes 131104 | tf_op jit(solution)/shard_map/ppermute | solution.py:350
  64.1 0.0 copy-start.13
  64.1 2.8 %collective-permute-start.12 = (bf16[512,128]{1,0:T(8,128)(2,1)S(1)}, bf16[512,128]{1,0:T(8,128)(2,1)S(1)}, u32[]{:S(2)}, u32[]{:S(2)}) collective-permute-start(bf16[512,128]{1,0:T(8,128)(2,1)S(1)} %add_convert_fusion.lat0), channel_id=1, source_target_pairs={{0,64},{8,72},{16,80},{24,88},{32,96},{40,104},{48,112},{56,120},{... | collective-permute-start | bytes 393224 | tf_op jit(solution)/shard_map/ppermute | solution.py:350
  66.9 4.5 %collective-permute-start.11 = (bf16[512,128]{1,0:T(8,128)(2,1)S(1)}, bf16[512,128]{1,0:T(8,128)(2,1)S(1)}, u32[]{:S(2)}, u32[]{:S(2)}) collective-permute-start(bf16[512,128]{1,0:T(8,128)(2,1)S(1)} %add_convert_fusion.lat0), channel_id=1, source_target_pairs={{0,8},{8,0},{16,24},{24,16},{32,40},{40,32},{48,56},{56,48},{64,72... | collective-permute-start | bytes 393224 | tf_op jit(solution)/shard_map/ppermute | solution.py:350
  71.4 0.0 collective-permute-done.12.lat2
  71.4 0.0 copy-start.14
  71.4 3.4 %collective-permute-start.13 = (bf16[512,128]{1,0:T(8,128)(2,1)S(1)}, bf16[512,128]{1,0:T(8,128)(2,1)S(1)}, u32[]{:S(2)}, u32[]{:S(2)}) collective-permute-start(bf16[512,128]{1,0:T(8,128)(2,1)S(1)} %collective-permute-done.12.lat2), channel_id=1, source_target_pairs={{0,8},{8,0},{16,24},{24,16},{32,40},{40,32},{48,56},{56,48},{64,72... | collective-permute-start | bytes 393224 | tf_op jit(solution)/shard_map/ppermute | solution.py:350
  74.9 0.0 collective-permute-done.11.lat1
  74.9 1.0 collective-permute-done.13.lat3
  75.9 0.0 copy-done.13
  75.9 0.0 copy-done.14
  75.9 0.0 copy-done.15
  75.9 0.6 copy-done.16
  76.5 57.3 %hi.1 = (bf16[512,512]{1,0:T(8,128)(2,1)}, bf16[64,128]{1,0:T(8,128)(2,1)}) custom-call(s32[4]{0:T(128)} %pad_add_fusion.pos, bf16[512,128]{1,0:T(8,128)(2,1)} %copy-done.13, bf16[512,128]{1,0:T(8,128)(2,1)} %copy-done.15, bf16[512,128]{1,0:T(8,128)(2,1)} %copy-done.14, bf16[512,128]{1,0:T(8,128)(2,1)} %copy-done.16, bf16[3456,512]{1,0:T(8,128)(2,1)} %bitcast.11, ...), custom_call_target="tpu_custom_call" | custom-call | tf_op jit(solution)/shard_map/hi/pallas_call | solution.py:310
  (13 shorter events, 0.2 us)
Async XLA Ops:
  3.8 7.3 %collective-permute-start = (bf16[128,384]{1,0:T(8,128)(2,1)}, bf16[128,384]{1,0:T(8,128)(2,1)S(1)}, u32[]{:S(2)}, u32[]{:S(2)}) collective-permute-start(bf16[128,384]{1,0:T(8,128)(2,1)} %get-tuple-element.12), channel_id=1, source_target_pairs={{0,16},{8,24},{16,32},{24,40},{32,48},{40,56},{48,0},{56,8},{64,80... | collective-permute-start | bytes 294920 | tf_op jit(solution)/shard_map/ppermute | solution.py:374
  6.3 7.5 %collective-permute-start.1 = (bf16[128,384]{1,0:T(8,128)(2,1)}, bf16[128,384]{1,0:T(8,128)(2,1)S(1)}, u32[]{:S(2)}, u32[]{:S(2)}) collective-permute-start(bf16[128,384]{1,0:T(8,128)(2,1)} %get-tuple-element.13), channel_id=1, source_target_pairs={{0,32},{8,40},{16,48},{24,56},{32,0},{40,8},{48,16},{56,24},{64,96... | collective-permute-start | bytes 294920 | tf_op jit(solution)/shard_map/ppermute | solution.py:374
  9.6 4.2 %collective-permute-start.2 = (bf16[128,384]{1,0:T(8,128)(2,1)}, bf16[128,384]{1,0:T(8,128)(2,1)S(1)}, u32[]{:S(2)}, u32[]{:S(2)}) collective-permute-start(bf16[128,384]{1,0:T(8,128)(2,1)} %get-tuple-element.14), channel_id=1, source_target_pairs={{0,48},{8,56},{16,0},{24,8},{32,16},{40,24},{48,32},{56,40},{64,11... | collective-permute-start | bytes 294920 | tf_op jit(solution)/shard_map/ppermute | solution.py:374
  13.8 7.5 %collective-permute-start.4 = (bf16[512,256]{1,0:T(8,128)(2,1)S(1)}, bf16[512,256]{1,0:T(8,128)(2,1)S(1)}, u32[]{:S(2)}, u32[]{:S(2)}) collective-permute-start(bf16[512,256]{1,0:T(8,128)(2,1)S(1)} %pad_maximum_fusion.kv0), channel_id=1, source_target_pairs={{0,64},{8,72},{16,80},{24,88},{32,96},{40,104},{48,112},{56,120},{... | collective-permute-start | bytes 786440 | tf_op jit(solution)/shard_map/ppermute | solution.py:350
  16.7 19.3 %collective-permute-start.3 = (bf16[512,256]{1,0:T(8,128)(2,1)S(1)}, bf16[512,256]{1,0:T(8,128)(2,1)S(1)}, u32[]{:S(2)}, u32[]{:S(2)}) collective-permute-start(bf16[512,256]{1,0:T(8,128)(2,1)S(1)} %pad_maximum_fusion.kv0), channel_id=1, source_target_pairs={{0,8},{8,0},{16,24},{24,16},{32,40},{40,32},{48,56},{56,48},{64,72... | collective-permute-start | bytes 786440 | tf_op jit(solution)/shard_map/ppermute | solution.py:350
  21.4 14.5 %collective-permute-start.5 = (bf16[512,256]{1,0:T(8,128)(2,1)S(1)}, bf16[512,256]{1,0:T(8,128)(2,1)S(1)}, u32[]{:S(2)}, u32[]{:S(2)}) collective-permute-start(bf16[512,256]{1,0:T(8,128)(2,1)S(1)} %collective-permute-done.4.kv2), channel_id=1, source_target_pairs={{0,8},{8,0},{16,24},{24,16},{32,40},{40,32},{48,56},{56,48},{64,72... | collective-permute-start | bytes 786440 | tf_op jit(solution)/shard_map/ppermute | solution.py:350
  24.1 2.2 %copy-start = (bf16[512,4096]{1,0:T(8,128)(2,1)S(1)}, bf16[512,4096]{1,0:T(8,128)(2,1)}, u32[]{:S(2)}) copy-start(bf16[512,4096]{1,0:T(8,128)(2,1)} %ow.1) | copy-start | bytes 12582916
  26.3 1.2 copy-start.1
  27.6 1.2 copy-start.2
  28.8 1.2 copy-start.3
  30.0 1.2 copy-start.4
  31.2 0.7 copy-start.9
  32.0 0.7 copy-start.10
  32.7 0.7 copy-start.11
  33.3 2.6 %copy-start.5 = (bf16[128,384]{1,0:T(8,128)(2,1)S(1)}, bf16[128,384]{1,0:T(8,128)(2,1)}, u32[]{:S(2)}) copy-start(bf16[128,384]{1,0:T(8,128)(2,1)} %get-tuple-element.11.p0) | copy-start | bytes 294916
  33.3 2.6 %copy-start.12 = (s32[4]{0:T(128)S(1)}, s32[4]{0:T(128)}, u32[]{:S(2)}) copy-start(s32[4]{0:T(128)} %pad_add_fusion.pos) | copy-start | bytes 52
  35.2 0.7 copy-start.6
  35.9 8.1 %copy-start.7 = (bf16[128,256]{1,0:T(8,128)(2,1)}, bf16[128,256]{1,0:T(8,128)(2,1)S(1)}, u32[]{:S(2)}) copy-start(bf16[128,256]{1,0:T(8,128)(2,1)S(1)} %get-tuple-element.17.gq) | copy-start | bytes 196612
  35.9 9.5 %copy-start.8 = (bf16[128,256]{1,0:T(8,128)(2,1)}, bf16[128,256]{1,0:T(8,128)(2,1)S(1)}, u32[]{:S(2)}) copy-start(bf16[128,256]{1,0:T(8,128)(2,1)S(1)} %get-tuple-element.18.gk) | copy-start | bytes 196612
  38.7 5.2 %collective-permute-start.6 = (bf16[512,128]{1,0:T(8,128)(2,1)S(1)}, bf16[512,128]{1,0:T(8,128)(2,1)S(1)}, u32[]{:S(2)}, u32[]{:S(2)}) collective-permute-start(bf16[512,128]{1,0:T(8,128)(2,1)S(1)} %low.1), channel_id=1, source_target_pairs={{0,1},{1,0},{2,3},{3,2},{4,5},{5,4},{6,7},{7,6},{8,9},{9,8},{10,11... | collective-permute-start | bytes 393224 | tf_op jit(solution)/shard_map/ppermute | solution.py:350
  44.0 4.3 %collective-permute-start.7 = (bf16[512,128]{1,0:T(8,128)(2,1)S(1)}, bf16[512,128]{1,0:T(8,128)(2,1)S(1)}, u32[]{:S(2)}, u32[]{:S(2)}) collective-permute-start(bf16[512,128]{1,0:T(8,128)(2,1)S(1)} %add_convert_fusion.4), channel_id=1, source_target_pairs={{0,2},{1,3},{2,0},{3,1},{4,6},{5,7},{6,4},{7,5},{8,10},{9,11},{10,... | collective-permute-start | bytes 393224 | tf_op jit(solution)/shard_map/ppermute | solution.py:350
  48.4 5.4 %collective-permute-start.8 = (bf16[512,128]{1,0:T(8,128)(2,1)S(1)}, bf16[512,128]{1,0:T(8,128)(2,1)S(1)}, u32[]{:S(2)}, u32[]{:S(2)}) collective-permute-start(bf16[512,128]{1,0:T(8,128)(2,1)S(1)} %add_convert_fusion.3), channel_id=1, source_target_pairs={{0,4},{1,5},{2,6},{3,7},{4,0},{5,1},{6,2},{7,3},{8,12},{9,13},{10,... | collective-permute-start | bytes 393224 | tf_op jit(solution)/shard_map/ppermute | solution.py:350
  53.8 3.9 %collective-permute-start.9 = (bf16[512,128]{1,0:T(8,128)(2,1)S(1)}, bf16[512,128]{1,0:T(8,128)(2,1)S(1)}, u32[]{:S(2)}, u32[]{:S(2)}) collective-permute-start(bf16[512,128]{1,0:T(8,128)(2,1)S(1)} %add_convert_fusion.2), channel_id=1, source_target_pairs={{0,16},{8,24},{16,0},{24,8},{32,48},{40,56},{48,32},{56,40},{64,80... | collective-permute-start | bytes 393224 | tf_op jit(solution)/shard_map/ppermute | solution.py:350
  57.7 6.3 %collective-permute-start.10 = (bf16[512,128]{1,0:T(8,128)(2,1)S(1)}, bf16[512,128]{1,0:T(8,128)(2,1)S(1)}, u32[]{:S(2)}, u32[]{:S(2)}) collective-permute-start(bf16[512,128]{1,0:T(8,128)(2,1)S(1)} %add_convert_fusion.1), channel_id=1, source_target_pairs={{0,32},{8,40},{16,48},{24,56},{32,0},{40,8},{48,16},{56,24},{64,96... | collective-permute-start | bytes 393224 | tf_op jit(solution)/shard_map/ppermute | solution.py:350
  64.1 11.8 %copy-start.13 = (bf16[512,128]{1,0:T(8,128)(2,1)}, bf16[512,128]{1,0:T(8,128)(2,1)S(1)}, u32[]{:S(2)}) copy-start(bf16[512,128]{1,0:T(8,128)(2,1)S(1)} %add_convert_fusion.lat0) | copy-start | bytes 393220
  64.1 7.3 %collective-permute-start.12 = (bf16[512,128]{1,0:T(8,128)(2,1)S(1)}, bf16[512,128]{1,0:T(8,128)(2,1)S(1)}, u32[]{:S(2)}, u32[]{:S(2)}) collective-permute-start(bf16[512,128]{1,0:T(8,128)(2,1)S(1)} %add_convert_fusion.lat0), channel_id=1, source_target_pairs={{0,64},{8,72},{16,80},{24,88},{32,96},{40,104},{48,112},{56,120},{... | collective-permute-start | bytes 393224 | tf_op jit(solution)/shard_map/ppermute | solution.py:350
  66.9 8.0 %collective-permute-start.11 = (bf16[512,128]{1,0:T(8,128)(2,1)S(1)}, bf16[512,128]{1,0:T(8,128)(2,1)S(1)}, u32[]{:S(2)}, u32[]{:S(2)}) collective-permute-start(bf16[512,128]{1,0:T(8,128)(2,1)S(1)} %add_convert_fusion.lat0), channel_id=1, source_target_pairs={{0,8},{8,0},{16,24},{24,16},{32,40},{40,32},{48,56},{56,48},{64,72... | collective-permute-start | bytes 393224 | tf_op jit(solution)/shard_map/ppermute | solution.py:350
  71.4 4.4 %copy-start.14 = (bf16[512,128]{1,0:T(8,128)(2,1)}, bf16[512,128]{1,0:T(8,128)(2,1)S(1)}, u32[]{:S(2)}) copy-start(bf16[512,128]{1,0:T(8,128)(2,1)S(1)} %collective-permute-done.12.lat2) | copy-start | bytes 393220
  71.4 4.4 %collective-permute-start.13 = (bf16[512,128]{1,0:T(8,128)(2,1)S(1)}, bf16[512,128]{1,0:T(8,128)(2,1)S(1)}, u32[]{:S(2)}, u32[]{:S(2)}) collective-permute-start(bf16[512,128]{1,0:T(8,128)(2,1)S(1)} %collective-permute-done.12.lat2), channel_id=1, source_target_pairs={{0,8},{8,0},{16,24},{24,16},{32,40},{40,32},{48,56},{56,48},{64,72... | collective-permute-start | bytes 393224 | tf_op jit(solution)/shard_map/ppermute | solution.py:350
  74.9 1.0 copy-start.15
  75.9 0.7 copy-start.16

commit v2 on v1

--- a/solution.py
+++ b/solution.py
@@ -18,6 +18,7 @@
 SCALE = LOG2E / math.sqrt(HD)
 BF = jnp.bfloat16
 F32 = jnp.float32
+VMEM = 60 * 2**20
 NT = (((1,), (1,)), ((), ()))
 
 
@@ -45,26 +46,37 @@
     return pl.BlockSpec(shape, lambda *_: (0,) * len(shape))
 
 
-def pack_kernel(pos, q_ref, k_ref, v_ref, *outs):
-    for shift, out in enumerate(outs):
+def pack_kernel(pos, q_ref, k_ref, v_ref, o0, o1, o2, o3, sems):
+    copies = []
+    for shift, out in enumerate((o0, o1, o2, o3)):
         head = lax.rem(pos[1] + shift, 4)
         columns = pl.ds(pl.multiple_of(head * HD, HD), HD)
-        out[:, 0:HD] = q_ref[:, columns]
-        out[:, HD : 2 * HD] = k_ref[:, columns]
-        out[:, 2 * HD : 3 * HD] = v_ref[:, columns]
+        for part, ref in enumerate((q_ref, k_ref, v_ref)):
+            copies.append(
+                pltpu.make_async_copy(
+                    ref.at[:, columns], out.at[:, part * HD : (part + 1) * HD], sems.at[shift, part]
+                )
+            )
+    for copy in copies:
+        copy.start()
+    for copy in copies:
+        copy.wait()
 
 
 def pack(pos, q, k, v):
     piece = jax.ShapeDtypeStruct((TOK, 3 * HD), BF)
+    anywhere = pl.BlockSpec(memory_space=pl.ANY)
     return pl.pallas_call(
         pack_kernel,
         grid_spec=pltpu.PrefetchScalarGridSpec(
             num_scalar_prefetch=1,
             grid=(1,),
-            in_specs=[whole(q.shape)] * 3,
-            out_specs=[whole(piece.shape)] * 4,
+            in_specs=[anywhere] * 3,
+            out_specs=[anywhere] * 4,
+            scratch_shapes=[pltpu.SemaphoreType.DMA((4, 3))],
         ),
         out_shape=[piece] * 4,
+        compiler_params=pltpu.CompilerParams(vmem_limit_bytes=VMEM),
         name="pack",
     )(pos, q, k, v)
 
@@ -118,7 +130,7 @@
             jax.ShapeDtypeStruct((HD, 2 * HD), BF),
             jax.ShapeDtypeStruct((HD, 2 * HD), BF),
         ],
-        compiler_params=pltpu.CompilerParams(vmem_limit_bytes=24 * 2**20),
+        compiler_params=pltpu.CompilerParams(vmem_limit_bytes=VMEM),
         cost_estimate=pl.CostEstimate(flops=900_000_000, bytes_accessed=5_000_000, transcendentals=0),
         name="prep",
     )(
@@ -170,7 +182,7 @@
             scratch_shapes=[pltpu.VMEM((4, TOK, HD), BF), pltpu.VMEM((4 * TOK, HD), F32)],
         ),
         out_shape=jax.ShapeDtypeStruct((4 * TOK, HD), BF),
-        compiler_params=pltpu.CompilerParams(vmem_limit_bytes=32 * 2**20),
+        compiler_params=pltpu.CompilerParams(vmem_limit_bytes=VMEM),
         name="low",
     )(pos, *args)
 
@@ -203,7 +215,7 @@
     q_s,
     nat_s,
     acc_s,
-    max_s,
+    bound_s,
 ):
     x, z, c, g = pos[0], pos[1], pos[2], pos[3]
     for dx, dc, piece in ((0, 0, lat0), (0, 1, lat1), (1, 0, lat2), (1, 1, lat3)):
@@ -229,7 +241,7 @@
                 for t in range(3):
                     taps.append(grid_s[t, first + a : first + a + CHUNK, b : b + H_LO].reshape(rows, HD))
         middle = dot(jnp.concatenate(taps, axis=1), conv[...]) + b1[...]
-        middle = (middle / (1.0 + jnp.exp(-middle))).astype(BF)
+        middle = (middle * (0.5 * jnp.tanh(0.5 * middle) + 0.5)).astype(BF)
         sub = dot(middle, second[...]) + b2[...]
         base = lat_s[first : first + CHUNK].reshape(rows, HD).astype(F32)
         for s in range(4):
@@ -251,8 +263,8 @@
     )
     to = lax.broadcasted_iota(jnp.int32, (4 * TOK, 4 * TOK), 0)
     source = lax.broadcasted_iota(jnp.int32, (4 * TOK, 4 * TOK), 1)
-    row, col = to // (2 * W_LO), lax.rem(to, 2 * W_LO)
-    wanted = (lax.rem(row, 2) * 2 + lax.rem(col, 2)) * TOK + (row // 2) * W_LO + col // 2
+    p, r = (to >> 6) & 1, to & 1
+    wanted = (((p << 1) | r) << 7) | ((to >> 7) << 5) | ((to >> 1) & (W_LO - 1))
     natural = dot(jnp.where(source == wanted, 1.0, 0.0).astype(BF), own)
     nat_s[...] = natural
     up_out[...] = nat_s[pl.ds(pl.multiple_of(g * 2 * W_LO, 2 * W_LO), 2 * W_LO), :].astype(BF)
@@ -262,43 +274,46 @@
     for head in range(4):
         q_s[head] = (dot2(mine, m[head]) * inverse).astype(BF)
 
-    def one_head(head, carry):
-        q = q_s[head]
-        qf = q.astype(F32)
+    for head in range(4):
+        qf = q_s[head].astype(F32)
         bound = jnp.sqrt(jnp.sum(qf * qf, axis=1, keepdims=True) * biggest)
-
-        def step(j, acc):
-            keys = pl.ds(pl.multiple_of(j * BLOCK, BLOCK), BLOCK)
-            scores = dot_nt(q, key_s[keys, :])
-            return acc + dot(jnp.exp2(scores - bound).astype(BF), val_s[keys, :])
-
-        acc = lax.fori_loop(0, KEYS // BLOCK, step, jnp.zeros((4 * TOK, 2 * HD), F32), unroll=2)
-        acc_s[...] = acc
-        weakest = jnp.min(acc[:, HD:])
-
-        @pl.when(jnp.logical_not(weakest > TINY))
-        def _():
-            acc_s[...] = jnp.zeros_like(acc_s)
-            max_s[...] = jnp.full_like(max_s, -1e30)
+        bound_s[head] = jnp.broadcast_to(bound, (4 * TOK, HD))
+    acc_s[...] = jnp.zeros_like(acc_s)
+
+    def step(j, carry):
+        keys = pl.ds(pl.multiple_of(j * BLOCK, BLOCK), BLOCK)
+        for head in range(4):
+            scores = dot_nt(q_s[head], key_s[keys, :])
+            weights = jnp.exp2(scores - bound_s[head, :, 0:1]).astype(BF)
+            acc_s[head] += dot(weights, val_s[keys, :])
+        return carry
+
+    lax.fori_loop(0, KEYS // BLOCK, step, 0)
+
+    @pl.when(jnp.logical_not(jnp.min(acc_s[:, :, HD:]) > TINY))
+    def _():
+        def careful_head(head, carry):
+            acc_s[head] = jnp.zeros((4 * TOK, 2 * HD), F32)
+            bound_s[head] = jnp.full((4 * TOK, HD), -1e30, F32)
 
             def careful(j, carry):
                 keys = pl.ds(pl.multiple_of(j * 512, 512), 512)
                 scores = dot_nt(q_s[head], key_s[keys, :])
-                before = max_s[:, 0:1]
+                before = bound_s[head, :, 0:1]
                 top = jnp.maximum(before, jnp.max(scores, axis=1, keepdims=True))
                 weights = jnp.exp2(scores - top).astype(BF)
-                acc_s[...] = acc_s[...] * jnp.exp2(before - top) + dot(weights, val_s[keys, :])
-                max_s[...] = jnp.broadcast_to(top, max_s.shape)
+                acc_s[head] = acc_s[head] * jnp.exp2(before - top) + dot(weights, val_s[keys, :])
+                bound_s[head] = jnp.broadcast_to(top, (4 * TOK, HD))
                 return carry
 
-            lax.fori_loop(0, KEYS // 512, careful, 0)
-
-        mixed = (acc_s[:, :HD] / acc_s[:, HD:]).astype(BF)
-        columns = pl.ds(pl.multiple_of(head * HD, HD), HD)
+            return lax.fori_loop(0, KEYS // 512, careful, carry)
+
+        lax.fori_loop(0, 4, careful_head, 0)
+
+    for head in range(4):
+        mixed = (acc_s[head, :, :HD] / acc_s[head, :, HD:]).astype(BF)
+        columns = slice(head * HD, (head + 1) * HD)
         attn_out[:, columns] = dot(mixed, wv[:, columns]).astype(BF)
-        return carry
-
-    lax.fori_loop(0, 4, one_head, 0)
 
 
 def hi_attention(pos, lats, conv_first, bias_first, conv_second, bias_second, gq, gk, m, value_weight):
@@ -321,33 +336,59 @@
                 pltpu.VMEM((KEYS, 2 * HD), BF),
                 pltpu.VMEM((4, 4 * TOK, HD), BF),
                 pltpu.VMEM((4 * TOK, HD), F32),
-                pltpu.VMEM((4 * TOK, 2 * HD), F32),
-                pltpu.VMEM((4 * TOK, HD), F32),
+                pltpu.VMEM((4, 4 * TOK, 2 * HD), F32),
+                pltpu.VMEM((4, 4 * TOK, HD), F32),
             ],
         ),
         out_shape=[
             jax.ShapeDtypeStruct((4 * TOK, 4 * HD), BF),
             jax.ShapeDtypeStruct((2 * W_LO, HD), BF),
         ],
-        compiler_params=pltpu.CompilerParams(vmem_limit_bytes=56 * 2**20),
+        compiler_params=pltpu.CompilerParams(vmem_limit_bytes=VMEM),
         name="hi",
     )(pos, *args)
 
 
-def swap(axis, bit):
-    return [(i, i ^ bit) for i in range(16 if axis == "seq" else 8)]
-
-
 def z_shift(step):
     return [(i, (i & 9) | ((((i >> 1) + step) & 3) << 1)) for i in range(16)]
 
 
-CORE, X_HI = ("seq", 1), ("seq", 8)
-
-
-def send(value, link):
-    axis, bit = link
-    return lax.ppermute(value, axis, swap(axis, bit))
+def trade(value, partner):
+    pairs = []
+    for seq in range(16):
+        for head in range(8):
+            x, y, z, core = (seq >> 3) * 2 + (head & 1), head >> 1, (seq >> 1) & 3, seq & 1
+            x, y, z, core = partner(x, y, z, core)
+            other = ((x >> 1) * 8 + z * 2 + core) * 8 + y * 2 + (x & 1)
+            pairs.append((seq * 8 + head, other))
+    return lax.ppermute(value, ("seq", "head"), pairs)
+
+
+def to_core(x, y, z, core):
+    return x, y, z, core ^ 1
+
+
+def to_x_far(x, y, z, core):
+    return x ^ 2, y, z, core
+
+
+def to_x_near(x, y, z, core):
+    return x ^ 3, y, z, core
+
+
+HOPS = (("x", 1), ("y", 1), ("y", 3), ("z", 1), ("z", 3))
+
+
+def sum_step(step):
+    def partner(x, y, z, core):
+        axis, bit = HOPS[(step + core) % 5]
+        if axis == "x":
+            return x ^ bit, y, z, core
+        if axis == "y":
+            return x, y ^ bit, z, core
+        return x, y, z ^ bit, core
+
+    return partner
 
 
 def local(
@@ -377,15 +418,15 @@
         pos, out_weight, latent_weight, hidden_low, query_weight, key_weight, query_gain, key_gain
     )
     kv = jnp.concatenate([piece[:, HD:] for piece in pieces], axis=0)
-    kv_x = send(kv, X_HI)
-    kv_c = send(kv, CORE)
-    kv_xc = send(kv_x, CORE)
+    kv_x = trade(kv, to_x_far)
+    kv_c = trade(kv, to_core)
+    kv_xc = trade(kv_x, to_core)
     latent = low_attention(pos, pieces, (kv, kv_c, kv_x, kv_xc), w2, hl)
-    for link in (("head", 1), ("head", 2), ("head", 4), ("seq", 2), ("seq", 4)):
-        latent = (latent.astype(F32) + send(latent, link).astype(F32)).astype(BF)
-    lat_x = send(latent, X_HI)
-    lat_c = send(latent, CORE)
-    lat_xc = send(lat_x, CORE)
+    for step in range(5):
+        latent = (latent.astype(F32) + trade(latent, sum_step(step)).astype(F32)).astype(BF)
+    lat_x = trade(latent, to_x_near)
+    lat_c = trade(latent, to_core)
+    lat_xc = trade(lat_x, to_core)
     attn, up = hi_attention(
         pos,
         (latent, lat_c, lat_x, lat_xc),

time: 134 us -> 196 us (1.46)
  Pallas kernels: 64.4 us -> 137 us
  local copies, waits for them, and re-layouts: 11.4 us -> 2.31 us
  waiting for transfers between devices: 22.3 us -> 20 us
    pallas_call x1, Pallas kernels: 57.3 us -> 113 us  [hi_attention(): pl.pallas_call(hi_kernel, grid_spec=pltpu.PrefetchScalarGridSpec(num_scal...]
    pallas_call x1, Pallas kernels: 2.47 us -> 13.8 us  [pack(): pl.pallas_call(pack_kernel, grid_spec=pltpu.PrefetchScalarGridSpec(num_sc...]
    unnamed x34 -> x22, local copies, waits for them, and re-layouts: 10.5 us -> 1.45 us
    pallas_call x1, Pallas kernels: 1.86 us -> 4.96 us  [prep(): pl.pallas_call(prep_kernel, grid_spec=pltpu.PrefetchScalarGridSpec(num_sc...]
    ppermute x11, waiting for transfers between devices: 19.7 us -> 17.3 us  [trade(): return lax.ppermute(value, ('seq', 'head'), pairs)]
    pallas_call x1, Pallas kernels: 2.78 us -> 4.88 us  [low_attention(): pl.pallas_call(low_kernel, grid_spec=pltpu.PrefetchScalarGridSpec(num_sca...]
  transfers between devices with their start and end apart: 14 -> 14, of which waited for: 8 -> 8; matrix products, arithmetic and copies ran while one was open for 1% -> 0% of each run, Pallas kernels for 1% -> 3%
where the time goes in v2:
time: 196 us
  Pallas kernels  137 us (70%)
  starting transfers between devices  34.7 us (18%)
  waiting for transfers between devices  20 us (10%)
  local copies, waits for them, and re-layouts  2.31 us (1%)
    pallas_call x1, Pallas kernels, hi_attention(): pl.pallas_call(hi_kernel, grid_spec=pltpu.PrefetchScalarGridSpec(num_scal...  113 us
    ppermute x11, starting transfers between devices, trade(): return lax.ppermute(value, ('seq', 'head'), pairs)  28.1 us
    ppermute x11, waiting for transfers between devices, trade(): return lax.ppermute(value, ('seq', 'head'), pairs)  17.3 us
    pallas_call x1, Pallas kernels, pack(): pl.pallas_call(pack_kernel, grid_spec=pltpu.PrefetchScalarGridSpec(num_sc...  13.8 us
    ppermute x3, starting transfers between devices, local(): lax.ppermute(pieces[step], 'seq', z_shift(step))  6.57 us
    pallas_call x1, Pallas kernels, prep(): pl.pallas_call(prep_kernel, grid_spec=pltpu.PrefetchScalarGridSpec(num_sc...  4.96 us
    pallas_call x1, Pallas kernels, low_attention(): pl.pallas_call(low_kernel, grid_spec=pltpu.PrefetchScalarGridSpec(num_sca...  4.88 us
  transfers between devices with their start and end apart: 14, of which 8 were waited for; matrix products, arithmetic and copies ran while one was open for 0% of the time, Pallas kernels for 3%

profile of v2, /device:TPU:1, one launch (start us, length us, event | category | flops | bytes accessed | tf_op | source)
XLA Modules:
  0.0 196.2 jit_solution(7209644762929245302)
XLA Ops:
  0.7 0.7 pad_add_fusion.pos
  1.3 13.8 %pack.1 = (bf16[128,384]{1,0:T(8,128)(2,1)}, bf16[128,384]{1,0:T(8,128)(2,1)}, bf16[128,384]{1,0:T(8,128)(2,1)}, bf16[128,384]{1,0:T(8,128)(2,1)}) custom-call(s32[4]{0:T(128)} %pad_add_fusion.pos, bf16[128,512]{1,0:T(8,128)(2,1)} %q_ref.1, bf16[128,512]{1,0:T(8,128)(2,1)} %k_ref.1, bf16[128,512]{1,0:T(8,128)(2,1)} %v_ref.1), custom_call_target="tpu_custom_call" | custom-call | tf_op jit(solution)/shard_map/pack/pallas_call | solution.py:69
  15.1 2.5 %collective-permute-start = (bf16[128,384]{1,0:T(8,128)(2,1)}, bf16[128,384]{1,0:T(8,128)(2,1)S(1)}, u32[]{:S(2)}, u32[]{:S(2)}) collective-permute-start(bf16[128,384]{1,0:T(8,128)(2,1)} %get-tuple-element.12), channel_id=1, source_target_pairs={{0,16},{8,24},{16,32},{24,40},{32,48},{40,56},{48,0},{56,8},{64,80... | collective-permute-start | bytes 294920 | tf_op jit(solution)/shard_map/ppermute | solution.py:415
  17.7 3.3 %collective-permute-start.1 = (bf16[128,384]{1,0:T(8,128)(2,1)}, bf16[128,384]{1,0:T(8,128)(2,1)S(1)}, u32[]{:S(2)}, u32[]{:S(2)}) collective-permute-start(bf16[128,384]{1,0:T(8,128)(2,1)} %get-tuple-element.13), channel_id=1, source_target_pairs={{0,32},{8,40},{16,48},{24,56},{32,0},{40,8},{48,16},{56,24},{64,96... | collective-permute-start | bytes 294920 | tf_op jit(solution)/shard_map/ppermute | solution.py:415
  21.0 0.7 collective-permute-start.2
  21.7 0.8 slice.12
  22.5 0.0 collective-permute-done.p1
  22.5 0.0 copy-start.2
  22.6 2.6 %collective-permute-done.1.p2 = bf16[128,384]{1,0:T(8,128)(2,1)S(1)} collective-permute-done((bf16[128,384]{1,0:T(8,128)(2,1)}, bf16[128,384]{1,0:T(8,128)(2,1)S(1)}, u32[]{:S(2)}, u32[]{:S(2)}) %collective-permute-start.1) | collective-permute-done | bytes 98336 | tf_op jit(solution)/shard_map/ppermute | solution.py:415
  25.2 0.0 copy-start.3
  25.2 0.0 collective-permute-done.2.p3
  25.2 0.0 copy-start.4
  25.3 0.0 copy-start
  25.3 2.8 %collective-permute-start.4 = (bf16[512,256]{1,0:T(8,128)(2,1)S(1)}, bf16[512,256]{1,0:T(8,128)(2,1)S(1)}, u32[]{:S(2)}, u32[]{:S(2)}) collective-permute-start(bf16[512,256]{1,0:T(8,128)(2,1)S(1)} %pad_maximum_fusion.kv0), channel_id=1, source_target_pairs={{0,64},{1,65},{2,66},{3,67},{4,68},{5,69},{6,70},{7,71},{8,72},{9,... | collective-permute-start | bytes 786440 | tf_op jit(solution)/shard_map/ppermute | solution.py:364
  28.1 2.1 %collective-permute-start.3 = (bf16[512,256]{1,0:T(8,128)(2,1)S(1)}, bf16[512,256]{1,0:T(8,128)(2,1)S(1)}, u32[]{:S(2)}, u32[]{:S(2)}) collective-permute-start(bf16[512,256]{1,0:T(8,128)(2,1)S(1)} %pad_maximum_fusion.kv0), channel_id=1, source_target_pairs={{0,8},{1,9},{2,10},{3,11},{4,12},{5,13},{6,14},{7,15},{8,0},{9,1},... | collective-permute-start | bytes 786440 | tf_op jit(solution)/shard_map/ppermute | solution.py:364
  30.2 2.6 %collective-permute-done.4.kv2 = bf16[512,256]{1,0:T(8,128)(2,1)S(1)} collective-permute-done((bf16[512,256]{1,0:T(8,128)(2,1)S(1)}, bf16[512,256]{1,0:T(8,128)(2,1)S(1)}, u32[]{:S(2)}, u32[]{:S(2)}) %collective-permute-start.4) | collective-permute-done | bytes 262176 | tf_op jit(solution)/shard_map/ppermute | solution.py:364
  32.8 0.0 copy-start.5
  32.8 2.8 %collective-permute-start.5 = (bf16[512,256]{1,0:T(8,128)(2,1)S(1)}, bf16[512,256]{1,0:T(8,128)(2,1)S(1)}, u32[]{:S(2)}, u32[]{:S(2)}) collective-permute-start(bf16[512,256]{1,0:T(8,128)(2,1)S(1)} %collective-permute-done.4.kv2), channel_id=1, source_target_pairs={{0,8},{1,9},{2,10},{3,11},{4,12},{5,13},{6,14},{7,15},{8,0},{9,1},... | collective-permute-start | bytes 786440 | tf_op jit(solution)/shard_map/ppermute | solution.py:364
  35.6 5.0 %prep.1 = (bf16[128,256]{1,0:T(8,128)(2,1)}, f32[16,128]{1,0:T(8,128)}, bf16[4,128,256]{2,1,0:T(8,128)(2,1)}, bf16[128,256]{1,0:T(8,128)(2,1)}, bf16[128,256]{1,0:T(8,128)(2,1)}) custom-call(s32[4]{0:T(128)} %pad_add_fusion.pos, bf16[512,4096]{1,0:T(8,128)(2,1)} %ow.1, bf16[4096,128]{1,0:T(8,128)(2,1)} %lw.1, bf16[128,4096]{1,0:T(8,128)(2,1)} %hid.1, ...), custom_call_target="tpu_custom_call" | custom-call | flops 900000000 | bytes 5000000 | tf_op jit(solution)/shard_map/prep/pallas_call | solution.py:102
  40.5 0.0 copy-done.2
  40.5 0.0 copy-done.3
  40.5 0.0 copy-done.4
  40.5 0.0 copy-done
  40.6 0.0 copy-done.5
  40.6 0.0 collective-permute-done.3.kv1
  40.6 0.0 copy-start.6
  40.6 0.0 collective-permute-done.5.kv3
  40.6 0.0 copy-start.7
  40.6 0.7 copy-done.6
  41.3 0.1 copy-done.7
  41.4 4.9 %low.1 = bf16[512,128]{1,0:T(8,128)(2,1)} custom-call(s32[4]{0:T(128)} %pad_add_fusion.pos, bf16[128,384]{1,0:T(8,128)(2,1)} %get-tuple-element.11.p0, bf16[128,384]{1,0:T(8,128)(2,1)} %copy-done.2, bf16[128,384]{1,0:T(8,128)(2,1)} %copy-done.3, bf16[128,384]{1,0:T(8,128)(2,1)} %copy-done.4, bf16[512,256]{1,0:T(8,128)(2,1)} %copy-done, ...), custom_call_target="tpu_custom_call" | custom-call | tf_op jit(solution)/shard_map/low/pallas_call | solution.py:175
  46.3 1.3 collective-permute-start.6
  47.6 3.0 %collective-permute-done.6 = bf16[512,128]{1,0:T(8,128)(2,1)S(1)} collective-permute-done((bf16[512,128]{1,0:T(8,128)(2,1)}, bf16[512,128]{1,0:T(8,128)(2,1)S(1)}, u32[]{:S(2)}, u32[]{:S(2)}) %collective-permute-start.6) | collective-permute-done | bytes 131104 | tf_op jit(solution)/shard_map/ppermute | solution.py:364
  50.6 0.9 add_convert_fusion.4
  51.5 2.8 %collective-permute-start.7 = (bf16[512,128]{1,0:T(8,128)(2,1)S(1)}, bf16[512,128]{1,0:T(8,128)(2,1)S(1)}, u32[]{:S(2)}, u32[]{:S(2)}) collective-permute-start(bf16[512,128]{1,0:T(8,128)(2,1)S(1)} %add_convert_fusion.4), channel_id=1, source_target_pairs={{0,2},{1,3},{2,0},{3,1},{4,6},{5,7},{6,4},{7,5},{8,14},{9,15},{10,... | collective-permute-start | bytes 393224 | tf_op jit(solution)/shard_map/ppermute | solution.py:364
  54.3 2.4 %collective-permute-done.7 = bf16[512,128]{1,0:T(8,128)(2,1)S(1)} collective-permute-done((bf16[512,128]{1,0:T(8,128)(2,1)S(1)}, bf16[512,128]{1,0:T(8,128)(2,1)S(1)}, u32[]{:S(2)}, u32[]{:S(2)}) %collective-permute-start.7) | collective-permute-done | bytes 131104 | tf_op jit(solution)/shard_map/ppermute | solution.py:364
  56.7 1.9 collective-permute-start.8
  58.7 2.4 %collective-permute-done.8 = bf16[512,128]{1,0:T(8,128)(2,1)S(1)} collective-permute-done((bf16[512,128]{1,0:T(8,128)(2,1)S(1)}, bf16[512,128]{1,0:T(8,128)(2,1)S(1)}, u32[]{:S(2)}, u32[]{:S(2)}) %collective-permute-start.8) | collective-permute-done | bytes 131104 | tf_op jit(solution)/shard_map/ppermute | solution.py:364
  61.1 1.7 collective-permute-start.9
  62.8 3.4 %collective-permute-done.9 = bf16[512,128]{1,0:T(8,128)(2,1)S(1)} collective-permute-done((bf16[512,128]{1,0:T(8,128)(2,1)S(1)}, bf16[512,128]{1,0:T(8,128)(2,1)S(1)}, u32[]{:S(2)}, u32[]{:S(2)}) %collective-permute-start.9) | collective-permute-done | bytes 131104 | tf_op jit(solution)/shard_map/ppermute | solution.py:364
  66.2 1.3 collective-permute-start.10
  67.5 2.6 %collective-permute-done.10 = bf16[512,128]{1,0:T(8,128)(2,1)S(1)} collective-permute-done((bf16[512,128]{1,0:T(8,128)(2,1)S(1)}, bf16[512,128]{1,0:T(8,128)(2,1)S(1)}, u32[]{:S(2)}, u32[]{:S(2)}) %collective-permute-start.10) | collective-permute-done | bytes 131104 | tf_op jit(solution)/shard_map/ppermute | solution.py:364
  70.2 0.0 copy-start.1
  70.2 2.6 %collective-permute-start.12 = (bf16[512,128]{1,0:T(8,128)(2,1)S(1)}, bf16[512,128]{1,0:T(8,128)(2,1)S(1)}, u32[]{:S(2)}, u32[]{:S(2)}) collective-permute-start(bf16[512,128]{1,0:T(8,128)(2,1)S(1)} %add_convert_fusion.lat0), channel_id=1, source_target_pairs={{0,65},{1,64},{2,67},{3,66},{4,69},{5,68},{6,71},{7,70},{8,73},{9,... | collective-permute-start | bytes 393224 | tf_op jit(solution)/shard_map/ppermute | solution.py:364
  72.7 5.4 %collective-permute-start.11 = (bf16[512,128]{1,0:T(8,128)(2,1)S(1)}, bf16[512,128]{1,0:T(8,128)(2,1)S(1)}, u32[]{:S(2)}, u32[]{:S(2)}) collective-permute-start(bf16[512,128]{1,0:T(8,128)(2,1)S(1)} %add_convert_fusion.lat0), channel_id=1, source_target_pairs={{0,8},{1,9},{2,10},{3,11},{4,12},{5,13},{6,14},{7,15},{8,0},{9,1},... | collective-permute-start | bytes 393224 | tf_op jit(solution)/shard_map/ppermute | solution.py:364
  78.1 0.0 collective-permute-done.12.lat2
  78.1 0.0 copy-start.8
  78.1 3.4 %collective-permute-start.13 = (bf16[512,128]{1,0:T(8,128)(2,1)S(1)}, bf16[512,128]{1,0:T(8,128)(2,1)S(1)}, u32[]{:S(2)}, u32[]{:S(2)}) collective-permute-start(bf16[512,128]{1,0:T(8,128)(2,1)S(1)} %collective-permute-done.12.lat2), channel_id=1, source_target_pairs={{0,8},{1,9},{2,10},{3,11},{4,12},{5,13},{6,14},{7,15},{8,0},{9,1},... | collective-permute-start | bytes 393224 | tf_op jit(solution)/shard_map/ppermute | solution.py:364
  81.6 0.0 collective-permute-done.11.lat1
  81.6 0.0 copy-start.9
  81.6 1.0 collective-permute-done.13.lat3
  82.5 0.0 copy-start.10
  82.5 0.0 copy-done.1
  82.5 0.0 copy-done.8
  82.6 0.0 copy-done.9
  82.6 0.6 copy-done.10
  83.2 113.0 %hi.1 = (bf16[512,512]{1,0:T(8,128)(2,1)}, bf16[64,128]{1,0:T(8,128)(2,1)}) custom-call(s32[4]{0:T(128)} %pad_add_fusion.pos, bf16[512,128]{1,0:T(8,128)(2,1)} %copy-done.1, bf16[512,128]{1,0:T(8,128)(2,1)} %copy-done.9, bf16[512,128]{1,0:T(8,128)(2,1)} %copy-done.8, bf16[512,128]{1,0:T(8,128)(2,1)} %copy-done.10, bf16[3456,512]{1,0:T(8,128)(2,1)} %bitcast.9, ...), custom_call_target="tpu_custom_call" | custom-call | tf_op jit(solution)/shard_map/hi/pallas_call | solution.py:325
  (8 shorter events, 0.2 us)
Async XLA Ops:
  15.1 7.4 %collective-permute-start = (bf16[128,384]{1,0:T(8,128)(2,1)}, bf16[128,384]{1,0:T(8,128)(2,1)S(1)}, u32[]{:S(2)}, u32[]{:S(2)}) collective-permute-start(bf16[128,384]{1,0:T(8,128)(2,1)} %get-tuple-element.12), channel_id=1, source_target_pairs={{0,16},{8,24},{16,32},{24,40},{32,48},{40,56},{48,0},{56,8},{64,80... | collective-permute-start | bytes 294920 | tf_op jit(solution)/shard_map/ppermute | solution.py:415
  17.7 7.5 %collective-permute-start.1 = (bf16[128,384]{1,0:T(8,128)(2,1)}, bf16[128,384]{1,0:T(8,128)(2,1)S(1)}, u32[]{:S(2)}, u32[]{:S(2)}) collective-permute-start(bf16[128,384]{1,0:T(8,128)(2,1)} %get-tuple-element.13), channel_id=1, source_target_pairs={{0,32},{8,40},{16,48},{24,56},{32,0},{40,8},{48,16},{56,24},{64,96... | collective-permute-start | bytes 294920 | tf_op jit(solution)/shard_map/ppermute | solution.py:415
  21.0 4.2 %collective-permute-start.2 = (bf16[128,384]{1,0:T(8,128)(2,1)}, bf16[128,384]{1,0:T(8,128)(2,1)S(1)}, u32[]{:S(2)}, u32[]{:S(2)}) collective-permute-start(bf16[128,384]{1,0:T(8,128)(2,1)} %get-tuple-element.14), channel_id=1, source_target_pairs={{0,48},{8,56},{16,0},{24,8},{32,16},{40,24},{48,32},{56,40},{64,11... | collective-permute-start | bytes 294920 | tf_op jit(solution)/shard_map/ppermute | solution.py:415
  22.5 18.0 %copy-start.2 = (bf16[128,384]{1,0:T(8,128)(2,1)}, bf16[128,384]{1,0:T(8,128)(2,1)S(1)}, u32[]{:S(2)}) copy-start(bf16[128,384]{1,0:T(8,128)(2,1)S(1)} %collective-permute-done.p1) | copy-start | bytes 294916
  25.2 15.4 %copy-start.3 = (bf16[128,384]{1,0:T(8,128)(2,1)}, bf16[128,384]{1,0:T(8,128)(2,1)S(1)}, u32[]{:S(2)}) copy-start(bf16[128,384]{1,0:T(8,128)(2,1)S(1)} %collective-permute-done.1.p2) | copy-start | bytes 294916
  25.2 15.3 %copy-start.4 = (bf16[128,384]{1,0:T(8,128)(2,1)}, bf16[128,384]{1,0:T(8,128)(2,1)S(1)}, u32[]{:S(2)}) copy-start(bf16[128,384]{1,0:T(8,128)(2,1)S(1)} %collective-permute-done.2.p3) | copy-start | bytes 294916
  25.3 15.3 %copy-start = (bf16[512,256]{1,0:T(8,128)(2,1)}, bf16[512,256]{1,0:T(8,128)(2,1)S(1)}, u32[]{:S(2)}) copy-start(bf16[512,256]{1,0:T(8,128)(2,1)S(1)} %pad_maximum_fusion.kv0) | copy-start | bytes 786436
  25.3 7.5 %collective-permute-start.4 = (bf16[512,256]{1,0:T(8,128)(2,1)S(1)}, bf16[512,256]{1,0:T(8,128)(2,1)S(1)}, u32[]{:S(2)}, u32[]{:S(2)}) collective-permute-start(bf16[512,256]{1,0:T(8,128)(2,1)S(1)} %pad_maximum_fusion.kv0), channel_id=1, source_target_pairs={{0,64},{1,65},{2,66},{3,67},{4,68},{5,69},{6,70},{7,71},{8,72},{9,... | collective-permute-start | bytes 786440 | tf_op jit(solution)/shard_map/ppermute | solution.py:364
  28.1 12.5 %collective-permute-start.3 = (bf16[512,256]{1,0:T(8,128)(2,1)S(1)}, bf16[512,256]{1,0:T(8,128)(2,1)S(1)}, u32[]{:S(2)}, u32[]{:S(2)}) collective-permute-start(bf16[512,256]{1,0:T(8,128)(2,1)S(1)} %pad_maximum_fusion.kv0), channel_id=1, source_target_pairs={{0,8},{1,9},{2,10},{3,11},{4,12},{5,13},{6,14},{7,15},{8,0},{9,1},... | collective-permute-start | bytes 786440 | tf_op jit(solution)/shard_map/ppermute | solution.py:364
  32.8 7.8 %copy-start.5 = (bf16[512,256]{1,0:T(8,128)(2,1)}, bf16[512,256]{1,0:T(8,128)(2,1)S(1)}, u32[]{:S(2)}) copy-start(bf16[512,256]{1,0:T(8,128)(2,1)S(1)} %collective-permute-done.4.kv2) | copy-start | bytes 786436
  32.8 7.8 %collective-permute-start.5 = (bf16[512,256]{1,0:T(8,128)(2,1)S(1)}, bf16[512,256]{1,0:T(8,128)(2,1)S(1)}, u32[]{:S(2)}, u32[]{:S(2)}) collective-permute-start(bf16[512,256]{1,0:T(8,128)(2,1)S(1)} %collective-permute-done.4.kv2), channel_id=1, source_target_pairs={{0,8},{1,9},{2,10},{3,11},{4,12},{5,13},{6,14},{7,15},{8,0},{9,1},... | collective-permute-start | bytes 786440 | tf_op jit(solution)/shard_map/ppermute | solution.py:364
  40.6 0.7 copy-start.6
  40.6 0.8 copy-start.7
  46.3 4.3 %collective-permute-start.6 = (bf16[512,128]{1,0:T(8,128)(2,1)}, bf16[512,128]{1,0:T(8,128)(2,1)S(1)}, u32[]{:S(2)}, u32[]{:S(2)}) collective-permute-start(bf16[512,128]{1,0:T(8,128)(2,1)} %low.1), channel_id=1, source_target_pairs={{0,1},{1,0},{2,3},{3,2},{4,5},{5,4},{6,7},{7,6},{8,10},{9,11},{10,... | collective-permute-start | bytes 393224 | tf_op jit(solution)/shard_map/ppermute | solution.py:364
  51.5 5.2 %collective-permute-start.7 = (bf16[512,128]{1,0:T(8,128)(2,1)S(1)}, bf16[512,128]{1,0:T(8,128)(2,1)S(1)}, u32[]{:S(2)}, u32[]{:S(2)}) collective-permute-start(bf16[512,128]{1,0:T(8,128)(2,1)S(1)} %add_convert_fusion.4), channel_id=1, source_target_pairs={{0,2},{1,3},{2,0},{3,1},{4,6},{5,7},{6,4},{7,5},{8,14},{9,15},{10,... | collective-permute-start | bytes 393224 | tf_op jit(solution)/shard_map/ppermute | solution.py:364
  56.7 4.3 %collective-permute-start.8 = (bf16[512,128]{1,0:T(8,128)(2,1)S(1)}, bf16[512,128]{1,0:T(8,128)(2,1)S(1)}, u32[]{:S(2)}, u32[]{:S(2)}) collective-permute-start(bf16[512,128]{1,0:T(8,128)(2,1)S(1)} %add_convert_fusion.3), channel_id=1, source_target_pairs={{0,6},{1,7},{2,4},{3,5},{4,2},{5,3},{6,0},{7,1},{8,24},{9,25},{10,... | collective-permute-start | bytes 393224 | tf_op jit(solution)/shard_map/ppermute | solution.py:364
  61.1 5.1 %collective-permute-start.9 = (bf16[512,128]{1,0:T(8,128)(2,1)S(1)}, bf16[512,128]{1,0:T(8,128)(2,1)S(1)}, u32[]{:S(2)}, u32[]{:S(2)}) collective-permute-start(bf16[512,128]{1,0:T(8,128)(2,1)S(1)} %add_convert_fusion.2), channel_id=1, source_target_pairs={{0,16},{1,17},{2,18},{3,19},{4,20},{5,21},{6,22},{7,23},{8,56},{9,... | collective-permute-start | bytes 393224 | tf_op jit(solution)/shard_map/ppermute | solution.py:364
  66.2 3.9 %collective-permute-start.10 = (bf16[512,128]{1,0:T(8,128)(2,1)S(1)}, bf16[512,128]{1,0:T(8,128)(2,1)S(1)}, u32[]{:S(2)}, u32[]{:S(2)}) collective-permute-start(bf16[512,128]{1,0:T(8,128)(2,1)S(1)} %add_convert_fusion.1), channel_id=1, source_target_pairs={{0,48},{1,49},{2,50},{3,51},{4,52},{5,53},{6,54},{7,55},{8,9},{9,8... | collective-permute-start | bytes 393224 | tf_op jit(solution)/shard_map/ppermute | solution.py:364
  70.2 12.4 %copy-start.1 = (bf16[512,128]{1,0:T(8,128)(2,1)}, bf16[512,128]{1,0:T(8,128)(2,1)S(1)}, u32[]{:S(2)}) copy-start(bf16[512,128]{1,0:T(8,128)(2,1)S(1)} %add_convert_fusion.lat0) | copy-start | bytes 393220
  70.2 7.9 %collective-permute-start.12 = (bf16[512,128]{1,0:T(8,128)(2,1)S(1)}, bf16[512,128]{1,0:T(8,128)(2,1)S(1)}, u32[]{:S(2)}, u32[]{:S(2)}) collective-permute-start(bf16[512,128]{1,0:T(8,128)(2,1)S(1)} %add_convert_fusion.lat0), channel_id=1, source_target_pairs={{0,65},{1,64},{2,67},{3,66},{4,69},{5,68},{6,71},{7,70},{8,73},{9,... | collective-permute-start | bytes 393224 | tf_op jit(solution)/shard_map/ppermute | solution.py:364
  72.7 8.8 %collective-permute-start.11 = (bf16[512,128]{1,0:T(8,128)(2,1)S(1)}, bf16[512,128]{1,0:T(8,128)(2,1)S(1)}, u32[]{:S(2)}, u32[]{:S(2)}) collective-permute-start(bf16[512,128]{1,0:T(8,128)(2,1)S(1)} %add_convert_fusion.lat0), channel_id=1, source_target_pairs={{0,8},{1,9},{2,10},{3,11},{4,12},{5,13},{6,14},{7,15},{8,0},{9,1},... | collective-permute-start | bytes 393224 | tf_op jit(solution)/shard_map/ppermute | solution.py:364
  78.1 4.4 %copy-start.8 = (bf16[512,128]{1,0:T(8,128)(2,1)}, bf16[512,128]{1,0:T(8,128)(2,1)S(1)}, u32[]{:S(2)}) copy-start(bf16[512,128]{1,0:T(8,128)(2,1)S(1)} %collective-permute-done.12.lat2) | copy-start | bytes 393220
  78.1 4.4 %collective-permute-start.13 = (bf16[512,128]{1,0:T(8,128)(2,1)S(1)}, bf16[512,128]{1,0:T(8,128)(2,1)S(1)}, u32[]{:S(2)}, u32[]{:S(2)}) collective-permute-start(bf16[512,128]{1,0:T(8,128)(2,1)S(1)} %collective-permute-done.12.lat2), channel_id=1, source_target_pairs={{0,8},{1,9},{2,10},{3,11},{4,12},{5,13},{6,14},{7,15},{8,0},{9,1},... | collective-permute-start | bytes 393224 | tf_op jit(solution)/shard_map/ppermute | solution.py:364
  81.6 1.0 copy-start.9
  82.5 0.6 copy-start.10

commit v3 on v2

--- a/solution.py
+++ b/solution.py
@@ -18,7 +18,7 @@
 SCALE = LOG2E / math.sqrt(HD)
 BF = jnp.bfloat16
 F32 = jnp.float32
-VMEM = 60 * 2**20
+SMALL, LARGE = 16 * 2**20, 46 * 2**20
 NT = (((1,), (1,)), ((), ()))
 
 
@@ -46,39 +46,29 @@
     return pl.BlockSpec(shape, lambda *_: (0,) * len(shape))
 
 
-def pack_kernel(pos, q_ref, k_ref, v_ref, o0, o1, o2, o3, sems):
-    copies = []
-    for shift, out in enumerate((o0, o1, o2, o3)):
+def pack_kernel(pos, q_ref, k_ref, v_ref, *outs):
+    for shift, out in enumerate(outs):
         head = lax.rem(pos[1] + shift, 4)
         columns = pl.ds(pl.multiple_of(head * HD, HD), HD)
-        for part, ref in enumerate((q_ref, k_ref, v_ref)):
-            copies.append(
-                pltpu.make_async_copy(
-                    ref.at[:, columns], out.at[:, part * HD : (part + 1) * HD], sems.at[shift, part]
-                )
-            )
-    for copy in copies:
-        copy.start()
-    for copy in copies:
-        copy.wait()
+        out[:, 0:HD] = q_ref[:, columns]
+        out[:, HD : 2 * HD] = k_ref[:, columns]
+        out[:, 2 * HD : 3 * HD] = v_ref[:, columns]
 
 
 def pack(pos, q, k, v):
-    piece = jax.ShapeDtypeStruct((TOK, 3 * HD), BF)
-    anywhere = pl.BlockSpec(memory_space=pl.ANY)
+    piece = pltpu.VMEM((TOK, 3 * HD), BF)
     return pl.pallas_call(
         pack_kernel,
         grid_spec=pltpu.PrefetchScalarGridSpec(
             num_scalar_prefetch=1,
             grid=(1,),
-            in_specs=[anywhere] * 3,
-            out_specs=[anywhere] * 4,
-            scratch_shapes=[pltpu.SemaphoreType.DMA((4, 3))],
+            in_specs=[whole(q.shape)] * 3,
+            out_specs=[whole(piece.shape)] * 4,
         ),
         out_shape=[piece] * 4,
-        compiler_params=pltpu.CompilerParams(vmem_limit_bytes=VMEM),
+        compiler_params=pltpu.CompilerParams(vmem_limit_bytes=SMALL),
         name="pack",
-    )(pos, q, k, v)
+    )(pos, *(pltpu.with_memory_space_constraint(array, pltpu.HBM) for array in (q, k, v)))
 
 
 def prep_kernel(pos, ow, lw, hid, wqh, wkh, gq, gk, wq, wk, w2_out, hl_out, m_out, gq_out, gk_out):
@@ -130,20 +120,25 @@
             jax.ShapeDtypeStruct((HD, 2 * HD), BF),
             jax.ShapeDtypeStruct((HD, 2 * HD), BF),
         ],
-        compiler_params=pltpu.CompilerParams(vmem_limit_bytes=VMEM),
+        compiler_params=pltpu.CompilerParams(vmem_limit_bytes=SMALL),
         cost_estimate=pl.CostEstimate(flops=900_000_000, bytes_accessed=5_000_000, transcendentals=0),
         name="prep",
     )(
         pos,
-        out_weight,
-        latent_weight,
-        hidden,
-        query_weight,
-        key_weight,
-        query_gain.reshape(1, -1),
-        key_gain.reshape(1, -1),
-        query_weight,
-        key_weight,
+        *(
+            pltpu.with_memory_space_constraint(array, pltpu.HBM)
+            for array in (
+                out_weight,
+                latent_weight,
+                hidden,
+                query_weight,
+                key_weight,
+                query_gain.reshape(1, -1),
+                key_gain.reshape(1, -1),
+                query_weight,
+                key_weight,
+            )
+        ),
     )
 
 
@@ -181,8 +176,8 @@
             out_specs=whole((4 * TOK, HD)),
             scratch_shapes=[pltpu.VMEM((4, TOK, HD), BF), pltpu.VMEM((4 * TOK, HD), F32)],
         ),
-        out_shape=jax.ShapeDtypeStruct((4 * TOK, HD), BF),
-        compiler_params=pltpu.CompilerParams(vmem_limit_bytes=VMEM),
+        out_shape=pltpu.VMEM((4 * TOK, HD), BF),
+        compiler_params=pltpu.CompilerParams(vmem_limit_bytes=2 * SMALL),
         name="low",
     )(pos, *args)
 
@@ -198,7 +193,7 @@
     lat1,
     lat2,
     lat3,
-    conv,
+    conv_hbm,
     b1,
     second,
     b2,
@@ -216,8 +211,12 @@
     nat_s,
     acc_s,
     bound_s,
+    conv,
+    conv_sem,
 ):
     x, z, c, g = pos[0], pos[1], pos[2], pos[3]
+    fetch = pltpu.make_async_copy(conv_hbm, conv, conv_sem)
+    fetch.start()
     for dx, dc, piece in ((0, 0, lat0), (0, 1, lat1), (1, 0, lat2), (1, 1, lat3)):
         px = lax.bitwise_xor(x, dx)
         pc = lax.bitwise_xor(c, dc)
@@ -232,6 +231,7 @@
         grid_s[index, 1 : FRAMES + 1, 1 : H_LO + 1] = shifted.astype(BF).reshape(FRAMES, H_LO, W_LO, HD)
 
     val_s[:, HD : 2 * HD] = jnp.ones((KEYS, HD), BF)
+    fetch.wait()
     biggest = jnp.zeros((1, 1), F32)
     rows = CHUNK * TOK
     for first in range(0, FRAMES, CHUNK):
@@ -322,6 +322,7 @@
     args = (*lats, conv, bias_first.reshape(1, -1), conv_second, bias_second.reshape(1, -1), gq, gk, m, value_weight)
     in_specs = [whole(a.shape) for a in args]
     in_specs[-1] = pl.BlockSpec((HD, 4 * HD), lambda i, pos: (0, pos[3]))
+    in_specs[len(lats)] = pl.BlockSpec(memory_space=pltpu.HBM)
     return pl.pallas_call(
         hi_kernel,
         grid_spec=pltpu.PrefetchScalarGridSpec(
@@ -338,13 +339,15 @@
                 pltpu.VMEM((4 * TOK, HD), F32),
                 pltpu.VMEM((4, 4 * TOK, 2 * HD), F32),
                 pltpu.VMEM((4, 4 * TOK, HD), F32),
+                pltpu.VMEM(conv.shape, BF),
+                pltpu.SemaphoreType.DMA,
             ],
         ),
         out_shape=[
             jax.ShapeDtypeStruct((4 * TOK, 4 * HD), BF),
             jax.ShapeDtypeStruct((2 * W_LO, HD), BF),
         ],
-        compiler_params=pltpu.CompilerParams(vmem_limit_bytes=VMEM),
+        compiler_params=pltpu.CompilerParams(vmem_limit_bytes=LARGE),
         name="hi",
     )(pos, *args)
 
@@ -420,6 +423,7 @@
     kv = jnp.concatenate([piece[:, HD:] for piece in pieces], axis=0)
     kv_x = trade(kv, to_x_far)
     kv_c = trade(kv, to_core)
+    kv_x, w2, hl, m, gq, gk = lax.optimization_barrier((kv_x, w2, hl, m, gq, gk))
     kv_xc = trade(kv_x, to_core)
     latent = low_attention(pos, pieces, (kv, kv_c, kv_x, kv_xc), w2, hl)
     for step in range(5):

time: 196 us -> 174 us (0.89)
  Pallas kernels: 137 us -> 120 us
  local copies, waits for them, and re-layouts: 2.31 us -> 0.04 us
    pallas_call x1, Pallas kernels: 13.8 us -> 1.64 us  [pack(): pl.pallas_call(pack_kernel, grid_spec=pltpu.PrefetchScalarGridSpec(num_sc...]
    pallas_call x1, Pallas kernels: 4.88 us -> 2.78 us  [low_attention(): pl.pallas_call(low_kernel, grid_spec=pltpu.PrefetchScalarGridSpec(num_sca...]
  transfers between devices with their start and end apart: 14 -> 14, of which waited for: 8 -> 10; matrix products, arithmetic and copies ran while one was open for 0% -> 0% of each run, Pallas kernels for 3% -> 2%
where the time goes in v3:
time: 174 us
  Pallas kernels  120 us (69%)
  starting transfers between devices  33.5 us (19%)
  waiting for transfers between devices  19 us (11%)
    pallas_call x1, Pallas kernels, hi_attention(): pl.pallas_call(hi_kernel, grid_spec=pltpu.PrefetchScalarGridSpec(num_scal...  111 us
    ppermute x11, starting transfers between devices, trade(): return lax.ppermute(value, ('seq', 'head'), pairs)  26.9 us
    ppermute x11, waiting for transfers between devices, trade(): return lax.ppermute(value, ('seq', 'head'), pairs)  15.7 us
    ppermute x3, starting transfers between devices, local(): lax.ppermute(pieces[step], 'seq', z_shift(step))  6.57 us
    pallas_call x1, Pallas kernels, prep(): pl.pallas_call(prep_kernel, grid_spec=pltpu.PrefetchScalarGridSpec(num_sc...  4.2 us
  transfers between devices with their start and end apart: 14, of which 10 were waited for; matrix products, arithmetic and copies ran while one was open for 0% of the time, Pallas kernels for 2%

profile of v3, /device:TPU:1, one launch (start us, length us, event | category | flops | bytes accessed | tf_op | source)
XLA Modules:
  0.0 173.6 jit_solution(6552451385294159142)
XLA Ops:
  0.7 0.1 pad_add_fusion.pos
  0.7 1.6 pack.1
  2.4 2.5 %collective-permute-start = (bf16[128,384]{1,0:T(8,128)(2,1)S(1)}, bf16[128,384]{1,0:T(8,128)(2,1)S(1)}, u32[]{:S(2)}, u32[]{:S(2)}) collective-permute-start(bf16[128,384]{1,0:T(8,128)(2,1)S(1)} %get-tuple-element.18), channel_id=1, source_target_pairs={{0,16},{8,24},{16,32},{24,40},{32,48},{40,56},{48,0},{56,8},{64,80... | collective-permute-start | bytes 294920 | tf_op jit(solution)/shard_map/ppermute | solution.py:418
  4.9 3.3 %collective-permute-start.1 = (bf16[128,384]{1,0:T(8,128)(2,1)S(1)}, bf16[128,384]{1,0:T(8,128)(2,1)S(1)}, u32[]{:S(2)}, u32[]{:S(2)}) collective-permute-start(bf16[128,384]{1,0:T(8,128)(2,1)S(1)} %get-tuple-element.19), channel_id=1, source_target_pairs={{0,32},{8,40},{16,48},{24,56},{32,0},{40,8},{48,16},{56,24},{64,96... | collective-permute-start | bytes 294920 | tf_op jit(solution)/shard_map/ppermute | solution.py:418
  8.2 0.7 collective-permute-start.2
  9.0 0.6 collective-permute-done.p1
  9.6 2.7 %collective-permute-done.1.p2 = bf16[128,384]{1,0:T(8,128)(2,1)S(1)} collective-permute-done((bf16[128,384]{1,0:T(8,128)(2,1)S(1)}, bf16[128,384]{1,0:T(8,128)(2,1)S(1)}, u32[]{:S(2)}, u32[]{:S(2)}) %collective-permute-start.1) | collective-permute-done | bytes 98336 | tf_op jit(solution)/shard_map/ppermute | solution.py:418
  12.3 0.0 collective-permute-done.2.p3
  12.3 2.8 %collective-permute-start.4 = (bf16[512,256]{1,0:T(8,128)(2,1)S(1)}, bf16[512,256]{1,0:T(8,128)(2,1)S(1)}, u32[]{:S(2)}, u32[]{:S(2)}) collective-permute-start(bf16[512,256]{1,0:T(8,128)(2,1)S(1)} %pad_maximum_fusion.kv0), channel_id=1, source_target_pairs={{0,64},{1,65},{2,66},{3,67},{4,68},{5,69},{6,70},{7,71},{8,72},{9,... | collective-permute-start | bytes 786440 | tf_op jit(solution)/shard_map/ppermute | solution.py:367
  15.1 0.0 copy-start.1
  15.1 0.0 copy-start.2
  15.1 0.0 copy-start.3
  15.1 0.0 copy-start.4
  15.1 4.2 %prep.1 = (bf16[128,256]{1,0:T(8,128)(2,1)S(1)}, f32[16,128]{1,0:T(8,128)S(1)}, bf16[4,128,256]{2,1,0:T(8,128)(2,1)S(1)}, bf16[128,256]{1,0:T(8,128)(2,1)S(1)}, bf16[128,256]{1,0:T(8,128)(2,1)S(1)}) custom-call(s32[4]{0:T(128)S(1)} %pad_add_fusion.pos, bf16[512,4096]{1,0:T(8,128)(2,1)} %ow.1, bf16[4096,128]{1,0:T(8,128)(2,1)} %lw.1, bf16[128,4096]{1,0:T(8,128)(2,1)} %hid.1, ...), custom_call_target="tpu_custom_call" | custom-call | flops 900000000 | bytes 5000000 | tf_op jit(solution)/shard_map/prep/pallas_call | solution.py:92
  19.3 0.0 copy-start
  19.4 2.2 %collective-permute-start.3 = (bf16[512,256]{1,0:T(8,128)(2,1)S(1)}, bf16[512,256]{1,0:T(8,128)(2,1)S(1)}, u32[]{:S(2)}, u32[]{:S(2)}) collective-permute-start(bf16[512,256]{1,0:T(8,128)(2,1)S(1)} %pad_maximum_fusion.kv0), channel_id=1, source_target_pairs={{0,8},{1,9},{2,10},{3,11},{4,12},{5,13},{6,14},{7,15},{8,0},{9,1},... | collective-permute-start | bytes 786440 | tf_op jit(solution)/shard_map/ppermute | solution.py:367
  21.6 0.0 collective-permute-done.4.kv2
  21.6 1.0 collective-permute-start.5
  22.6 0.1 collective-permute-done.3.kv1
  22.7 1.0 collective-permute-done.5.kv3
  23.8 2.8 %low.1 = bf16[512,128]{1,0:T(8,128)(2,1)S(1)} custom-call(s32[4]{0:T(128)S(1)} %pad_add_fusion.pos, bf16[128,384]{1,0:T(8,128)(2,1)S(1)} %get-tuple-element.17.p0, bf16[128,384]{1,0:T(8,128)(2,1)S(1)} %collective-permute-done.p1, bf16[128,384]{1,0:T(8,128)(2,1)S(1)} %collective-permute-done.1.p2, bf16[128,384]{1,0:T(8,128)(2,1)S(1)} %collective-permute-done.2.p3, ...), custom_call_target="tpu_custom_call" | custom-call | tf_op jit(solution)/shard_map/low/pallas_call | solution.py:170
  26.6 1.4 collective-permute-start.6
  27.9 2.8 %collective-permute-done.6 = bf16[512,128]{1,0:T(8,128)(2,1)S(1)} collective-permute-done((bf16[512,128]{1,0:T(8,128)(2,1)S(1)}, bf16[512,128]{1,0:T(8,128)(2,1)S(1)}, u32[]{:S(2)}, u32[]{:S(2)}) %collective-permute-start.6) | collective-permute-done | bytes 131104 | tf_op jit(solution)/shard_map/ppermute | solution.py:367
  30.8 2.8 %collective-permute-start.7 = (bf16[512,128]{1,0:T(8,128)(2,1)S(1)}, bf16[512,128]{1,0:T(8,128)(2,1)S(1)}, u32[]{:S(2)}, u32[]{:S(2)}) collective-permute-start(bf16[512,128]{1,0:T(8,128)(2,1)S(1)} %add_convert_fusion.4), channel_id=1, source_target_pairs={{0,2},{1,3},{2,0},{3,1},{4,6},{5,7},{6,4},{7,5},{8,14},{9,15},{10,... | collective-permute-start | bytes 393224 | tf_op jit(solution)/shard_map/ppermute | solution.py:367
  33.6 2.4 %collective-permute-done.7 = bf16[512,128]{1,0:T(8,128)(2,1)S(1)} collective-permute-done((bf16[512,128]{1,0:T(8,128)(2,1)S(1)}, bf16[512,128]{1,0:T(8,128)(2,1)S(1)}, u32[]{:S(2)}, u32[]{:S(2)}) %collective-permute-start.7) | collective-permute-done | bytes 131104 | tf_op jit(solution)/shard_map/ppermute | solution.py:367
  36.0 1.9 %collective-permute-start.8 = (bf16[512,128]{1,0:T(8,128)(2,1)S(1)}, bf16[512,128]{1,0:T(8,128)(2,1)S(1)}, u32[]{:S(2)}, u32[]{:S(2)}) collective-permute-start(bf16[512,128]{1,0:T(8,128)(2,1)S(1)} %add_convert_fusion.3), channel_id=1, source_target_pairs={{0,6},{1,7},{2,4},{3,5},{4,2},{5,3},{6,0},{7,1},{8,24},{9,25},{10,... | collective-permute-start | bytes 393224 | tf_op jit(solution)/shard_map/ppermute | solution.py:367
  37.9 2.4 %collective-permute-done.8 = bf16[512,128]{1,0:T(8,128)(2,1)S(1)} collective-permute-done((bf16[512,128]{1,0:T(8,128)(2,1)S(1)}, bf16[512,128]{1,0:T(8,128)(2,1)S(1)}, u32[]{:S(2)}, u32[]{:S(2)}) %collective-permute-start.8) | collective-permute-done | bytes 131104 | tf_op jit(solution)/shard_map/ppermute | solution.py:367
  40.3 1.7 collective-permute-start.9
  42.1 3.4 %collective-permute-done.9 = bf16[512,128]{1,0:T(8,128)(2,1)S(1)} collective-permute-done((bf16[512,128]{1,0:T(8,128)(2,1)S(1)}, bf16[512,128]{1,0:T(8,128)(2,1)S(1)}, u32[]{:S(2)}, u32[]{:S(2)}) %collective-permute-start.9) | collective-permute-done | bytes 131104 | tf_op jit(solution)/shard_map/ppermute | solution.py:367
  45.5 1.3 collective-permute-start.10
  46.8 2.6 %collective-permute-done.10 = bf16[512,128]{1,0:T(8,128)(2,1)S(1)} collective-permute-done((bf16[512,128]{1,0:T(8,128)(2,1)S(1)}, bf16[512,128]{1,0:T(8,128)(2,1)S(1)}, u32[]{:S(2)}, u32[]{:S(2)}) %collective-permute-start.10) | collective-permute-done | bytes 131104 | tf_op jit(solution)/shard_map/ppermute | solution.py:367
  49.4 2.6 %collective-permute-start.12 = (bf16[512,128]{1,0:T(8,128)(2,1)S(1)}, bf16[512,128]{1,0:T(8,128)(2,1)S(1)}, u32[]{:S(2)}, u32[]{:S(2)}) collective-permute-start(bf16[512,128]{1,0:T(8,128)(2,1)S(1)} %add_convert_fusion.lat0), channel_id=1, source_target_pairs={{0,65},{1,64},{2,67},{3,66},{4,69},{5,68},{6,71},{7,70},{8,73},{9,... | collective-permute-start | bytes 393224 | tf_op jit(solution)/shard_map/ppermute | solution.py:367
  52.0 5.8 %collective-permute-start.11 = (bf16[512,128]{1,0:T(8,128)(2,1)S(1)}, bf16[512,128]{1,0:T(8,128)(2,1)S(1)}, u32[]{:S(2)}, u32[]{:S(2)}) collective-permute-start(bf16[512,128]{1,0:T(8,128)(2,1)S(1)} %add_convert_fusion.lat0), channel_id=1, source_target_pairs={{0,8},{1,9},{2,10},{3,11},{4,12},{5,13},{6,14},{7,15},{8,0},{9,1},... | collective-permute-start | bytes 393224 | tf_op jit(solution)/shard_map/ppermute | solution.py:367
  57.8 0.0 collective-permute-done.12.lat2
  57.8 3.4 %collective-permute-start.13 = (bf16[512,128]{1,0:T(8,128)(2,1)S(1)}, bf16[512,128]{1,0:T(8,128)(2,1)S(1)}, u32[]{:S(2)}, u32[]{:S(2)}) collective-permute-start(bf16[512,128]{1,0:T(8,128)(2,1)S(1)} %collective-permute-done.12.lat2), channel_id=1, source_target_pairs={{0,8},{1,9},{2,10},{3,11},{4,12},{5,13},{6,14},{7,15},{8,0},{9,1},... | collective-permute-start | bytes 393224 | tf_op jit(solution)/shard_map/ppermute | solution.py:367
  61.2 0.0 collective-permute-done.11.lat1
  61.2 1.0 collective-permute-done.13.lat3
  62.2 0.0 copy-done.1
  62.2 0.0 copy-done.2
  62.2 0.0 copy-done.3
  62.2 0.0 copy-done.4
  62.2 0.0 copy-done
  62.2 111.2 %hi.1 = (bf16[512,512]{1,0:T(8,128)(2,1)}, bf16[64,128]{1,0:T(8,128)(2,1)}) custom-call(s32[4]{0:T(128)S(1)} %pad_add_fusion.pos, bf16[512,128]{1,0:T(8,128)(2,1)S(1)} %add_convert_fusion.lat0, bf16[512,128]{1,0:T(8,128)(2,1)S(1)} %collective-permute-done.11.lat1, bf16[512,128]{1,0:T(8,128)(2,1)S(1)} %collective-permute-done.12.lat2, ...), custom_call_target="tpu_custom_call" | custom-call | tf_op jit(solution)/shard_map/hi/pallas_call | solution.py:326
  (10 shorter events, 0.2 us)
Async XLA Ops:
  2.4 7.2 %collective-permute-start = (bf16[128,384]{1,0:T(8,128)(2,1)S(1)}, bf16[128,384]{1,0:T(8,128)(2,1)S(1)}, u32[]{:S(2)}, u32[]{:S(2)}) collective-permute-start(bf16[128,384]{1,0:T(8,128)(2,1)S(1)} %get-tuple-element.18), channel_id=1, source_target_pairs={{0,16},{8,24},{16,32},{24,40},{32,48},{40,56},{48,0},{56,8},{64,80... | collective-permute-start | bytes 294920 | tf_op jit(solution)/shard_map/ppermute | solution.py:418
  4.9 7.3 %collective-permute-start.1 = (bf16[128,384]{1,0:T(8,128)(2,1)S(1)}, bf16[128,384]{1,0:T(8,128)(2,1)S(1)}, u32[]{:S(2)}, u32[]{:S(2)}) collective-permute-start(bf16[128,384]{1,0:T(8,128)(2,1)S(1)} %get-tuple-element.19), channel_id=1, source_target_pairs={{0,32},{8,40},{16,48},{24,56},{32,0},{40,8},{48,16},{56,24},{64,96... | collective-permute-start | bytes 294920 | tf_op jit(solution)/shard_map/ppermute | solution.py:418
  8.2 4.0 %collective-permute-start.2 = (bf16[128,384]{1,0:T(8,128)(2,1)S(1)}, bf16[128,384]{1,0:T(8,128)(2,1)S(1)}, u32[]{:S(2)}, u32[]{:S(2)}) collective-permute-start(bf16[128,384]{1,0:T(8,128)(2,1)S(1)} %get-tuple-element.20), channel_id=1, source_target_pairs={{0,48},{8,56},{16,0},{24,8},{32,16},{40,24},{48,32},{56,40},{64,11... | collective-permute-start | bytes 294920 | tf_op jit(solution)/shard_map/ppermute | solution.py:418
  12.3 9.3 %collective-permute-start.4 = (bf16[512,256]{1,0:T(8,128)(2,1)S(1)}, bf16[512,256]{1,0:T(8,128)(2,1)S(1)}, u32[]{:S(2)}, u32[]{:S(2)}) collective-permute-start(bf16[512,256]{1,0:T(8,128)(2,1)S(1)} %pad_maximum_fusion.kv0), channel_id=1, source_target_pairs={{0,64},{1,65},{2,66},{3,67},{4,68},{5,69},{6,70},{7,71},{8,72},{9,... | collective-permute-start | bytes 786440 | tf_op jit(solution)/shard_map/ppermute | solution.py:367
  15.1 47.0 %copy-start.1 = (bf16[128,4096]{1,0:T(8,128)(2,1)S(1)}, bf16[128,4096]{1,0:T(8,128)(2,1)}, u32[]{:S(2)}) copy-start(bf16[128,4096]{1,0:T(8,128)(2,1)} %wv.1) | copy-start | bytes 3145732
  15.1 47.0 %copy-start.2 = (bf16[512,512]{1,0:T(8,128)(2,1)S(1)}, bf16[512,512]{1,0:T(8,128)(2,1)}, u32[]{:S(2)}) copy-start(bf16[512,512]{1,0:T(8,128)(2,1)} %second.1) | copy-start | bytes 1572868
  15.1 47.0 %copy-start.3 = (f32[512]{0:T(512)S(1)}, f32[512]{0:T(512)}, u32[]{:S(2)}) copy-start(f32[512]{0:T(512)} %param.22) | copy-start | bytes 6148
  15.1 47.0 %copy-start.4 = (f32[512]{0:T(512)S(1)}, f32[512]{0:T(512)}, u32[]{:S(2)}) copy-start(f32[512]{0:T(512)} %param.24) | copy-start | bytes 6148
  19.3 42.8 %copy-start = (bf16[3,3,3,128,512]{4,3,2,1,0:T(8,128)(2,1)S(1)}, bf16[3,3,3,128,512]{4,3,2,1,0:T(8,128)(2,1)}, u32[]{:S(2)}) copy-start(bf16[3,3,3,128,512]{4,3,2,1,0:T(8,128)(2,1)} %param.21) | copy-start | bytes 10616836
  19.4 3.4 %collective-permute-start.3 = (bf16[512,256]{1,0:T(8,128)(2,1)S(1)}, bf16[512,256]{1,0:T(8,128)(2,1)S(1)}, u32[]{:S(2)}, u32[]{:S(2)}) collective-permute-start(bf16[512,256]{1,0:T(8,128)(2,1)S(1)} %pad_maximum_fusion.kv0), channel_id=1, source_target_pairs={{0,8},{1,9},{2,10},{3,11},{4,12},{5,13},{6,14},{7,15},{8,0},{9,1},... | collective-permute-start | bytes 786440 | tf_op jit(solution)/shard_map/ppermute | solution.py:367
  21.6 2.2 %collective-permute-start.5 = (bf16[512,256]{1,0:T(8,128)(2,1)S(1)}, bf16[512,256]{1,0:T(8,128)(2,1)S(1)}, u32[]{:S(2)}, u32[]{:S(2)}) collective-permute-start(bf16[512,256]{1,0:T(8,128)(2,1)S(1)} %collective-permute-done.4.kv2), channel_id=1, source_target_pairs={{0,8},{1,9},{2,10},{3,11},{4,12},{5,13},{6,14},{7,15},{8,0},{9,1},... | collective-permute-start | bytes 786440 | tf_op jit(solution)/shard_map/ppermute | solution.py:367
  26.6 4.2 %collective-permute-start.6 = (bf16[512,128]{1,0:T(8,128)(2,1)S(1)}, bf16[512,128]{1,0:T(8,128)(2,1)S(1)}, u32[]{:S(2)}, u32[]{:S(2)}) collective-permute-start(bf16[512,128]{1,0:T(8,128)(2,1)S(1)} %low.1), channel_id=1, source_target_pairs={{0,1},{1,0},{2,3},{3,2},{4,5},{5,4},{6,7},{7,6},{8,10},{9,11},{10,... | collective-permute-start | bytes 393224 | tf_op jit(solution)/shard_map/ppermute | solution.py:367
  30.8 5.2 %collective-permute-start.7 = (bf16[512,128]{1,0:T(8,128)(2,1)S(1)}, bf16[512,128]{1,0:T(8,128)(2,1)S(1)}, u32[]{:S(2)}, u32[]{:S(2)}) collective-permute-start(bf16[512,128]{1,0:T(8,128)(2,1)S(1)} %add_convert_fusion.4), channel_id=1, source_target_pairs={{0,2},{1,3},{2,0},{3,1},{4,6},{5,7},{6,4},{7,5},{8,14},{9,15},{10,... | collective-permute-start | bytes 393224 | tf_op jit(solution)/shard_map/ppermute | solution.py:367
  36.0 4.3 %collective-permute-start.8 = (bf16[512,128]{1,0:T(8,128)(2,1)S(1)}, bf16[512,128]{1,0:T(8,128)(2,1)S(1)}, u32[]{:S(2)}, u32[]{:S(2)}) collective-permute-start(bf16[512,128]{1,0:T(8,128)(2,1)S(1)} %add_convert_fusion.3), channel_id=1, source_target_pairs={{0,6},{1,7},{2,4},{3,5},{4,2},{5,3},{6,0},{7,1},{8,24},{9,25},{10,... | collective-permute-start | bytes 393224 | tf_op jit(solution)/shard_map/ppermute | solution.py:367
  40.3 5.1 %collective-permute-start.9 = (bf16[512,128]{1,0:T(8,128)(2,1)S(1)}, bf16[512,128]{1,0:T(8,128)(2,1)S(1)}, u32[]{:S(2)}, u32[]{:S(2)}) collective-permute-start(bf16[512,128]{1,0:T(8,128)(2,1)S(1)} %add_convert_fusion.2), channel_id=1, source_target_pairs={{0,16},{1,17},{2,18},{3,19},{4,20},{5,21},{6,22},{7,23},{8,56},{9,... | collective-permute-start | bytes 393224 | tf_op jit(solution)/shard_map/ppermute | solution.py:367
  45.5 3.9 %collective-permute-start.10 = (bf16[512,128]{1,0:T(8,128)(2,1)S(1)}, bf16[512,128]{1,0:T(8,128)(2,1)S(1)}, u32[]{:S(2)}, u32[]{:S(2)}) collective-permute-start(bf16[512,128]{1,0:T(8,128)(2,1)S(1)} %add_convert_fusion.1), channel_id=1, source_target_pairs={{0,48},{1,49},{2,50},{3,51},{4,52},{5,53},{6,54},{7,55},{8,9},{9,8... | collective-permute-start | bytes 393224 | tf_op jit(solution)/shard_map/ppermute | solution.py:367
  49.4 8.3 %collective-permute-start.12 = (bf16[512,128]{1,0:T(8,128)(2,1)S(1)}, bf16[512,128]{1,0:T(8,128)(2,1)S(1)}, u32[]{:S(2)}, u32[]{:S(2)}) collective-permute-start(bf16[512,128]{1,0:T(8,128)(2,1)S(1)} %add_convert_fusion.lat0), channel_id=1, source_target_pairs={{0,65},{1,64},{2,67},{3,66},{4,69},{5,68},{6,71},{7,70},{8,73},{9,... | collective-permute-start | bytes 393224 | tf_op jit(solution)/shard_map/ppermute | solution.py:367
  52.0 9.2 %collective-permute-start.11 = (bf16[512,128]{1,0:T(8,128)(2,1)S(1)}, bf16[512,128]{1,0:T(8,128)(2,1)S(1)}, u32[]{:S(2)}, u32[]{:S(2)}) collective-permute-start(bf16[512,128]{1,0:T(8,128)(2,1)S(1)} %add_convert_fusion.lat0), channel_id=1, source_target_pairs={{0,8},{1,9},{2,10},{3,11},{4,12},{5,13},{6,14},{7,15},{8,0},{9,1},... | collective-permute-start | bytes 393224 | tf_op jit(solution)/shard_map/ppermute | solution.py:367
  57.8 4.4 %collective-permute-start.13 = (bf16[512,128]{1,0:T(8,128)(2,1)S(1)}, bf16[512,128]{1,0:T(8,128)(2,1)S(1)}, u32[]{:S(2)}, u32[]{:S(2)}) collective-permute-start(bf16[512,128]{1,0:T(8,128)(2,1)S(1)} %collective-permute-done.12.lat2), channel_id=1, source_target_pairs={{0,8},{1,9},{2,10},{3,11},{4,12},{5,13},{6,14},{7,15},{8,0},{9,1},... | collective-permute-start | bytes 393224 | tf_op jit(solution)/shard_map/ppermute | solution.py:367

commit v4 on v3

--- a/solution.py
+++ b/solution.py
@@ -46,29 +46,23 @@
     return pl.BlockSpec(shape, lambda *_: (0,) * len(shape))
 
 
-def pack_kernel(pos, q_ref, k_ref, v_ref, *outs):
+def pack_kernel(q_ref, k_ref, v_ref, *outs):
+    z = (lax.axis_index("seq") >> 1) & 3
     for shift, out in enumerate(outs):
-        head = lax.rem(pos[1] + shift, 4)
+        head = (z + shift) & 3
         columns = pl.ds(pl.multiple_of(head * HD, HD), HD)
         out[:, 0:HD] = q_ref[:, columns]
         out[:, HD : 2 * HD] = k_ref[:, columns]
         out[:, 2 * HD : 3 * HD] = v_ref[:, columns]
 
 
-def pack(pos, q, k, v):
-    piece = pltpu.VMEM((TOK, 3 * HD), BF)
+def pack(q, k, v):
     return pl.pallas_call(
         pack_kernel,
-        grid_spec=pltpu.PrefetchScalarGridSpec(
-            num_scalar_prefetch=1,
-            grid=(1,),
-            in_specs=[whole(q.shape)] * 3,
-            out_specs=[whole(piece.shape)] * 4,
-        ),
-        out_shape=[piece] * 4,
+        out_shape=[pltpu.VMEM((TOK, 3 * HD), BF)] * 4,
         compiler_params=pltpu.CompilerParams(vmem_limit_bytes=SMALL),
         name="pack",
-    )(pos, *(pltpu.with_memory_space_constraint(array, pltpu.HBM) for array in (q, k, v)))
+    )(*(pltpu.with_memory_space_constraint(array, pltpu.HBM) for array in (q, k, v)))
 
 
 def prep_kernel(pos, ow, lw, hid, wqh, wkh, gq, gk, wq, wk, w2_out, hl_out, m_out, gq_out, gk_out):
@@ -193,7 +187,7 @@
     lat1,
     lat2,
     lat3,
-    conv_hbm,
+    conv,
     b1,
     second,
     b2,
@@ -211,18 +205,19 @@
     nat_s,
     acc_s,
     bound_s,
-    conv,
-    conv_sem,
 ):
     x, z, c, g = pos[0], pos[1], pos[2], pos[3]
-    fetch = pltpu.make_async_copy(conv_hbm, conv, conv_sem)
-    fetch.start()
     for dx, dc, piece in ((0, 0, lat0), (0, 1, lat1), (1, 0, lat2), (1, 1, lat3)):
         px = lax.bitwise_xor(x, dx)
         pc = lax.bitwise_xor(c, dc)
         for pz in range(4):
             lat_s[px * 8 + pz * 2 + pc] = piece[pz * TOK : (pz + 1) * TOK, :]
-    grid_s[...] = jnp.zeros_like(grid_s)
+    edge = jnp.zeros((3, 1, H_LO + 2, W_LO, HD), BF)
+    grid_s[:, 0:1] = edge
+    grid_s[:, FRAMES + 1 : FRAMES + 2] = edge
+    edge = jnp.zeros((3, FRAMES + 2, 1, W_LO, HD), BF)
+    grid_s[:, :, 0:1] = edge
+    grid_s[:, :, H_LO + 1 : H_LO + 2] = edge
     lat = lat_s[...].reshape(FRAMES * TOK, HD).astype(F32)
     column = lax.rem(lax.broadcasted_iota(jnp.int32, (FRAMES * TOK, HD), 0), W_LO)
     left = jnp.where(column == 0, 0.0, pltpu.roll(lat, 1, 0))
@@ -231,7 +226,6 @@
         grid_s[index, 1 : FRAMES + 1, 1 : H_LO + 1] = shifted.astype(BF).reshape(FRAMES, H_LO, W_LO, HD)
 
     val_s[:, HD : 2 * HD] = jnp.ones((KEYS, HD), BF)
-    fetch.wait()
     biggest = jnp.zeros((1, 1), F32)
     rows = CHUNK * TOK
     for first in range(0, FRAMES, CHUNK):
@@ -288,7 +282,7 @@
             acc_s[head] += dot(weights, val_s[keys, :])
         return carry
 
-    lax.fori_loop(0, KEYS // BLOCK, step, 0)
+    lax.fori_loop(0, KEYS // BLOCK, step, 0, unroll=2)
 
     @pl.when(jnp.logical_not(jnp.min(acc_s[:, :, HD:]) > TINY))
     def _():
@@ -322,7 +316,6 @@
     args = (*lats, conv, bias_first.reshape(1, -1), conv_second, bias_second.reshape(1, -1), gq, gk, m, value_weight)
     in_specs = [whole(a.shape) for a in args]
     in_specs[-1] = pl.BlockSpec((HD, 4 * HD), lambda i, pos: (0, pos[3]))
-    in_specs[len(lats)] = pl.BlockSpec(memory_space=pltpu.HBM)
     return pl.pallas_call(
         hi_kernel,
         grid_spec=pltpu.PrefetchScalarGridSpec(
@@ -339,8 +332,6 @@
                 pltpu.VMEM((4 * TOK, HD), F32),
                 pltpu.VMEM((4, 4 * TOK, 2 * HD), F32),
                 pltpu.VMEM((4, 4 * TOK, HD), F32),
-                pltpu.VMEM(conv.shape, BF),
-                pltpu.SemaphoreType.DMA,
             ],
         ),
         out_shape=[
@@ -379,19 +370,20 @@
     return x ^ 3, y, z, core
 
 
-HOPS = (("x", 1), ("y", 1), ("y", 3), ("z", 1), ("z", 3))
-
-
-def sum_step(step):
+ROUNDS = ((("x", "x"), (1,)), (("y", "z"), (1, 3, 2)), (("z", "y"), (1, 3, 2)))
+
+
+def along(axes, bit):
     def partner(x, y, z, core):
-        axis, bit = HOPS[(step + core) % 5]
-        if axis == "x":
-            return x ^ bit, y, z, core
-        if axis == "y":
-            return x, y ^ bit, z, core
-        return x, y, z ^ bit, core
+        flip = {"x": 0, "y": 0, "z": 0, axes[core]: bit}
+        return x ^ flip["x"], y ^ flip["y"], z ^ flip["z"], core
 
     return partner
+
+
+def sum_round(value, axes, bits):
+    arrived = [trade(value, along(axes, bit)).astype(F32) for bit in bits]
+    return sum(arrived, value.astype(F32)).astype(BF)
 
 
 def local(
@@ -413,7 +405,7 @@
 ):
     seq, head = lax.axis_index("seq"), lax.axis_index("head")
     pos = jnp.stack([seq // 8, (seq // 2) % 4, seq % 2, head]).astype(jnp.int32)
-    pieces = pack(pos, query_low, key_low, value_low)
+    pieces = pack(query_low, key_low, value_low)
     pieces = [pieces[0]] + [
         lax.ppermute(pieces[step], "seq", z_shift(step)) for step in (1, 2, 3)
     ]
@@ -426,8 +418,8 @@
     kv_x, w2, hl, m, gq, gk = lax.optimization_barrier((kv_x, w2, hl, m, gq, gk))
     kv_xc = trade(kv_x, to_core)
     latent = low_attention(pos, pieces, (kv, kv_c, kv_x, kv_xc), w2, hl)
-    for step in range(5):
-        latent = (latent.astype(F32) + trade(latent, sum_step(step)).astype(F32)).astype(BF)
+    for axes, bits in ROUNDS:
+        latent = sum_round(latent, axes, bits)
     lat_x = trade(latent, to_x_near)
     lat_c = trade(latent, to_core)
     lat_xc = trade(lat_x, to_core)

time: 174 us -> 169 us (0.971)
  Pallas kernels: 120 us -> 118 us
    ppermute x11 -> x13, waiting for transfers between devices: 15.7 us -> 14 us  [trade(): return lax.ppermute(value, ('seq', 'head'), pairs)]
    ppermute x11 -> x13, starting transfers between devices: 26.9 us -> 25.4 us  [trade(): return lax.ppermute(value, ('seq', 'head'), pairs)]
  transfers between devices with their start and end apart: 14 -> 16, of which waited for: 10 -> 11; matrix products, arithmetic and copies ran while one was open for 0% -> 0% of each run, Pallas kernels for 2% -> 3%
where the time goes in v4:
time: 169 us; the launch traced here: 168 us
  Pallas kernels  118 us (70%)
  starting transfers between devices  32 us (19%)
  waiting for transfers between devices  17.3 us (10%)
    pallas_call x1, Pallas kernels, hi_attention(): pl.pallas_call(hi_kernel, grid_spec=pltpu.PrefetchScalarGridSpec(num_scal...  110 us
    ppermute x13, starting transfers between devices, trade(): return lax.ppermute(value, ('seq', 'head'), pairs)  25.4 us
    ppermute x13, waiting for transfers between devices, trade(): return lax.ppermute(value, ('seq', 'head'), pairs)  14 us
    ppermute x3, starting transfers between devices, local(): lax.ppermute(pieces[step], 'seq', z_shift(step))  6.57 us
    pallas_call x1, Pallas kernels, prep(): pl.pallas_call(prep_kernel, grid_spec=pltpu.PrefetchScalarGridSpec(num_sc...  4.47 us
  transfers between devices with their start and end apart: 16, of which 11 were waited for; matrix products, arithmetic and copies ran while one was open for 0% of the time, Pallas kernels for 3%

profile of v4, /device:TPU:1, one launch (start us, length us, event | category | flops | bytes accessed | tf_op | source)
XLA Modules:
  0.0 168.4 jit_solution(16200761697548201327)
XLA Ops:
  0.6 1.1 pack.1
  1.7 2.5 %collective-permute-start = (bf16[128,384]{1,0:T(8,128)(2,1)S(1)}, bf16[128,384]{1,0:T(8,128)(2,1)S(1)}, u32[]{:S(2)}, u32[]{:S(2)}) collective-permute-start(bf16[128,384]{1,0:T(8,128)(2,1)S(1)} %get-tuple-element.18), channel_id=1, source_target_pairs={{0,16},{8,24},{16,32},{24,40},{32,48},{40,56},{48,0},{56,8},{64,80... | collective-permute-start | bytes 294920 | tf_op jit(solution)/shard_map/ppermute | solution.py:410
  4.3 3.3 %collective-permute-start.1 = (bf16[128,384]{1,0:T(8,128)(2,1)S(1)}, bf16[128,384]{1,0:T(8,128)(2,1)S(1)}, u32[]{:S(2)}, u32[]{:S(2)}) collective-permute-start(bf16[128,384]{1,0:T(8,128)(2,1)S(1)} %get-tuple-element.19), channel_id=1, source_target_pairs={{0,32},{8,40},{16,48},{24,56},{32,0},{40,8},{48,16},{56,24},{64,96... | collective-permute-start | bytes 294920 | tf_op jit(solution)/shard_map/ppermute | solution.py:410
  7.6 0.7 collective-permute-start.2
  8.3 0.6 collective-permute-done.p1
  8.9 2.7 %collective-permute-done.1.p2 = bf16[128,384]{1,0:T(8,128)(2,1)S(1)} collective-permute-done((bf16[128,384]{1,0:T(8,128)(2,1)S(1)}, bf16[128,384]{1,0:T(8,128)(2,1)S(1)}, u32[]{:S(2)}, u32[]{:S(2)}) %collective-permute-start.1) | collective-permute-done | bytes 98336 | tf_op jit(solution)/shard_map/ppermute | solution.py:410
  11.6 0.0 collective-permute-done.2.p3
  11.6 2.8 %collective-permute-start.4 = (bf16[512,256]{1,0:T(8,128)(2,1)S(1)}, bf16[512,256]{1,0:T(8,128)(2,1)S(1)}, u32[]{:S(2)}, u32[]{:S(2)}) collective-permute-start(bf16[512,256]{1,0:T(8,128)(2,1)S(1)} %pad_maximum_fusion.kv0), channel_id=1, source_target_pairs={{0,64},{1,65},{2,66},{3,67},{4,68},{5,69},{6,70},{7,71},{8,72},{9,... | collective-permute-start | bytes 786440 | tf_op jit(solution)/shard_map/ppermute | solution.py:358
  14.5 0.1 pad_add_fusion.pos
  14.5 0.0 copy-start
  14.5 0.0 copy-start.1
  14.5 0.0 copy-start.2
  14.5 0.0 copy-start.3
  14.6 0.0 copy-start.4
  14.6 4.5 %prep.1 = (bf16[128,256]{1,0:T(8,128)(2,1)S(1)}, f32[16,128]{1,0:T(8,128)S(1)}, bf16[4,128,256]{2,1,0:T(8,128)(2,1)S(1)}, bf16[128,256]{1,0:T(8,128)(2,1)S(1)}, bf16[128,256]{1,0:T(8,128)(2,1)S(1)}) custom-call(s32[4]{0:T(128)S(1)} %pad_add_fusion.pos, bf16[512,4096]{1,0:T(8,128)(2,1)} %ow.1, bf16[4096,128]{1,0:T(8,128)(2,1)} %lw.1, bf16[128,4096]{1,0:T(8,128)(2,1)} %hid.1, ...), custom_call_target="tpu_custom_call" | custom-call | flops 900000000 | bytes 5000000 | tf_op jit(solution)/shard_map/prep/pallas_call | solution.py:86
  19.0 2.2 %collective-permute-start.3 = (bf16[512,256]{1,0:T(8,128)(2,1)S(1)}, bf16[512,256]{1,0:T(8,128)(2,1)S(1)}, u32[]{:S(2)}, u32[]{:S(2)}) collective-permute-start(bf16[512,256]{1,0:T(8,128)(2,1)S(1)} %pad_maximum_fusion.kv0), channel_id=1, source_target_pairs={{0,8},{1,9},{2,10},{3,11},{4,12},{5,13},{6,14},{7,15},{8,0},{9,1},... | collective-permute-start | bytes 786440 | tf_op jit(solution)/shard_map/ppermute | solution.py:358
  21.2 0.0 collective-permute-done.4.kv2
  21.2 0.7 collective-permute-start.5
  21.9 0.5 collective-permute-done.3.kv1
  22.4 0.7 collective-permute-done.5.kv3
  23.1 2.8 %low.1 = bf16[512,128]{1,0:T(8,128)(2,1)S(1)} custom-call(s32[4]{0:T(128)S(1)} %pad_add_fusion.pos, bf16[128,384]{1,0:T(8,128)(2,1)S(1)} %get-tuple-element.17.p0, bf16[128,384]{1,0:T(8,128)(2,1)S(1)} %collective-permute-done.p1, bf16[128,384]{1,0:T(8,128)(2,1)S(1)} %collective-permute-done.1.p2, bf16[128,384]{1,0:T(8,128)(2,1)S(1)} %collective-permute-done.2.p3, ...), custom_call_target="tpu_custom_call" | custom-call | tf_op jit(solution)/shard_map/low/pallas_call | solution.py:164
  25.9 1.3 collective-permute-start.6
  27.2 3.5 %collective-permute-done.6 = bf16[512,128]{1,0:T(8,128)(2,1)S(1)} collective-permute-done((bf16[512,128]{1,0:T(8,128)(2,1)S(1)}, bf16[512,128]{1,0:T(8,128)(2,1)S(1)}, u32[]{:S(2)}, u32[]{:S(2)}) %collective-permute-start.6) | collective-permute-done | bytes 131104 | tf_op jit(solution)/shard_map/ppermute | solution.py:358
  30.7 2.1 %collective-permute-start.9 = (bf16[512,128]{1,0:T(8,128)(2,1)S(1)}, bf16[512,128]{1,0:T(8,128)(2,1)S(1)}, u32[]{:S(2)}, u32[]{:S(2)}) collective-permute-start(bf16[512,128]{1,0:T(8,128)(2,1)S(1)} %add_convert_fusion.2), channel_id=1, source_target_pairs={{0,4},{1,5},{2,6},{3,7},{4,0},{5,1},{6,2},{7,3},{8,40},{9,41},{10,... | collective-permute-start | bytes 393224 | tf_op jit(solution)/shard_map/ppermute | solution.py:358
  32.8 2.3 %collective-permute-start.8 = (bf16[512,128]{1,0:T(8,128)(2,1)S(1)}, bf16[512,128]{1,0:T(8,128)(2,1)S(1)}, u32[]{:S(2)}, u32[]{:S(2)}) collective-permute-start(bf16[512,128]{1,0:T(8,128)(2,1)S(1)} %add_convert_fusion.2), channel_id=1, source_target_pairs={{0,6},{1,7},{2,4},{3,5},{4,2},{5,3},{6,0},{7,1},{8,56},{9,57},{10,... | collective-permute-start | bytes 393224 | tf_op jit(solution)/shard_map/ppermute | solution.py:358
  35.1 0.0 collective-permute-start.7
  35.1 1.0 collective-permute-done.9
  36.1 2.0 %collective-permute-done.8 = bf16[512,128]{1,0:T(8,128)(2,1)S(1)} collective-permute-done((bf16[512,128]{1,0:T(8,128)(2,1)S(1)}, bf16[512,128]{1,0:T(8,128)(2,1)S(1)}, u32[]{:S(2)}, u32[]{:S(2)}) %collective-permute-start.8) | collective-permute-done | bytes 131104 | tf_op jit(solution)/shard_map/ppermute | solution.py:358
  38.1 0.8 collective-permute-done.7
  38.9 0.1 add_convert_fusion.1
  39.0 3.3 %collective-permute-start.12 = (bf16[512,128]{1,0:T(8,128)(2,1)S(1)}, bf16[512,128]{1,0:T(8,128)(2,1)S(1)}, u32[]{:S(2)}, u32[]{:S(2)}) collective-permute-start(bf16[512,128]{1,0:T(8,128)(2,1)S(1)} %add_convert_fusion.1), channel_id=1, source_target_pairs={{0,32},{1,33},{2,34},{3,35},{4,36},{5,37},{6,38},{7,39},{8,12},{9,... | collective-permute-start | bytes 393224 | tf_op jit(solution)/shard_map/ppermute | solution.py:358
  42.2 0.8 collective-permute-start.11
  43.0 0.0 collective-permute-start.10
  43.0 1.6 collective-permute-done.12
  44.6 3.0 %collective-permute-done.11 = bf16[512,128]{1,0:T(8,128)(2,1)S(1)} collective-permute-done((bf16[512,128]{1,0:T(8,128)(2,1)S(1)}, bf16[512,128]{1,0:T(8,128)(2,1)S(1)}, u32[]{:S(2)}, u32[]{:S(2)}) %collective-permute-start.11) | collective-permute-done | bytes 131104 | tf_op jit(solution)/shard_map/ppermute | solution.py:358
  47.6 0.0 collective-permute-done.10
  47.6 0.1 add_convert_fusion.lat0
  47.6 2.6 %collective-permute-start.14 = (bf16[512,128]{1,0:T(8,128)(2,1)S(1)}, bf16[512,128]{1,0:T(8,128)(2,1)S(1)}, u32[]{:S(2)}, u32[]{:S(2)}) collective-permute-start(bf16[512,128]{1,0:T(8,128)(2,1)S(1)} %add_convert_fusion.lat0), channel_id=1, source_target_pairs={{0,65},{1,64},{2,67},{3,66},{4,69},{5,68},{6,71},{7,70},{8,73},{9,... | collective-permute-start | bytes 393224 | tf_op jit(solution)/shard_map/ppermute | solution.py:358
  50.2 4.0 %collective-permute-start.13 = (bf16[512,128]{1,0:T(8,128)(2,1)S(1)}, bf16[512,128]{1,0:T(8,128)(2,1)S(1)}, u32[]{:S(2)}, u32[]{:S(2)}) collective-permute-start(bf16[512,128]{1,0:T(8,128)(2,1)S(1)} %add_convert_fusion.lat0), channel_id=1, source_target_pairs={{0,8},{1,9},{2,10},{3,11},{4,12},{5,13},{6,14},{7,15},{8,0},{9,1},... | collective-permute-start | bytes 393224 | tf_op jit(solution)/shard_map/ppermute | solution.py:358
  54.2 0.0 collective-permute-done.14.lat2
  54.2 3.4 %collective-permute-start.15 = (bf16[512,128]{1,0:T(8,128)(2,1)S(1)}, bf16[512,128]{1,0:T(8,128)(2,1)S(1)}, u32[]{:S(2)}, u32[]{:S(2)}) collective-permute-start(bf16[512,128]{1,0:T(8,128)(2,1)S(1)} %collective-permute-done.14.lat2), channel_id=1, source_target_pairs={{0,8},{1,9},{2,10},{3,11},{4,12},{5,13},{6,14},{7,15},{8,0},{9,1},... | collective-permute-start | bytes 393224 | tf_op jit(solution)/shard_map/ppermute | solution.py:358
  57.7 0.0 collective-permute-done.13.lat1
  57.7 1.0 collective-permute-done.15.lat3
  58.6 0.0 copy-done
  58.6 0.0 copy-done.1
  58.6 0.0 copy-done.2
  58.6 0.0 copy-done.3
  58.7 0.0 copy-done.4
  58.7 109.7 %hi.1 = (bf16[512,512]{1,0:T(8,128)(2,1)}, bf16[64,128]{1,0:T(8,128)(2,1)}) custom-call(s32[4]{0:T(128)S(1)} %pad_add_fusion.pos, bf16[512,128]{1,0:T(8,128)(2,1)S(1)} %add_convert_fusion.lat0, bf16[512,128]{1,0:T(8,128)(2,1)S(1)} %collective-permute-done.13.lat1, bf16[512,128]{1,0:T(8,128)(2,1)S(1)} %collective-permute-done.14.lat2, ...), custom_call_target="tpu_custom_call" | custom-call | tf_op jit(solution)/shard_map/hi/pallas_call | solution.py:319
  (6 shorter events, 0.1 us)
Async XLA Ops:
  1.7 7.2 %collective-permute-start = (bf16[128,384]{1,0:T(8,128)(2,1)S(1)}, bf16[128,384]{1,0:T(8,128)(2,1)S(1)}, u32[]{:S(2)}, u32[]{:S(2)}) collective-permute-start(bf16[128,384]{1,0:T(8,128)(2,1)S(1)} %get-tuple-element.18), channel_id=1, source_target_pairs={{0,16},{8,24},{16,32},{24,40},{32,48},{40,56},{48,0},{56,8},{64,80... | collective-permute-start | bytes 294920 | tf_op jit(solution)/shard_map/ppermute | solution.py:410
  4.3 7.3 %collective-permute-start.1 = (bf16[128,384]{1,0:T(8,128)(2,1)S(1)}, bf16[128,384]{1,0:T(8,128)(2,1)S(1)}, u32[]{:S(2)}, u32[]{:S(2)}) collective-permute-start(bf16[128,384]{1,0:T(8,128)(2,1)S(1)} %get-tuple-element.19), channel_id=1, source_target_pairs={{0,32},{8,40},{16,48},{24,56},{32,0},{40,8},{48,16},{56,24},{64,96... | collective-permute-start | bytes 294920 | tf_op jit(solution)/shard_map/ppermute | solution.py:410
  7.6 4.0 %collective-permute-start.2 = (bf16[128,384]{1,0:T(8,128)(2,1)S(1)}, bf16[128,384]{1,0:T(8,128)(2,1)S(1)}, u32[]{:S(2)}, u32[]{:S(2)}) collective-permute-start(bf16[128,384]{1,0:T(8,128)(2,1)S(1)} %get-tuple-element.20), channel_id=1, source_target_pairs={{0,48},{8,56},{16,0},{24,8},{32,16},{40,24},{48,32},{56,40},{64,11... | collective-permute-start | bytes 294920 | tf_op jit(solution)/shard_map/ppermute | solution.py:410
  11.6 9.6 %collective-permute-start.4 = (bf16[512,256]{1,0:T(8,128)(2,1)S(1)}, bf16[512,256]{1,0:T(8,128)(2,1)S(1)}, u32[]{:S(2)}, u32[]{:S(2)}) collective-permute-start(bf16[512,256]{1,0:T(8,128)(2,1)S(1)} %pad_maximum_fusion.kv0), channel_id=1, source_target_pairs={{0,64},{1,65},{2,66},{3,67},{4,68},{5,69},{6,70},{7,71},{8,72},{9,... | collective-permute-start | bytes 786440 | tf_op jit(solution)/shard_map/ppermute | solution.py:358
  14.5 44.1 %copy-start = (bf16[3,3,3,128,512]{4,3,2,1,0:T(8,128)(2,1)S(1)}, bf16[3,3,3,128,512]{4,3,2,1,0:T(8,128)(2,1)}, u32[]{:S(2)}) copy-start(bf16[3,3,3,128,512]{4,3,2,1,0:T(8,128)(2,1)} %param.21) | copy-start | bytes 10616836
  14.5 44.1 %copy-start.1 = (bf16[128,4096]{1,0:T(8,128)(2,1)S(1)}, bf16[128,4096]{1,0:T(8,128)(2,1)}, u32[]{:S(2)}) copy-start(bf16[128,4096]{1,0:T(8,128)(2,1)} %wv.1) | copy-start | bytes 3145732
  14.5 44.1 %copy-start.2 = (bf16[512,512]{1,0:T(8,128)(2,1)S(1)}, bf16[512,512]{1,0:T(8,128)(2,1)}, u32[]{:S(2)}) copy-start(bf16[512,512]{1,0:T(8,128)(2,1)} %second.1) | copy-start | bytes 1572868
  14.5 44.1 %copy-start.3 = (f32[512]{0:T(512)S(1)}, f32[512]{0:T(512)}, u32[]{:S(2)}) copy-start(f32[512]{0:T(512)} %param.22) | copy-start | bytes 6148
  14.6 44.1 %copy-start.4 = (f32[512]{0:T(512)S(1)}, f32[512]{0:T(512)}, u32[]{:S(2)}) copy-start(f32[512]{0:T(512)} %param.24) | copy-start | bytes 6148
  19.0 3.4 %collective-permute-start.3 = (bf16[512,256]{1,0:T(8,128)(2,1)S(1)}, bf16[512,256]{1,0:T(8,128)(2,1)S(1)}, u32[]{:S(2)}, u32[]{:S(2)}) collective-permute-start(bf16[512,256]{1,0:T(8,128)(2,1)S(1)} %pad_maximum_fusion.kv0), channel_id=1, source_target_pairs={{0,8},{1,9},{2,10},{3,11},{4,12},{5,13},{6,14},{7,15},{8,0},{9,1},... | collective-permute-start | bytes 786440 | tf_op jit(solution)/shard_map/ppermute | solution.py:358
  21.2 1.9 %collective-permute-start.5 = (bf16[512,256]{1,0:T(8,128)(2,1)S(1)}, bf16[512,256]{1,0:T(8,128)(2,1)S(1)}, u32[]{:S(2)}, u32[]{:S(2)}) collective-permute-start(bf16[512,256]{1,0:T(8,128)(2,1)S(1)} %collective-permute-done.4.kv2), channel_id=1, source_target_pairs={{0,8},{1,9},{2,10},{3,11},{4,12},{5,13},{6,14},{7,15},{8,0},{9,1},... | collective-permute-start | bytes 786440 | tf_op jit(solution)/shard_map/ppermute | solution.py:358
  25.9 4.8 %collective-permute-start.6 = (bf16[512,128]{1,0:T(8,128)(2,1)S(1)}, bf16[512,128]{1,0:T(8,128)(2,1)S(1)}, u32[]{:S(2)}, u32[]{:S(2)}) collective-permute-start(bf16[512,128]{1,0:T(8,128)(2,1)S(1)} %low.1), channel_id=1, source_target_pairs={{0,1},{1,0},{2,3},{3,2},{4,5},{5,4},{6,7},{7,6},{8,9},{9,8},{10,11... | collective-permute-start | bytes 393224 | tf_op jit(solution)/shard_map/ppermute | solution.py:358
  30.7 5.4 %collective-permute-start.9 = (bf16[512,128]{1,0:T(8,128)(2,1)S(1)}, bf16[512,128]{1,0:T(8,128)(2,1)S(1)}, u32[]{:S(2)}, u32[]{:S(2)}) collective-permute-start(bf16[512,128]{1,0:T(8,128)(2,1)S(1)} %add_convert_fusion.2), channel_id=1, source_target_pairs={{0,4},{1,5},{2,6},{3,7},{4,0},{5,1},{6,2},{7,3},{8,40},{9,41},{10,... | collective-permute-start | bytes 393224 | tf_op jit(solution)/shard_map/ppermute | solution.py:358
  32.8 5.3 %collective-permute-start.8 = (bf16[512,128]{1,0:T(8,128)(2,1)S(1)}, bf16[512,128]{1,0:T(8,128)(2,1)S(1)}, u32[]{:S(2)}, u32[]{:S(2)}) collective-permute-start(bf16[512,128]{1,0:T(8,128)(2,1)S(1)} %add_convert_fusion.2), channel_id=1, source_target_pairs={{0,6},{1,7},{2,4},{3,5},{4,2},{5,3},{6,0},{7,1},{8,56},{9,57},{10,... | collective-permute-start | bytes 393224 | tf_op jit(solution)/shard_map/ppermute | solution.py:358
  35.1 3.8 %collective-permute-start.7 = (bf16[512,128]{1,0:T(8,128)(2,1)S(1)}, bf16[512,128]{1,0:T(8,128)(2,1)S(1)}, u32[]{:S(2)}, u32[]{:S(2)}) collective-permute-start(bf16[512,128]{1,0:T(8,128)(2,1)S(1)} %add_convert_fusion.2), channel_id=1, source_target_pairs={{0,2},{1,3},{2,0},{3,1},{4,6},{5,7},{6,4},{7,5},{8,24},{9,25},{10,... | collective-permute-start | bytes 393224 | tf_op jit(solution)/shard_map/ppermute | solution.py:358
  39.0 5.6 %collective-permute-start.12 = (bf16[512,128]{1,0:T(8,128)(2,1)S(1)}, bf16[512,128]{1,0:T(8,128)(2,1)S(1)}, u32[]{:S(2)}, u32[]{:S(2)}) collective-permute-start(bf16[512,128]{1,0:T(8,128)(2,1)S(1)} %add_convert_fusion.1), channel_id=1, source_target_pairs={{0,32},{1,33},{2,34},{3,35},{4,36},{5,37},{6,38},{7,39},{8,12},{9,... | collective-permute-start | bytes 393224 | tf_op jit(solution)/shard_map/ppermute | solution.py:358
  42.2 5.3 %collective-permute-start.11 = (bf16[512,128]{1,0:T(8,128)(2,1)S(1)}, bf16[512,128]{1,0:T(8,128)(2,1)S(1)}, u32[]{:S(2)}, u32[]{:S(2)}) collective-permute-start(bf16[512,128]{1,0:T(8,128)(2,1)S(1)} %add_convert_fusion.1), channel_id=1, source_target_pairs={{0,48},{1,49},{2,50},{3,51},{4,52},{5,53},{6,54},{7,55},{8,14},{9,... | collective-permute-start | bytes 393224 | tf_op jit(solution)/shard_map/ppermute | solution.py:358
  43.0 4.5 %collective-permute-start.10 = (bf16[512,128]{1,0:T(8,128)(2,1)S(1)}, bf16[512,128]{1,0:T(8,128)(2,1)S(1)}, u32[]{:S(2)}, u32[]{:S(2)}) collective-permute-start(bf16[512,128]{1,0:T(8,128)(2,1)S(1)} %add_convert_fusion.1), channel_id=1, source_target_pairs={{0,16},{1,17},{2,18},{3,19},{4,20},{5,21},{6,22},{7,23},{8,10},{9,... | collective-permute-start | bytes 393224 | tf_op jit(solution)/shard_map/ppermute | solution.py:358
  47.6 6.6 %collective-permute-start.14 = (bf16[512,128]{1,0:T(8,128)(2,1)S(1)}, bf16[512,128]{1,0:T(8,128)(2,1)S(1)}, u32[]{:S(2)}, u32[]{:S(2)}) collective-permute-start(bf16[512,128]{1,0:T(8,128)(2,1)S(1)} %add_convert_fusion.lat0), channel_id=1, source_target_pairs={{0,65},{1,64},{2,67},{3,66},{4,69},{5,68},{6,71},{7,70},{8,73},{9,... | collective-permute-start | bytes 393224 | tf_op jit(solution)/shard_map/ppermute | solution.py:358
  50.2 7.5 %collective-permute-start.13 = (bf16[512,128]{1,0:T(8,128)(2,1)S(1)}, bf16[512,128]{1,0:T(8,128)(2,1)S(1)}, u32[]{:S(2)}, u32[]{:S(2)}) collective-permute-start(bf16[512,128]{1,0:T(8,128)(2,1)S(1)} %add_convert_fusion.lat0), channel_id=1, source_target_pairs={{0,8},{1,9},{2,10},{3,11},{4,12},{5,13},{6,14},{7,15},{8,0},{9,1},... | collective-permute-start | bytes 393224 | tf_op jit(solution)/shard_map/ppermute | solution.py:358
  54.2 4.4 %collective-permute-start.15 = (bf16[512,128]{1,0:T(8,128)(2,1)S(1)}, bf16[512,128]{1,0:T(8,128)(2,1)S(1)}, u32[]{:S(2)}, u32[]{:S(2)}) collective-permute-start(bf16[512,128]{1,0:T(8,128)(2,1)S(1)} %collective-permute-done.14.lat2), channel_id=1, source_target_pairs={{0,8},{1,9},{2,10},{3,11},{4,12},{5,13},{6,14},{7,15},{8,0},{9,1},... | collective-permute-start | bytes 393224 | tf_op jit(solution)/shard_map/ppermute | solution.py:358

commit v5 on v4

--- a/solution.py
+++ b/solution.py
@@ -177,8 +177,86 @@
 
 
 CHUNK = 4
+ROWS = CHUNK * TOK
+HALF = FRAMES // 2
 BLOCK = 2048
 TINY = 2.0**-90
+
+
+def fill_grid(grid_s, lat_s):
+    frames = lat_s.shape[0]
+    edge = jnp.zeros((3, 1, H_LO + 2, W_LO, HD), BF)
+    grid_s[:, 0:1] = edge
+    grid_s[:, frames + 1 : frames + 2] = edge
+    edge = jnp.zeros((3, frames + 2, 1, W_LO, HD), BF)
+    grid_s[:, :, 0:1] = edge
+    grid_s[:, :, H_LO + 1 : H_LO + 2] = edge
+    lat = lat_s[...].reshape(frames * TOK, HD).astype(F32)
+    column = lax.broadcasted_iota(jnp.int32, (frames * TOK, HD), 0) & (W_LO - 1)
+    left = jnp.where(column == 0, 0.0, pltpu.roll(lat, 1, 0))
+    right = jnp.where(column == W_LO - 1, 0.0, pltpu.roll(lat, frames * TOK - 1, 0))
+    for index, shifted in enumerate((left, lat, right)):
+        grid_s[index, 1 : frames + 1, 1 : H_LO + 1] = shifted.astype(BF).reshape(frames, H_LO, W_LO, HD)
+
+
+def upsample_chunk(first, grid_s, lat_s, conv, b1, second, b2, gk):
+    taps = []
+    for a in range(3):
+        for b in range(3):
+            for t in range(3):
+                taps.append(grid_s[t, pl.ds(first + a, CHUNK), b : b + H_LO].reshape(ROWS, HD))
+    middle = dot(jnp.concatenate(taps, axis=1), conv[...]) + b1[...]
+    middle = (middle * (0.5 * jnp.tanh(0.5 * middle) + 0.5)).astype(BF)
+    sub = dot(middle, second[...]) + b2[...]
+    base = lat_s[pl.ds(first, CHUNK)].reshape(ROWS, HD).astype(F32)
+    pairs = []
+    longest = jnp.zeros((1, 1), F32)
+    for s in range(4):
+        up = (sub[:, s * HD : (s + 1) * HD] + base).astype(BF)
+        upf = up.astype(F32)
+        square = jnp.sum(dot2(up, gk[...]) * upf, axis=1, keepdims=True)
+        key = (upf * lax.rsqrt(jnp.maximum(square, 0.0) * (1.0 / 4096.0) + 1e-6)).astype(BF)
+        keyf = key.astype(F32)
+        length = jnp.sum(keyf * keyf, axis=1, keepdims=True)
+        longest = jnp.maximum(longest, jnp.max(length, axis=0, keepdims=True))
+        pairs.append((up, key))
+    return pairs, longest
+
+
+def early_kernel(pos, lat0, lat1, conv, b1, second, b2, gk, up_out, key_out, long_out, grid_s, lat_s):
+    x, c = pos[0], pos[2]
+    for dc, piece in ((0, lat0), (1, lat1)):
+        pc = lax.bitwise_xor(c, dc)
+        for pz in range(4):
+            lat_s[pz * 2 + pc] = piece[pz * TOK : (pz + 1) * TOK, :]
+    fill_grid(grid_s, lat_s)
+    pairs, longest = upsample_chunk(x * (HALF - CHUNK), grid_s, lat_s, conv, b1, second, b2, gk)
+    for s, (up, key) in enumerate(pairs):
+        up_out[s] = up
+        key_out[s] = key
+    long_out[...] = jnp.broadcast_to(longest, long_out.shape)
+
+
+def early_frames(pos, lats, conv, b1, second, b2, gk):
+    args = (*lats, conv, b1, second, b2, gk)
+    piece = jax.ShapeDtypeStruct((4, ROWS, HD), BF)
+    return pl.pallas_call(
+        early_kernel,
+        grid_spec=pltpu.PrefetchScalarGridSpec(
+            num_scalar_prefetch=1,
+            grid=(1,),
+            in_specs=[whole(a.shape) for a in args],
+            out_specs=[whole(piece.shape), whole(piece.shape), whole((8, HD))],
+            scratch_shapes=[
+                pltpu.VMEM((3, HALF + 2, H_LO + 2, W_LO, HD), BF),
+                pltpu.VMEM((HALF, TOK, HD), BF),
+            ],
+        ),
+        out_shape=[piece, piece, jax.ShapeDtypeStruct((8, HD), F32)],
+        compiler_params=pltpu.CompilerParams(vmem_limit_bytes=2 * SMALL),
+        cost_estimate=pl.CostEstimate(flops=2_400_000_000, bytes_accessed=6_000_000, transcendentals=300_000),
+        name="early",
+    )(pos, *args)
 
 
 def hi_kernel(
@@ -187,6 +265,9 @@
     lat1,
     lat2,
     lat3,
+    up_in,
+    key_in,
+    long_in,
     conv,
     b1,
     second,
@@ -212,44 +293,23 @@
         pc = lax.bitwise_xor(c, dc)
         for pz in range(4):
             lat_s[px * 8 + pz * 2 + pc] = piece[pz * TOK : (pz + 1) * TOK, :]
-    edge = jnp.zeros((3, 1, H_LO + 2, W_LO, HD), BF)
-    grid_s[:, 0:1] = edge
-    grid_s[:, FRAMES + 1 : FRAMES + 2] = edge
-    edge = jnp.zeros((3, FRAMES + 2, 1, W_LO, HD), BF)
-    grid_s[:, :, 0:1] = edge
-    grid_s[:, :, H_LO + 1 : H_LO + 2] = edge
-    lat = lat_s[...].reshape(FRAMES * TOK, HD).astype(F32)
-    column = lax.rem(lax.broadcasted_iota(jnp.int32, (FRAMES * TOK, HD), 0), W_LO)
-    left = jnp.where(column == 0, 0.0, pltpu.roll(lat, 1, 0))
-    right = jnp.where(column == W_LO - 1, 0.0, pltpu.roll(lat, FRAMES * TOK - 1, 0))
-    for index, shifted in enumerate((left, lat, right)):
-        grid_s[index, 1 : FRAMES + 1, 1 : H_LO + 1] = shifted.astype(BF).reshape(FRAMES, H_LO, W_LO, HD)
-
+    fill_grid(grid_s, lat_s)
     val_s[:, HD : 2 * HD] = jnp.ones((KEYS, HD), BF)
-    biggest = jnp.zeros((1, 1), F32)
-    rows = CHUNK * TOK
-    for first in range(0, FRAMES, CHUNK):
-        taps = []
-        for a in range(3):
-            for b in range(3):
-                for t in range(3):
-                    taps.append(grid_s[t, first + a : first + a + CHUNK, b : b + H_LO].reshape(rows, HD))
-        middle = dot(jnp.concatenate(taps, axis=1), conv[...]) + b1[...]
-        middle = (middle * (0.5 * jnp.tanh(0.5 * middle) + 0.5)).astype(BF)
-        sub = dot(middle, second[...]) + b2[...]
-        base = lat_s[first : first + CHUNK].reshape(rows, HD).astype(F32)
-        for s in range(4):
-            up = (sub[:, s * HD : (s + 1) * HD] + base).astype(BF)
-            upf = up.astype(F32)
-            square = jnp.sum(dot2(up, gk[...]) * upf, axis=1, keepdims=True)
-            inverse = lax.rsqrt(jnp.maximum(square, 0.0) * (1.0 / 4096.0) + 1e-6)
-            key = (upf * inverse).astype(BF)
-            where = pl.ds(s * FRAMES * TOK + first * TOK, rows)
-            val_s[where, 0:HD] = up
-            key_s[where, :] = key
-            keyf = key.astype(F32)
-            length = jnp.sum(keyf * keyf, axis=1, keepdims=True)
-            biggest = jnp.maximum(biggest, jnp.max(length, axis=0, keepdims=True))
+
+    def keep(first, s, up, key):
+        rows = pl.ds(pl.multiple_of(s * FRAMES * TOK + first * TOK, ROWS), ROWS)
+        val_s[rows, 0:HD] = up
+        key_s[rows, :] = key
+
+    ends = FRAMES - CHUNK
+    for s in range(4):
+        keep(x * ends, s, up_in[s], key_in[s])
+    biggest = long_in[0:1, 0:1]
+    for first in (CHUNK, 2 * CHUNK, (1 - x) * ends):
+        pairs, longest = upsample_chunk(first, grid_s, lat_s, conv, b1, second, b2, gk)
+        biggest = jnp.maximum(biggest, longest)
+        for s, (up, key) in enumerate(pairs):
+            keep(first, s, up, key)
 
     frame = x * 8 + z * 2 + c
     own = jnp.concatenate(
@@ -310,10 +370,8 @@
         attn_out[:, columns] = dot(mixed, wv[:, columns]).astype(BF)
 
 
-def hi_attention(pos, lats, conv_first, bias_first, conv_second, bias_second, gq, gk, m, value_weight):
-    mid = conv_second.shape[0]
-    conv = conv_first.reshape(27 * HD, mid)
-    args = (*lats, conv, bias_first.reshape(1, -1), conv_second, bias_second.reshape(1, -1), gq, gk, m, value_weight)
+def hi_attention(pos, lats, early, conv, b1, second, b2, gq, gk, m, value_weight):
+    args = (*lats, *early, conv, b1, second, b2, gq, gk, m, value_weight)
     in_specs = [whole(a.shape) for a in args]
     in_specs[-1] = pl.BlockSpec((HD, 4 * HD), lambda i, pos: (0, pos[3]))
     return pl.pallas_call(
@@ -420,20 +478,19 @@
     latent = low_attention(pos, pieces, (kv, kv_c, kv_x, kv_xc), w2, hl)
     for axes, bits in ROUNDS:
         latent = sum_round(latent, axes, bits)
+    upsampler = (
+        conv_first.reshape(27 * HD, -1),
+        bias_first.reshape(1, -1),
+        conv_second,
+        bias_second.reshape(1, -1),
+    )
     lat_x = trade(latent, to_x_near)
     lat_c = trade(latent, to_core)
+    early = early_frames(pos, (latent, lat_c), *upsampler, gk)
+    lat_x, *early = lax.optimization_barrier((lat_x, *early))
     lat_xc = trade(lat_x, to_core)
     attn, up = hi_attention(
-        pos,
-        (latent, lat_c, lat_x, lat_xc),
-        conv_first,
-        bias_first,
-        conv_second,
-        bias_second,
-        gq,
-        gk,
-        m,
-        value_weight,
+        pos, (latent, lat_c, lat_x, lat_xc), early, *upsampler, gq, gk, m, value_weight
     )
     return attn, up
 

time: 169 us -> 169 us (level)
  Pallas kernels: 118 us -> 121 us
  starting transfers between devices: 32 us -> 29 us
    pallas_call x0 -> x1, Pallas kernels: none -> 3.96 us  [early_frames(): pl.pallas_call(early_kernel, grid_spec=pltpu.PrefetchScalarGridSpec(num_s...]
    ppermute x13, starting transfers between devices: 25.4 us -> 22.4 us  [trade(): return lax.ppermute(value, ('seq', 'head'), pairs)]
  transfers between devices with their start and end apart: 16 -> 16, of which waited for: 11 -> 11; matrix products, arithmetic and copies ran while one was open for 0% -> 0% of each run, Pallas kernels for 3% -> 5%
where the time goes in v5:
time: 169 us
  Pallas kernels  121 us (72%)
  starting transfers between devices  29 us (17%)
  waiting for transfers between devices  17.3 us (10%)
    pallas_call x1, Pallas kernels, hi_attention(): pl.pallas_call(hi_kernel, grid_spec=pltpu.PrefetchScalarGridSpec(num_scal...  109 us
    ppermute x13, starting transfers between devices, trade(): return lax.ppermute(value, ('seq', 'head'), pairs)  22.4 us
    ppermute x13, waiting for transfers between devices, trade(): return lax.ppermute(value, ('seq', 'head'), pairs)  14 us
    ppermute x3, starting transfers between devices, local(): lax.ppermute(pieces[step], 'seq', z_shift(step))  6.57 us
    pallas_call x1, Pallas kernels, prep(): pl.pallas_call(prep_kernel, grid_spec=pltpu.PrefetchScalarGridSpec(num_sc...  4.46 us
    pallas_call x1, Pallas kernels, early_frames(): pl.pallas_call(early_kernel, grid_spec=pltpu.PrefetchScalarGridSpec(num_s...  3.96 us
  transfers between devices with their start and end apart: 16, of which 11 were waited for; matrix products, arithmetic and copies ran while one was open for 0% of the time, Pallas kernels for 5%

profile of v5, /device:TPU:1, one launch (start us, length us, event | category | flops | bytes accessed | tf_op | source)
XLA Modules:
  0.0 168.6 jit_solution(8767824653795495970)
XLA Ops:
  0.6 1.1 pack.1
  1.7 2.5 %collective-permute-start = (bf16[128,384]{1,0:T(8,128)(2,1)S(1)}, bf16[128,384]{1,0:T(8,128)(2,1)S(1)}, u32[]{:S(2)}, u32[]{:S(2)}) collective-permute-start(bf16[128,384]{1,0:T(8,128)(2,1)S(1)} %get-tuple-element.25), channel_id=1, source_target_pairs={{0,16},{8,24},{16,32},{24,40},{32,48},{40,56},{48,0},{56,8},{64,80... | collective-permute-start | bytes 294920 | tf_op jit(solution)/shard_map/ppermute | solution.py:468
  4.3 3.3 %collective-permute-start.1 = (bf16[128,384]{1,0:T(8,128)(2,1)S(1)}, bf16[128,384]{1,0:T(8,128)(2,1)S(1)}, u32[]{:S(2)}, u32[]{:S(2)}) collective-permute-start(bf16[128,384]{1,0:T(8,128)(2,1)S(1)} %get-tuple-element.26), channel_id=1, source_target_pairs={{0,32},{8,40},{16,48},{24,56},{32,0},{40,8},{48,16},{56,24},{64,96... | collective-permute-start | bytes 294920 | tf_op jit(solution)/shard_map/ppermute | solution.py:468
  7.6 0.7 collective-permute-start.2
  8.3 0.6 collective-permute-done.p1
  8.9 2.7 %collective-permute-done.1.p2 = bf16[128,384]{1,0:T(8,128)(2,1)S(1)} collective-permute-done((bf16[128,384]{1,0:T(8,128)(2,1)S(1)}, bf16[128,384]{1,0:T(8,128)(2,1)S(1)}, u32[]{:S(2)}, u32[]{:S(2)}) %collective-permute-start.1) | collective-permute-done | bytes 98336 | tf_op jit(solution)/shard_map/ppermute | solution.py:468
  11.6 0.0 collective-permute-done.2.p3
  11.6 2.8 %collective-permute-start.4 = (bf16[512,256]{1,0:T(8,128)(2,1)S(1)}, bf16[512,256]{1,0:T(8,128)(2,1)S(1)}, u32[]{:S(2)}, u32[]{:S(2)}) collective-permute-start(bf16[512,256]{1,0:T(8,128)(2,1)S(1)} %pad_maximum_fusion.kv0), channel_id=1, source_target_pairs={{0,64},{1,65},{2,66},{3,67},{4,68},{5,69},{6,70},{7,71},{8,72},{9,... | collective-permute-start | bytes 786440 | tf_op jit(solution)/shard_map/ppermute | solution.py:416
  14.5 0.1 pad_add_fusion.pos
  14.5 0.0 copy-start
  14.5 0.0 copy-start.2
  14.5 0.0 copy-start.3
  14.5 0.0 copy-start.4
  14.6 4.5 %prep.1 = (bf16[128,256]{1,0:T(8,128)(2,1)S(1)}, f32[16,128]{1,0:T(8,128)S(1)}, bf16[4,128,256]{2,1,0:T(8,128)(2,1)S(1)}, bf16[128,256]{1,0:T(8,128)(2,1)S(1)}, bf16[128,256]{1,0:T(8,128)(2,1)S(1)}) custom-call(s32[4]{0:T(128)S(1)} %pad_add_fusion.pos, bf16[512,4096]{1,0:T(8,128)(2,1)} %ow.1, bf16[4096,128]{1,0:T(8,128)(2,1)} %lw.1, bf16[128,4096]{1,0:T(8,128)(2,1)} %hid.1, ...), custom_call_target="tpu_custom_call" | custom-call | flops 900000000 | bytes 5000000 | tf_op jit(solution)/shard_map/prep/pallas_call | solution.py:86
  19.0 2.2 %collective-permute-start.3 = (bf16[512,256]{1,0:T(8,128)(2,1)S(1)}, bf16[512,256]{1,0:T(8,128)(2,1)S(1)}, u32[]{:S(2)}, u32[]{:S(2)}) collective-permute-start(bf16[512,256]{1,0:T(8,128)(2,1)S(1)} %pad_maximum_fusion.kv0), channel_id=1, source_target_pairs={{0,8},{1,9},{2,10},{3,11},{4,12},{5,13},{6,14},{7,15},{8,0},{9,1},... | collective-permute-start | bytes 786440 | tf_op jit(solution)/shard_map/ppermute | solution.py:416
  21.2 0.0 collective-permute-done.4.kv2
  21.2 0.7 collective-permute-start.5
  21.9 0.4 collective-permute-done.3.kv1
  22.4 0.7 collective-permute-done.5.kv3
  23.1 2.8 %low.1 = bf16[512,128]{1,0:T(8,128)(2,1)S(1)} custom-call(s32[4]{0:T(128)S(1)} %pad_add_fusion.pos, bf16[128,384]{1,0:T(8,128)(2,1)S(1)} %get-tuple-element.24.p0, bf16[128,384]{1,0:T(8,128)(2,1)S(1)} %collective-permute-done.p1, bf16[128,384]{1,0:T(8,128)(2,1)S(1)} %collective-permute-done.1.p2, bf16[128,384]{1,0:T(8,128)(2,1)S(1)} %collective-permute-done.2.p3, ...), custom_call_target="tpu_custom_call" | custom-call | tf_op jit(solution)/shard_map/low/pallas_call | solution.py:164
  25.9 1.3 collective-permute-start.6
  27.2 3.5 %collective-permute-done.6 = bf16[512,128]{1,0:T(8,128)(2,1)S(1)} collective-permute-done((bf16[512,128]{1,0:T(8,128)(2,1)S(1)}, bf16[512,128]{1,0:T(8,128)(2,1)S(1)}, u32[]{:S(2)}, u32[]{:S(2)}) %collective-permute-start.6) | collective-permute-done | bytes 131104 | tf_op jit(solution)/shard_map/ppermute | solution.py:416
  30.7 2.1 %collective-permute-start.9 = (bf16[512,128]{1,0:T(8,128)(2,1)S(1)}, bf16[512,128]{1,0:T(8,128)(2,1)S(1)}, u32[]{:S(2)}, u32[]{:S(2)}) collective-permute-start(bf16[512,128]{1,0:T(8,128)(2,1)S(1)} %add_convert_fusion.2), channel_id=1, source_target_pairs={{0,4},{1,5},{2,6},{3,7},{4,0},{5,1},{6,2},{7,3},{8,40},{9,41},{10,... | collective-permute-start | bytes 393224 | tf_op jit(solution)/shard_map/ppermute | solution.py:416
  32.8 2.3 %collective-permute-start.8 = (bf16[512,128]{1,0:T(8,128)(2,1)S(1)}, bf16[512,128]{1,0:T(8,128)(2,1)S(1)}, u32[]{:S(2)}, u32[]{:S(2)}) collective-permute-start(bf16[512,128]{1,0:T(8,128)(2,1)S(1)} %add_convert_fusion.2), channel_id=1, source_target_pairs={{0,6},{1,7},{2,4},{3,5},{4,2},{5,3},{6,0},{7,1},{8,56},{9,57},{10,... | collective-permute-start | bytes 393224 | tf_op jit(solution)/shard_map/ppermute | solution.py:416
  35.1 0.0 collective-permute-start.7
  35.1 1.0 collective-permute-done.9
  36.1 2.0 %collective-permute-done.8 = bf16[512,128]{1,0:T(8,128)(2,1)S(1)} collective-permute-done((bf16[512,128]{1,0:T(8,128)(2,1)S(1)}, bf16[512,128]{1,0:T(8,128)(2,1)S(1)}, u32[]{:S(2)}, u32[]{:S(2)}) %collective-permute-start.8) | collective-permute-done | bytes 131104 | tf_op jit(solution)/shard_map/ppermute | solution.py:416
  38.1 0.8 collective-permute-done.7
  38.9 0.1 add_convert_fusion.1
  39.0 3.3 %collective-permute-start.12 = (bf16[512,128]{1,0:T(8,128)(2,1)S(1)}, bf16[512,128]{1,0:T(8,128)(2,1)S(1)}, u32[]{:S(2)}, u32[]{:S(2)}) collective-permute-start(bf16[512,128]{1,0:T(8,128)(2,1)S(1)} %add_convert_fusion.1), channel_id=1, source_target_pairs={{0,32},{1,33},{2,34},{3,35},{4,36},{5,37},{6,38},{7,39},{8,12},{9,... | collective-permute-start | bytes 393224 | tf_op jit(solution)/shard_map/ppermute | solution.py:416
  42.2 0.8 collective-permute-start.11
  43.0 0.0 collective-permute-start.10
  43.0 1.6 collective-permute-done.12
  44.6 3.0 %collective-permute-done.11 = bf16[512,128]{1,0:T(8,128)(2,1)S(1)} collective-permute-done((bf16[512,128]{1,0:T(8,128)(2,1)S(1)}, bf16[512,128]{1,0:T(8,128)(2,1)S(1)}, u32[]{:S(2)}, u32[]{:S(2)}) %collective-permute-start.11) | collective-permute-done | bytes 131104 | tf_op jit(solution)/shard_map/ppermute | solution.py:416
  47.6 0.0 collective-permute-done.10
  47.6 0.1 add_convert_fusion.lat0
  47.6 3.8 %collective-permute-start.13 = (bf16[512,128]{1,0:T(8,128)(2,1)S(1)}, bf16[512,128]{1,0:T(8,128)(2,1)S(1)}, u32[]{:S(2)}, u32[]{:S(2)}) collective-permute-start(bf16[512,128]{1,0:T(8,128)(2,1)S(1)} %add_convert_fusion.lat0), channel_id=1, source_target_pairs={{0,8},{1,9},{2,10},{3,11},{4,12},{5,13},{6,14},{7,15},{8,0},{9,1},... | collective-permute-start | bytes 393224 | tf_op jit(solution)/shard_map/ppermute | solution.py:416
  51.5 2.5 %collective-permute-start.14 = (bf16[512,128]{1,0:T(8,128)(2,1)S(1)}, bf16[512,128]{1,0:T(8,128)(2,1)S(1)}, u32[]{:S(2)}, u32[]{:S(2)}) collective-permute-start(bf16[512,128]{1,0:T(8,128)(2,1)S(1)} %add_convert_fusion.lat0), channel_id=1, source_target_pairs={{0,65},{1,64},{2,67},{3,66},{4,69},{5,68},{6,71},{7,70},{8,73},{9,... | collective-permute-start | bytes 393224 | tf_op jit(solution)/shard_map/ppermute | solution.py:416
  54.0 0.0 collective-permute-done.13.lat1
  54.0 0.0 copy-done
  54.0 0.0 copy-done.2
  54.0 0.0 copy-done.3
  54.0 0.0 copy-done.4
  54.0 0.0 copy-start.1
  54.0 4.0 %early.1 = (bf16[4,512,128]{2,1,0:T(8,128)(2,1)S(1)}, bf16[4,512,128]{2,1,0:T(8,128)(2,1)S(1)}, f32[8,128]{1,0:T(8,128)S(1)}) custom-call(s32[4]{0:T(128)S(1)} %pad_add_fusion.pos, bf16[512,128]{1,0:T(8,128)(2,1)S(1)} %add_convert_fusion.lat0, bf16[512,128]{1,0:T(8,128)(2,1)S(1)} %collective-permute-done.13.lat1, bf16[3456,512]{1,0:T(8,128)(2,1)S(1)} %bitcast.9, ...), custom_call_target="tpu_custom_call" | custom-call | flops 2400000000 | bytes 6000000 | tf_op jit(solution)/shard_map/early/pallas_call | solution.py:243
  58.0 0.0 collective-permute-done.14.lat2
  58.0 0.6 collective-permute-start.15
  58.6 1.0 collective-permute-done.15.lat3
  59.6 0.0 copy-done.1
  59.6 109.0 %hi.1 = (bf16[512,512]{1,0:T(8,128)(2,1)}, bf16[64,128]{1,0:T(8,128)(2,1)}) custom-call(s32[4]{0:T(128)S(1)} %pad_add_fusion.pos, bf16[512,128]{1,0:T(8,128)(2,1)S(1)} %add_convert_fusion.lat0, bf16[512,128]{1,0:T(8,128)(2,1)S(1)} %collective-permute-done.13.lat1, bf16[512,128]{1,0:T(8,128)(2,1)S(1)} %collective-permute-done.14.lat2, ...), custom_call_target="tpu_custom_call" | custom-call | tf_op jit(solution)/shard_map/hi/pallas_call | solution.py:377
  (6 shorter events, 0.1 us)
Async XLA Ops:
  1.7 7.2 %collective-permute-start = (bf16[128,384]{1,0:T(8,128)(2,1)S(1)}, bf16[128,384]{1,0:T(8,128)(2,1)S(1)}, u32[]{:S(2)}, u32[]{:S(2)}) collective-permute-start(bf16[128,384]{1,0:T(8,128)(2,1)S(1)} %get-tuple-element.25), channel_id=1, source_target_pairs={{0,16},{8,24},{16,32},{24,40},{32,48},{40,56},{48,0},{56,8},{64,80... | collective-permute-start | bytes 294920 | tf_op jit(solution)/shard_map/ppermute | solution.py:468
  4.3 7.3 %collective-permute-start.1 = (bf16[128,384]{1,0:T(8,128)(2,1)S(1)}, bf16[128,384]{1,0:T(8,128)(2,1)S(1)}, u32[]{:S(2)}, u32[]{:S(2)}) collective-permute-start(bf16[128,384]{1,0:T(8,128)(2,1)S(1)} %get-tuple-element.26), channel_id=1, source_target_pairs={{0,32},{8,40},{16,48},{24,56},{32,0},{40,8},{48,16},{56,24},{64,96... | collective-permute-start | bytes 294920 | tf_op jit(solution)/shard_map/ppermute | solution.py:468
  7.6 4.0 %collective-permute-start.2 = (bf16[128,384]{1,0:T(8,128)(2,1)S(1)}, bf16[128,384]{1,0:T(8,128)(2,1)S(1)}, u32[]{:S(2)}, u32[]{:S(2)}) collective-permute-start(bf16[128,384]{1,0:T(8,128)(2,1)S(1)} %get-tuple-element.27), channel_id=1, source_target_pairs={{0,48},{8,56},{16,0},{24,8},{32,16},{40,24},{48,32},{56,40},{64,11... | collective-permute-start | bytes 294920 | tf_op jit(solution)/shard_map/ppermute | solution.py:468
  11.6 9.6 %collective-permute-start.4 = (bf16[512,256]{1,0:T(8,128)(2,1)S(1)}, bf16[512,256]{1,0:T(8,128)(2,1)S(1)}, u32[]{:S(2)}, u32[]{:S(2)}) collective-permute-start(bf16[512,256]{1,0:T(8,128)(2,1)S(1)} %pad_maximum_fusion.kv0), channel_id=1, source_target_pairs={{0,64},{1,65},{2,66},{3,67},{4,68},{5,69},{6,70},{7,71},{8,72},{9,... | collective-permute-start | bytes 786440 | tf_op jit(solution)/shard_map/ppermute | solution.py:416
  14.5 39.4 %copy-start = (bf16[3,3,3,128,512]{4,3,2,1,0:T(8,128)(2,1)S(1)}, bf16[3,3,3,128,512]{4,3,2,1,0:T(8,128)(2,1)}, u32[]{:S(2)}) copy-start(bf16[3,3,3,128,512]{4,3,2,1,0:T(8,128)(2,1)} %param.21) | copy-start | bytes 10616836
  14.5 39.4 %copy-start.2 = (bf16[512,512]{1,0:T(8,128)(2,1)S(1)}, bf16[512,512]{1,0:T(8,128)(2,1)}, u32[]{:S(2)}) copy-start(bf16[512,512]{1,0:T(8,128)(2,1)} %second.3) | copy-start | bytes 1572868
  14.5 39.4 %copy-start.3 = (f32[512]{0:T(512)S(1)}, f32[512]{0:T(512)}, u32[]{:S(2)}) copy-start(f32[512]{0:T(512)} %param.22) | copy-start | bytes 6148
  14.5 39.4 %copy-start.4 = (f32[512]{0:T(512)S(1)}, f32[512]{0:T(512)}, u32[]{:S(2)}) copy-start(f32[512]{0:T(512)} %param.24) | copy-start | bytes 6148
  19.0 3.4 %collective-permute-start.3 = (bf16[512,256]{1,0:T(8,128)(2,1)S(1)}, bf16[512,256]{1,0:T(8,128)(2,1)S(1)}, u32[]{:S(2)}, u32[]{:S(2)}) collective-permute-start(bf16[512,256]{1,0:T(8,128)(2,1)S(1)} %pad_maximum_fusion.kv0), channel_id=1, source_target_pairs={{0,8},{1,9},{2,10},{3,11},{4,12},{5,13},{6,14},{7,15},{8,0},{9,1},... | collective-permute-start | bytes 786440 | tf_op jit(solution)/shard_map/ppermute | solution.py:416
  21.2 1.9 %collective-permute-start.5 = (bf16[512,256]{1,0:T(8,128)(2,1)S(1)}, bf16[512,256]{1,0:T(8,128)(2,1)S(1)}, u32[]{:S(2)}, u32[]{:S(2)}) collective-permute-start(bf16[512,256]{1,0:T(8,128)(2,1)S(1)} %collective-permute-done.4.kv2), channel_id=1, source_target_pairs={{0,8},{1,9},{2,10},{3,11},{4,12},{5,13},{6,14},{7,15},{8,0},{9,1},... | collective-permute-start | bytes 786440 | tf_op jit(solution)/shard_map/ppermute | solution.py:416
  25.9 4.8 %collective-permute-start.6 = (bf16[512,128]{1,0:T(8,128)(2,1)S(1)}, bf16[512,128]{1,0:T(8,128)(2,1)S(1)}, u32[]{:S(2)}, u32[]{:S(2)}) collective-permute-start(bf16[512,128]{1,0:T(8,128)(2,1)S(1)} %low.1), channel_id=1, source_target_pairs={{0,1},{1,0},{2,3},{3,2},{4,5},{5,4},{6,7},{7,6},{8,9},{9,8},{10,11... | collective-permute-start | bytes 393224 | tf_op jit(solution)/shard_map/ppermute | solution.py:416
  30.7 5.4 %collective-permute-start.9 = (bf16[512,128]{1,0:T(8,128)(2,1)S(1)}, bf16[512,128]{1,0:T(8,128)(2,1)S(1)}, u32[]{:S(2)}, u32[]{:S(2)}) collective-permute-start(bf16[512,128]{1,0:T(8,128)(2,1)S(1)} %add_convert_fusion.2), channel_id=1, source_target_pairs={{0,4},{1,5},{2,6},{3,7},{4,0},{5,1},{6,2},{7,3},{8,40},{9,41},{10,... | collective-permute-start | bytes 393224 | tf_op jit(solution)/shard_map/ppermute | solution.py:416
  32.8 5.3 %collective-permute-start.8 = (bf16[512,128]{1,0:T(8,128)(2,1)S(1)}, bf16[512,128]{1,0:T(8,128)(2,1)S(1)}, u32[]{:S(2)}, u32[]{:S(2)}) collective-permute-start(bf16[512,128]{1,0:T(8,128)(2,1)S(1)} %add_convert_fusion.2), channel_id=1, source_target_pairs={{0,6},{1,7},{2,4},{3,5},{4,2},{5,3},{6,0},{7,1},{8,56},{9,57},{10,... | collective-permute-start | bytes 393224 | tf_op jit(solution)/shard_map/ppermute | solution.py:416
  35.1 3.8 %collective-permute-start.7 = (bf16[512,128]{1,0:T(8,128)(2,1)S(1)}, bf16[512,128]{1,0:T(8,128)(2,1)S(1)}, u32[]{:S(2)}, u32[]{:S(2)}) collective-permute-start(bf16[512,128]{1,0:T(8,128)(2,1)S(1)} %add_convert_fusion.2), channel_id=1, source_target_pairs={{0,2},{1,3},{2,0},{3,1},{4,6},{5,7},{6,4},{7,5},{8,24},{9,25},{10,... | collective-permute-start | bytes 393224 | tf_op jit(solution)/shard_map/ppermute | solution.py:416
  39.0 5.6 %collective-permute-start.12 = (bf16[512,128]{1,0:T(8,128)(2,1)S(1)}, bf16[512,128]{1,0:T(8,128)(2,1)S(1)}, u32[]{:S(2)}, u32[]{:S(2)}) collective-permute-start(bf16[512,128]{1,0:T(8,128)(2,1)S(1)} %add_convert_fusion.1), channel_id=1, source_target_pairs={{0,32},{1,33},{2,34},{3,35},{4,36},{5,37},{6,38},{7,39},{8,12},{9,... | collective-permute-start | bytes 393224 | tf_op jit(solution)/shard_map/ppermute | solution.py:416
  42.2 5.3 %collective-permute-start.11 = (bf16[512,128]{1,0:T(8,128)(2,1)S(1)}, bf16[512,128]{1,0:T(8,128)(2,1)S(1)}, u32[]{:S(2)}, u32[]{:S(2)}) collective-permute-start(bf16[512,128]{1,0:T(8,128)(2,1)S(1)} %add_convert_fusion.1), channel_id=1, source_target_pairs={{0,48},{1,49},{2,50},{3,51},{4,52},{5,53},{6,54},{7,55},{8,14},{9,... | collective-permute-start | bytes 393224 | tf_op jit(solution)/shard_map/ppermute | solution.py:416
  43.0 4.5 %collective-permute-start.10 = (bf16[512,128]{1,0:T(8,128)(2,1)S(1)}, bf16[512,128]{1,0:T(8,128)(2,1)S(1)}, u32[]{:S(2)}, u32[]{:S(2)}) collective-permute-start(bf16[512,128]{1,0:T(8,128)(2,1)S(1)} %add_convert_fusion.1), channel_id=1, source_target_pairs={{0,16},{1,17},{2,18},{3,19},{4,20},{5,21},{6,22},{7,23},{8,10},{9,... | collective-permute-start | bytes 393224 | tf_op jit(solution)/shard_map/ppermute | solution.py:416
  47.6 6.3 %collective-permute-start.13 = (bf16[512,128]{1,0:T(8,128)(2,1)S(1)}, bf16[512,128]{1,0:T(8,128)(2,1)S(1)}, u32[]{:S(2)}, u32[]{:S(2)}) collective-permute-start(bf16[512,128]{1,0:T(8,128)(2,1)S(1)} %add_convert_fusion.lat0), channel_id=1, source_target_pairs={{0,8},{1,9},{2,10},{3,11},{4,12},{5,13},{6,14},{7,15},{8,0},{9,1},... | collective-permute-start | bytes 393224 | tf_op jit(solution)/shard_map/ppermute | solution.py:416
  51.5 6.5 %collective-permute-start.14 = (bf16[512,128]{1,0:T(8,128)(2,1)S(1)}, bf16[512,128]{1,0:T(8,128)(2,1)S(1)}, u32[]{:S(2)}, u32[]{:S(2)}) collective-permute-start(bf16[512,128]{1,0:T(8,128)(2,1)S(1)} %add_convert_fusion.lat0), channel_id=1, source_target_pairs={{0,65},{1,64},{2,67},{3,66},{4,69},{5,68},{6,71},{7,70},{8,73},{9,... | collective-permute-start | bytes 393224 | tf_op jit(solution)/shard_map/ppermute | solution.py:416
  54.0 5.6 %copy-start.1 = (bf16[128,4096]{1,0:T(8,128)(2,1)S(1)}, bf16[128,4096]{1,0:T(8,128)(2,1)}, u32[]{:S(2)}) copy-start(bf16[128,4096]{1,0:T(8,128)(2,1)} %wv.1) | copy-start | bytes 3145732
  58.0 1.6 collective-permute-start.15

commit v6 on v4

--- a/solution.py
+++ b/solution.py
@@ -176,9 +176,28 @@
     )(pos, *args)
 
 
+PAIRS = FRAMES // 2
 CHUNK = 4
+TAPS = 9 * HD
 BLOCK = 2048
 TINY = 2.0**-90
+
+
+def mids_kernel(conv, out):
+    ends = conv[0:TAPS, :].astype(F32) + conv[2 * TAPS : 3 * TAPS, :].astype(F32)
+    centre = conv[TAPS : 2 * TAPS, :].astype(F32)
+    out[0:TAPS, :] = (0.5 * (ends + centre)).astype(BF)
+    out[TAPS : 2 * TAPS, :] = (0.5 * (ends - centre)).astype(BF)
+
+
+def middle_weights(conv):
+    return pl.pallas_call(
+        mids_kernel,
+        out_shape=jax.ShapeDtypeStruct((2 * TAPS, conv.shape[1]), BF),
+        compiler_params=pltpu.CompilerParams(vmem_limit_bytes=SMALL),
+        cost_estimate=pl.CostEstimate(flops=3_000_000, bytes_accessed=6_000_000, transcendentals=0),
+        name="mids",
+    )(conv)
 
 
 def hi_kernel(
@@ -188,6 +207,7 @@
     lat2,
     lat3,
     conv,
+    mids,
     b1,
     second,
     b2,
@@ -205,55 +225,70 @@
     nat_s,
     acc_s,
     bound_s,
+    prod_s,
 ):
     x, z, c, g = pos[0], pos[1], pos[2], pos[3]
     for dx, dc, piece in ((0, 0, lat0), (0, 1, lat1), (1, 0, lat2), (1, 1, lat3)):
         px = lax.bitwise_xor(x, dx)
         pc = lax.bitwise_xor(c, dc)
         for pz in range(4):
-            lat_s[px * 8 + pz * 2 + pc] = piece[pz * TOK : (pz + 1) * TOK, :]
-    edge = jnp.zeros((3, 1, H_LO + 2, W_LO, HD), BF)
-    grid_s[:, 0:1] = edge
-    grid_s[:, FRAMES + 1 : FRAMES + 2] = edge
-    edge = jnp.zeros((3, FRAMES + 2, 1, W_LO, HD), BF)
+            lat_s[1 + px * 8 + pz * 2 + pc] = piece[pz * TOK : (pz + 1) * TOK, :]
+    lat_s[0:1] = jnp.zeros((1, TOK, HD), BF)
+    lat_s[FRAMES + 1 : FRAMES + 2] = jnp.zeros((1, TOK, HD), BF)
+    edge = jnp.zeros((12, PAIRS, 1, W_LO, HD), BF)
     grid_s[:, :, 0:1] = edge
     grid_s[:, :, H_LO + 1 : H_LO + 2] = edge
-    lat = lat_s[...].reshape(FRAMES * TOK, HD).astype(F32)
-    column = lax.rem(lax.broadcasted_iota(jnp.int32, (FRAMES * TOK, HD), 0), W_LO)
-    left = jnp.where(column == 0, 0.0, pltpu.roll(lat, 1, 0))
-    right = jnp.where(column == W_LO - 1, 0.0, pltpu.roll(lat, FRAMES * TOK - 1, 0))
-    for index, shifted in enumerate((left, lat, right)):
-        grid_s[index, 1 : FRAMES + 1, 1 : H_LO + 1] = shifted.astype(BF).reshape(FRAMES, H_LO, W_LO, HD)
+    d0, d1, d2, d3 = (
+        jnp.concatenate([lat_s[2 * pair + d : 2 * pair + d + 1] for pair in range(PAIRS)], axis=0).astype(F32)
+        for d in range(4)
+    )
+    count = PAIRS * TOK
+    column = lax.broadcasted_iota(jnp.int32, (count, HD), 0) & (W_LO - 1)
+    for index, mixed in enumerate((d0 - d2, d1 + d2, d2 - d1, d1 - d3)):
+        mixed = mixed.reshape(count, HD)
+        left = jnp.where(column == 0, 0.0, pltpu.roll(mixed, 1, 0))
+        right = jnp.where(column == W_LO - 1, 0.0, pltpu.roll(mixed, count - 1, 0))
+        for offset, shifted in enumerate((left, mixed, right)):
+            grid_s[3 * index + offset, :, 1 : H_LO + 1] = shifted.astype(BF).reshape(PAIRS, H_LO, W_LO, HD)
 
     val_s[:, HD : 2 * HD] = jnp.ones((KEYS, HD), BF)
     biggest = jnp.zeros((1, 1), F32)
     rows = CHUNK * TOK
-    for first in range(0, FRAMES, CHUNK):
-        taps = []
-        for a in range(3):
+    weights = (conv.at[0:TAPS], mids.at[0:TAPS], mids.at[TAPS : 2 * TAPS], conv.at[2 * TAPS : 3 * TAPS])
+    for first in range(0, PAIRS, CHUNK):
+        def product(index):
+            taps = []
             for b in range(3):
                 for t in range(3):
-                    taps.append(grid_s[t, first + a : first + a + CHUNK, b : b + H_LO].reshape(rows, HD))
-        middle = dot(jnp.concatenate(taps, axis=1), conv[...]) + b1[...]
-        middle = (middle * (0.5 * jnp.tanh(0.5 * middle) + 0.5)).astype(BF)
-        sub = dot(middle, second[...]) + b2[...]
-        base = lat_s[first : first + CHUNK].reshape(rows, HD).astype(F32)
-        for s in range(4):
-            up = (sub[:, s * HD : (s + 1) * HD] + base).astype(BF)
-            upf = up.astype(F32)
-            square = jnp.sum(dot2(up, gk[...]) * upf, axis=1, keepdims=True)
-            inverse = lax.rsqrt(jnp.maximum(square, 0.0) * (1.0 / 4096.0) + 1e-6)
-            key = (upf * inverse).astype(BF)
-            where = pl.ds(s * FRAMES * TOK + first * TOK, rows)
-            val_s[where, 0:HD] = up
-            key_s[where, :] = key
-            keyf = key.astype(F32)
-            length = jnp.sum(keyf * keyf, axis=1, keepdims=True)
-            biggest = jnp.maximum(biggest, jnp.max(length, axis=0, keepdims=True))
-
-    frame = x * 8 + z * 2 + c
+                    taps.append(grid_s[3 * index + t, first : first + CHUNK, b : b + H_LO].reshape(rows, HD))
+            return dot(jnp.concatenate(taps, axis=1), weights[index][...])
+
+        prod_s[0] = product(1)
+        prod_s[1] = product(2)
+        prod_s[2] = prod_s[0] - prod_s[1] - product(3)
+        prod_s[0] = prod_s[0] + prod_s[1] + product(0)
+        for parity in range(2):
+            middle = prod_s[2 * parity] + b1[...]
+            middle = (middle * (0.5 * jnp.tanh(0.5 * middle) + 0.5)).astype(BF)
+            sub = dot(middle, second[...]) + b2[...]
+            mine = [lat_s[1 + 2 * pair + parity] for pair in range(first, first + CHUNK)]
+            base = jnp.concatenate(mine, axis=0).astype(F32)
+            for s in range(4):
+                up = (sub[:, s * HD : (s + 1) * HD] + base).astype(BF)
+                upf = up.astype(F32)
+                square = jnp.sum(dot2(up, gk[...]) * upf, axis=1, keepdims=True)
+                inverse = lax.rsqrt(jnp.maximum(square, 0.0) * (1.0 / 4096.0) + 1e-6)
+                key = (upf * inverse).astype(BF)
+                where = pl.ds(s * FRAMES * TOK + 2 * first * TOK + parity * rows, rows)
+                val_s[where, 0:HD] = up
+                key_s[where, :] = key
+                keyf = key.astype(F32)
+                length = jnp.sum(keyf * keyf, axis=1, keepdims=True)
+                biggest = jnp.maximum(biggest, jnp.max(length, axis=0, keepdims=True))
+
+    place = x * (2 * CHUNK) + c * CHUNK + z
     own = jnp.concatenate(
-        [val_s[pl.ds(pl.multiple_of(s * FRAMES * TOK + frame * TOK, TOK), TOK), 0:HD] for s in range(4)], axis=0
+        [val_s[pl.ds(pl.multiple_of(s * FRAMES * TOK + place * TOK, TOK), TOK), 0:HD] for s in range(4)], axis=0
     )
     to = lax.broadcasted_iota(jnp.int32, (4 * TOK, 4 * TOK), 0)
     source = lax.broadcasted_iota(jnp.int32, (4 * TOK, 4 * TOK), 1)
@@ -310,10 +345,8 @@
         attn_out[:, columns] = dot(mixed, wv[:, columns]).astype(BF)
 
 
-def hi_attention(pos, lats, conv_first, bias_first, conv_second, bias_second, gq, gk, m, value_weight):
-    mid = conv_second.shape[0]
-    conv = conv_first.reshape(27 * HD, mid)
-    args = (*lats, conv, bias_first.reshape(1, -1), conv_second, bias_second.reshape(1, -1), gq, gk, m, value_weight)
+def hi_attention(pos, lats, conv, mids, bias_first, conv_second, bias_second, gq, gk, m, value_weight):
+    args = (*lats, conv, mids, bias_first.reshape(1, -1), conv_second, bias_second.reshape(1, -1), gq, gk, m, value_weight)
     in_specs = [whole(a.shape) for a in args]
     in_specs[-1] = pl.BlockSpec((HD, 4 * HD), lambda i, pos: (0, pos[3]))
     return pl.pallas_call(
@@ -324,14 +357,15 @@
             in_specs=in_specs,
             out_specs=[whole((4 * TOK, 4 * HD)), whole((2 * W_LO, HD))],
             scratch_shapes=[
-                pltpu.VMEM((3, FRAMES + 2, H_LO + 2, W_LO, HD), BF),
-                pltpu.VMEM((FRAMES, TOK, HD), BF),
+                pltpu.VMEM((12, PAIRS, H_LO + 2, W_LO, HD), BF),
+                pltpu.VMEM((FRAMES + 2, TOK, HD), BF),
                 pltpu.VMEM((KEYS, HD), BF),
                 pltpu.VMEM((KEYS, 2 * HD), BF),
                 pltpu.VMEM((4, 4 * TOK, HD), BF),
                 pltpu.VMEM((4 * TOK, HD), F32),
                 pltpu.VMEM((4, 4 * TOK, 2 * HD), F32),
                 pltpu.VMEM((4, 4 * TOK, HD), F32),
+                pltpu.VMEM((3, CHUNK * TOK, conv.shape[1]), F32),
             ],
         ),
         out_shape=[
@@ -370,7 +404,7 @@
     return x ^ 3, y, z, core
 
 
-ROUNDS = ((("x", "x"), (1,)), (("y", "z"), (1, 3, 2)), (("z", "y"), (1, 3, 2)))
+ROUNDS = (("yz", (1, 3, 2)), ("zy", (1, 3, 2)))
 
 
 def along(axes, bit):
@@ -382,8 +416,11 @@
 
 
 def sum_round(value, axes, bits):
-    arrived = [trade(value, along(axes, bit)).astype(F32) for bit in bits]
-    return sum(arrived, value.astype(F32)).astype(BF)
+    return add_up(value, [trade(value, along(axes, bit)) for bit in bits])
+
+
+def add_up(value, arrived):
+    return sum((other.astype(F32) for other in arrived), value.astype(F32)).astype(BF)
 
 
 def local(
@@ -418,6 +455,9 @@
     kv_x, w2, hl, m, gq, gk = lax.optimization_barrier((kv_x, w2, hl, m, gq, gk))
     kv_xc = trade(kv_x, to_core)
     latent = low_attention(pos, pieces, (kv, kv_c, kv_x, kv_xc), w2, hl)
+    conv = conv_first.reshape(27 * HD, -1)
+    other, mids = lax.optimization_barrier((trade(latent, along("xx", 1)), middle_weights(conv)))
+    latent = add_up(latent, [other])
     for axes, bits in ROUNDS:
         latent = sum_round(latent, axes, bits)
     lat_x = trade(latent, to_x_near)
@@ -426,7 +466,8 @@
     attn, up = hi_attention(
         pos,
         (latent, lat_c, lat_x, lat_xc),
-        conv_first,
+        conv,
+        mids,
         bias_first,
         conv_second,
         bias_second,

time: 169 us -> 168 us (level)
  no operation moved by 1% of the time
where the time goes in v6:
time: 168 us
  Pallas kernels  119 us (71%)
  starting transfers between devices  32.1 us (19%)
  waiting for transfers between devices  16.5 us (10%)
    pallas_call x1, Pallas kernels, hi_attention(): pl.pallas_call(hi_kernel, grid_spec=pltpu.PrefetchScalarGridSpec(num_scal...  110 us
    ppermute x13, starting transfers between devices, trade(): return lax.ppermute(value, ('seq', 'head'), pairs)  25.5 us
    ppermute x13, waiting for transfers between devices, trade(): return lax.ppermute(value, ('seq', 'head'), pairs)  13.2 us
    ppermute x3, starting transfers between devices, local(): lax.ppermute(pieces[step], 'seq', z_shift(step))  6.57 us
    pallas_call x1, Pallas kernels, prep(): pl.pallas_call(prep_kernel, grid_spec=pltpu.PrefetchScalarGridSpec(num_sc...  4.44 us
  transfers between devices with their start and end apart: 16, of which 11 were waited for; matrix products, arithmetic and copies ran while one was open for 0% of the time, Pallas kernels for 3%

profile of v6, /device:TPU:1, one launch (start us, length us, event | category | flops | bytes accessed | tf_op | source)
XLA Modules:
  0.0 168.2 jit_solution(242762862984066485)
XLA Ops:
  0.6 1.1 pack.1
  1.7 2.5 %collective-permute-start = (bf16[128,384]{1,0:T(8,128)(2,1)S(1)}, bf16[128,384]{1,0:T(8,128)(2,1)S(1)}, u32[]{:S(2)}, u32[]{:S(2)}) collective-permute-start(bf16[128,384]{1,0:T(8,128)(2,1)S(1)} %get-tuple-element.20), channel_id=1, source_target_pairs={{0,16},{8,24},{16,32},{24,40},{32,48},{40,56},{48,0},{56,8},{64,80... | collective-permute-start | bytes 294920 | tf_op jit(solution)/shard_map/ppermute | solution.py:447
  4.3 3.3 %collective-permute-start.1 = (bf16[128,384]{1,0:T(8,128)(2,1)S(1)}, bf16[128,384]{1,0:T(8,128)(2,1)S(1)}, u32[]{:S(2)}, u32[]{:S(2)}) collective-permute-start(bf16[128,384]{1,0:T(8,128)(2,1)S(1)} %get-tuple-element.21), channel_id=1, source_target_pairs={{0,32},{8,40},{16,48},{24,56},{32,0},{40,8},{48,16},{56,24},{64,96... | collective-permute-start | bytes 294920 | tf_op jit(solution)/shard_map/ppermute | solution.py:447
  7.6 0.7 collective-permute-start.2
  8.3 0.6 collective-permute-done.p1
  8.9 2.7 %collective-permute-done.1.p2 = bf16[128,384]{1,0:T(8,128)(2,1)S(1)} collective-permute-done((bf16[128,384]{1,0:T(8,128)(2,1)S(1)}, bf16[128,384]{1,0:T(8,128)(2,1)S(1)}, u32[]{:S(2)}, u32[]{:S(2)}) %collective-permute-start.1) | collective-permute-done | bytes 98336 | tf_op jit(solution)/shard_map/ppermute | solution.py:447
  11.6 0.0 collective-permute-done.2.p3
  11.6 2.8 %collective-permute-start.4 = (bf16[512,256]{1,0:T(8,128)(2,1)S(1)}, bf16[512,256]{1,0:T(8,128)(2,1)S(1)}, u32[]{:S(2)}, u32[]{:S(2)}) collective-permute-start(bf16[512,256]{1,0:T(8,128)(2,1)S(1)} %pad_maximum_fusion.kv0), channel_id=1, source_target_pairs={{0,64},{1,65},{2,66},{3,67},{4,68},{5,69},{6,70},{7,71},{8,72},{9,... | collective-permute-start | bytes 786440 | tf_op jit(solution)/shard_map/ppermute | solution.py:392
  14.5 0.1 pad_add_fusion.pos
  14.5 0.0 copy-start
  14.5 4.4 %prep.1 = (bf16[128,256]{1,0:T(8,128)(2,1)S(1)}, f32[16,128]{1,0:T(8,128)S(1)}, bf16[4,128,256]{2,1,0:T(8,128)(2,1)S(1)}, bf16[128,256]{1,0:T(8,128)(2,1)S(1)}, bf16[128,256]{1,0:T(8,128)(2,1)S(1)}) custom-call(s32[4]{0:T(128)S(1)} %pad_add_fusion.pos, bf16[512,4096]{1,0:T(8,128)(2,1)} %ow.1, bf16[4096,128]{1,0:T(8,128)(2,1)} %lw.1, bf16[128,4096]{1,0:T(8,128)(2,1)} %hid.1, ...), custom_call_target="tpu_custom_call" | custom-call | flops 900000000 | bytes 5000000 | tf_op jit(solution)/shard_map/prep/pallas_call | solution.py:86
  19.0 2.2 %collective-permute-start.3 = (bf16[512,256]{1,0:T(8,128)(2,1)S(1)}, bf16[512,256]{1,0:T(8,128)(2,1)S(1)}, u32[]{:S(2)}, u32[]{:S(2)}) collective-permute-start(bf16[512,256]{1,0:T(8,128)(2,1)S(1)} %pad_maximum_fusion.kv0), channel_id=1, source_target_pairs={{0,8},{1,9},{2,10},{3,11},{4,12},{5,13},{6,14},{7,15},{8,0},{9,1},... | collective-permute-start | bytes 786440 | tf_op jit(solution)/shard_map/ppermute | solution.py:392
  21.2 0.0 collective-permute-done.4.kv2
  21.2 0.7 collective-permute-start.5
  21.9 0.4 collective-permute-done.3.kv1
  22.4 0.7 collective-permute-done.5.kv3
  23.1 2.8 %low.1 = bf16[512,128]{1,0:T(8,128)(2,1)S(1)} custom-call(s32[4]{0:T(128)S(1)} %pad_add_fusion.pos, bf16[128,384]{1,0:T(8,128)(2,1)S(1)} %get-tuple-element.19.p0, bf16[128,384]{1,0:T(8,128)(2,1)S(1)} %collective-permute-done.p1, bf16[128,384]{1,0:T(8,128)(2,1)S(1)} %collective-permute-done.1.p2, bf16[128,384]{1,0:T(8,128)(2,1)S(1)} %collective-permute-done.2.p3, ...), custom_call_target="tpu_custom_call" | custom-call | tf_op jit(solution)/shard_map/low/pallas_call | solution.py:164
  25.9 1.3 collective-permute-start.6
  27.2 0.0 copy-done
  27.2 0.0 copy-start.1
  27.2 0.0 copy-start.2
  27.2 0.0 copy-start.3
  27.2 0.0 copy-start.4
  27.2 0.8 mids.1
  28.0 2.7 %collective-permute-done.6 = bf16[512,128]{1,0:T(8,128)(2,1)S(1)} collective-permute-done((bf16[512,128]{1,0:T(8,128)(2,1)S(1)}, bf16[512,128]{1,0:T(8,128)(2,1)S(1)}, u32[]{:S(2)}, u32[]{:S(2)}) %collective-permute-start.6) | collective-permute-done | bytes 131104 | tf_op jit(solution)/shard_map/ppermute | solution.py:392
  30.7 2.1 %collective-permute-start.9 = (bf16[512,128]{1,0:T(8,128)(2,1)S(1)}, bf16[512,128]{1,0:T(8,128)(2,1)S(1)}, u32[]{:S(2)}, u32[]{:S(2)}) collective-permute-start(bf16[512,128]{1,0:T(8,128)(2,1)S(1)} %add_convert_fusion.2), channel_id=1, source_target_pairs={{0,4},{1,5},{2,6},{3,7},{4,0},{5,1},{6,2},{7,3},{8,40},{9,41},{10,... | collective-permute-start | bytes 393224 | tf_op jit(solution)/shard_map/ppermute | solution.py:392
  32.8 2.3 %collective-permute-start.8 = (bf16[512,128]{1,0:T(8,128)(2,1)S(1)}, bf16[512,128]{1,0:T(8,128)(2,1)S(1)}, u32[]{:S(2)}, u32[]{:S(2)}) collective-permute-start(bf16[512,128]{1,0:T(8,128)(2,1)S(1)} %add_convert_fusion.2), channel_id=1, source_target_pairs={{0,6},{1,7},{2,4},{3,5},{4,2},{5,3},{6,0},{7,1},{8,56},{9,57},{10,... | collective-permute-start | bytes 393224 | tf_op jit(solution)/shard_map/ppermute | solution.py:392
  35.1 0.0 collective-permute-start.7
  35.1 1.0 collective-permute-done.9
  36.1 2.0 %collective-permute-done.8 = bf16[512,128]{1,0:T(8,128)(2,1)S(1)} collective-permute-done((bf16[512,128]{1,0:T(8,128)(2,1)S(1)}, bf16[512,128]{1,0:T(8,128)(2,1)S(1)}, u32[]{:S(2)}, u32[]{:S(2)}) %collective-permute-start.8) | collective-permute-done | bytes 131104 | tf_op jit(solution)/shard_map/ppermute | solution.py:392
  38.1 0.8 collective-permute-done.7
  38.9 0.1 add_convert_fusion.1
  39.0 3.3 %collective-permute-start.12 = (bf16[512,128]{1,0:T(8,128)(2,1)S(1)}, bf16[512,128]{1,0:T(8,128)(2,1)S(1)}, u32[]{:S(2)}, u32[]{:S(2)}) collective-permute-start(bf16[512,128]{1,0:T(8,128)(2,1)S(1)} %add_convert_fusion.1), channel_id=1, source_target_pairs={{0,32},{1,33},{2,34},{3,35},{4,36},{5,37},{6,38},{7,39},{8,12},{9,... | collective-permute-start | bytes 393224 | tf_op jit(solution)/shard_map/ppermute | solution.py:392
  42.2 0.8 collective-permute-start.11
  43.0 0.0 collective-permute-start.10
  43.0 1.6 collective-permute-done.12
  44.6 3.0 %collective-permute-done.11 = bf16[512,128]{1,0:T(8,128)(2,1)S(1)} collective-permute-done((bf16[512,128]{1,0:T(8,128)(2,1)S(1)}, bf16[512,128]{1,0:T(8,128)(2,1)S(1)}, u32[]{:S(2)}, u32[]{:S(2)}) %collective-permute-start.11) | collective-permute-done | bytes 131104 | tf_op jit(solution)/shard_map/ppermute | solution.py:392
  47.6 0.0 collective-permute-done.10
  47.6 0.1 add_convert_fusion.lat0
  47.6 2.6 %collective-permute-start.14 = (bf16[512,128]{1,0:T(8,128)(2,1)S(1)}, bf16[512,128]{1,0:T(8,128)(2,1)S(1)}, u32[]{:S(2)}, u32[]{:S(2)}) collective-permute-start(bf16[512,128]{1,0:T(8,128)(2,1)S(1)} %add_convert_fusion.lat0), channel_id=1, source_target_pairs={{0,65},{1,64},{2,67},{3,66},{4,69},{5,68},{6,71},{7,70},{8,73},{9,... | collective-permute-start | bytes 393224 | tf_op jit(solution)/shard_map/ppermute | solution.py:392
  50.2 4.0 %collective-permute-start.13 = (bf16[512,128]{1,0:T(8,128)(2,1)S(1)}, bf16[512,128]{1,0:T(8,128)(2,1)S(1)}, u32[]{:S(2)}, u32[]{:S(2)}) collective-permute-start(bf16[512,128]{1,0:T(8,128)(2,1)S(1)} %add_convert_fusion.lat0), channel_id=1, source_target_pairs={{0,8},{1,9},{2,10},{3,11},{4,12},{5,13},{6,14},{7,15},{8,0},{9,1},... | collective-permute-start | bytes 393224 | tf_op jit(solution)/shard_map/ppermute | solution.py:392
  54.2 0.0 collective-permute-done.14.lat2
  54.2 3.4 %collective-permute-start.15 = (bf16[512,128]{1,0:T(8,128)(2,1)S(1)}, bf16[512,128]{1,0:T(8,128)(2,1)S(1)}, u32[]{:S(2)}, u32[]{:S(2)}) collective-permute-start(bf16[512,128]{1,0:T(8,128)(2,1)S(1)} %collective-permute-done.14.lat2), channel_id=1, source_target_pairs={{0,8},{1,9},{2,10},{3,11},{4,12},{5,13},{6,14},{7,15},{8,0},{9,1},... | collective-permute-start | bytes 393224 | tf_op jit(solution)/shard_map/ppermute | solution.py:392
  57.7 0.0 collective-permute-done.13.lat1
  57.7 1.0 collective-permute-done.15.lat3
  58.6 0.0 copy-done.1
  58.6 0.0 copy-done.2
  58.6 0.0 copy-done.3
  58.6 0.0 copy-done.4
  58.7 109.6 %hi.1 = (bf16[512,512]{1,0:T(8,128)(2,1)}, bf16[64,128]{1,0:T(8,128)(2,1)}) custom-call(s32[4]{0:T(128)S(1)} %pad_add_fusion.pos, bf16[512,128]{1,0:T(8,128)(2,1)S(1)} %add_convert_fusion.lat0, bf16[512,128]{1,0:T(8,128)(2,1)S(1)} %collective-permute-done.13.lat1, bf16[512,128]{1,0:T(8,128)(2,1)S(1)} %collective-permute-done.14.lat2, ...), custom_call_target="tpu_custom_call" | custom-call | tf_op jit(solution)/shard_map/hi/pallas_call | solution.py:352
  (6 shorter events, 0.1 us)
Async XLA Ops:
  1.7 7.2 %collective-permute-start = (bf16[128,384]{1,0:T(8,128)(2,1)S(1)}, bf16[128,384]{1,0:T(8,128)(2,1)S(1)}, u32[]{:S(2)}, u32[]{:S(2)}) collective-permute-start(bf16[128,384]{1,0:T(8,128)(2,1)S(1)} %get-tuple-element.20), channel_id=1, source_target_pairs={{0,16},{8,24},{16,32},{24,40},{32,48},{40,56},{48,0},{56,8},{64,80... | collective-permute-start | bytes 294920 | tf_op jit(solution)/shard_map/ppermute | solution.py:447
  4.3 7.3 %collective-permute-start.1 = (bf16[128,384]{1,0:T(8,128)(2,1)S(1)}, bf16[128,384]{1,0:T(8,128)(2,1)S(1)}, u32[]{:S(2)}, u32[]{:S(2)}) collective-permute-start(bf16[128,384]{1,0:T(8,128)(2,1)S(1)} %get-tuple-element.21), channel_id=1, source_target_pairs={{0,32},{8,40},{16,48},{24,56},{32,0},{40,8},{48,16},{56,24},{64,96... | collective-permute-start | bytes 294920 | tf_op jit(solution)/shard_map/ppermute | solution.py:447
  7.6 4.0 %collective-permute-start.2 = (bf16[128,384]{1,0:T(8,128)(2,1)S(1)}, bf16[128,384]{1,0:T(8,128)(2,1)S(1)}, u32[]{:S(2)}, u32[]{:S(2)}) collective-permute-start(bf16[128,384]{1,0:T(8,128)(2,1)S(1)} %get-tuple-element.22), channel_id=1, source_target_pairs={{0,48},{8,56},{16,0},{24,8},{32,16},{40,24},{48,32},{56,40},{64,11... | collective-permute-start | bytes 294920 | tf_op jit(solution)/shard_map/ppermute | solution.py:447
  11.6 9.6 %collective-permute-start.4 = (bf16[512,256]{1,0:T(8,128)(2,1)S(1)}, bf16[512,256]{1,0:T(8,128)(2,1)S(1)}, u32[]{:S(2)}, u32[]{:S(2)}) collective-permute-start(bf16[512,256]{1,0:T(8,128)(2,1)S(1)} %pad_maximum_fusion.kv0), channel_id=1, source_target_pairs={{0,64},{1,65},{2,66},{3,67},{4,68},{5,69},{6,70},{7,71},{8,72},{9,... | collective-permute-start | bytes 786440 | tf_op jit(solution)/shard_map/ppermute | solution.py:392
  14.5 12.6 %copy-start = (bf16[3,3,3,128,512]{4,3,2,1,0:T(8,128)(2,1)S(1)}, bf16[3,3,3,128,512]{4,3,2,1,0:T(8,128)(2,1)}, u32[]{:S(2)}) copy-start(bf16[3,3,3,128,512]{4,3,2,1,0:T(8,128)(2,1)} %param.21) | copy-start | bytes 10616836
  19.0 3.4 %collective-permute-start.3 = (bf16[512,256]{1,0:T(8,128)(2,1)S(1)}, bf16[512,256]{1,0:T(8,128)(2,1)S(1)}, u32[]{:S(2)}, u32[]{:S(2)}) collective-permute-start(bf16[512,256]{1,0:T(8,128)(2,1)S(1)} %pad_maximum_fusion.kv0), channel_id=1, source_target_pairs={{0,8},{1,9},{2,10},{3,11},{4,12},{5,13},{6,14},{7,15},{8,0},{9,1},... | collective-permute-start | bytes 786440 | tf_op jit(solution)/shard_map/ppermute | solution.py:392
  21.2 1.9 %collective-permute-start.5 = (bf16[512,256]{1,0:T(8,128)(2,1)S(1)}, bf16[512,256]{1,0:T(8,128)(2,1)S(1)}, u32[]{:S(2)}, u32[]{:S(2)}) collective-permute-start(bf16[512,256]{1,0:T(8,128)(2,1)S(1)} %collective-permute-done.4.kv2), channel_id=1, source_target_pairs={{0,8},{1,9},{2,10},{3,11},{4,12},{5,13},{6,14},{7,15},{8,0},{9,1},... | collective-permute-start | bytes 786440 | tf_op jit(solution)/shard_map/ppermute | solution.py:392
  25.9 4.8 %collective-permute-start.6 = (bf16[512,128]{1,0:T(8,128)(2,1)S(1)}, bf16[512,128]{1,0:T(8,128)(2,1)S(1)}, u32[]{:S(2)}, u32[]{:S(2)}) collective-permute-start(bf16[512,128]{1,0:T(8,128)(2,1)S(1)} %low.1), channel_id=1, source_target_pairs={{0,1},{1,0},{2,3},{3,2},{4,5},{5,4},{6,7},{7,6},{8,9},{9,8},{10,11... | collective-permute-start | bytes 393224 | tf_op jit(solution)/shard_map/ppermute | solution.py:392
  27.2 31.5 %copy-start.1 = (bf16[128,4096]{1,0:T(8,128)(2,1)S(1)}, bf16[128,4096]{1,0:T(8,128)(2,1)}, u32[]{:S(2)}) copy-start(bf16[128,4096]{1,0:T(8,128)(2,1)} %wv.1) | copy-start | bytes 3145732
  27.2 31.5 %copy-start.2 = (bf16[512,512]{1,0:T(8,128)(2,1)S(1)}, bf16[512,512]{1,0:T(8,128)(2,1)}, u32[]{:S(2)}) copy-start(bf16[512,512]{1,0:T(8,128)(2,1)} %second.1) | copy-start | bytes 1572868
  27.2 31.5 %copy-start.3 = (f32[512]{0:T(512)S(1)}, f32[512]{0:T(512)}, u32[]{:S(2)}) copy-start(f32[512]{0:T(512)} %param.22) | copy-start | bytes 6148
  27.2 31.5 %copy-start.4 = (f32[512]{0:T(512)S(1)}, f32[512]{0:T(512)}, u32[]{:S(2)}) copy-start(f32[512]{0:T(512)} %param.24) | copy-start | bytes 6148
  30.7 5.4 %collective-permute-start.9 = (bf16[512,128]{1,0:T(8,128)(2,1)S(1)}, bf16[512,128]{1,0:T(8,128)(2,1)S(1)}, u32[]{:S(2)}, u32[]{:S(2)}) collective-permute-start(bf16[512,128]{1,0:T(8,128)(2,1)S(1)} %add_convert_fusion.2), channel_id=1, source_target_pairs={{0,4},{1,5},{2,6},{3,7},{4,0},{5,1},{6,2},{7,3},{8,40},{9,41},{10,... | collective-permute-start | bytes 393224 | tf_op jit(solution)/shard_map/ppermute | solution.py:392
  32.8 5.3 %collective-permute-start.8 = (bf16[512,128]{1,0:T(8,128)(2,1)S(1)}, bf16[512,128]{1,0:T(8,128)(2,1)S(1)}, u32[]{:S(2)}, u32[]{:S(2)}) collective-permute-start(bf16[512,128]{1,0:T(8,128)(2,1)S(1)} %add_convert_fusion.2), channel_id=1, source_target_pairs={{0,6},{1,7},{2,4},{3,5},{4,2},{5,3},{6,0},{7,1},{8,56},{9,57},{10,... | collective-permute-start | bytes 393224 | tf_op jit(solution)/shard_map/ppermute | solution.py:392
  35.1 3.8 %collective-permute-start.7 = (bf16[512,128]{1,0:T(8,128)(2,1)S(1)}, bf16[512,128]{1,0:T(8,128)(2,1)S(1)}, u32[]{:S(2)}, u32[]{:S(2)}) collective-permute-start(bf16[512,128]{1,0:T(8,128)(2,1)S(1)} %add_convert_fusion.2), channel_id=1, source_target_pairs={{0,2},{1,3},{2,0},{3,1},{4,6},{5,7},{6,4},{7,5},{8,24},{9,25},{10,... | collective-permute-start | bytes 393224 | tf_op jit(solution)/shard_map/ppermute | solution.py:392
  39.0 5.6 %collective-permute-start.12 = (bf16[512,128]{1,0:T(8,128)(2,1)S(1)}, bf16[512,128]{1,0:T(8,128)(2,1)S(1)}, u32[]{:S(2)}, u32[]{:S(2)}) collective-permute-start(bf16[512,128]{1,0:T(8,128)(2,1)S(1)} %add_convert_fusion.1), channel_id=1, source_target_pairs={{0,32},{1,33},{2,34},{3,35},{4,36},{5,37},{6,38},{7,39},{8,12},{9,... | collective-permute-start | bytes 393224 | tf_op jit(solution)/shard_map/ppermute | solution.py:392
  42.2 5.3 %collective-permute-start.11 = (bf16[512,128]{1,0:T(8,128)(2,1)S(1)}, bf16[512,128]{1,0:T(8,128)(2,1)S(1)}, u32[]{:S(2)}, u32[]{:S(2)}) collective-permute-start(bf16[512,128]{1,0:T(8,128)(2,1)S(1)} %add_convert_fusion.1), channel_id=1, source_target_pairs={{0,48},{1,49},{2,50},{3,51},{4,52},{5,53},{6,54},{7,55},{8,14},{9,... | collective-permute-start | bytes 393224 | tf_op jit(solution)/shard_map/ppermute | solution.py:392
  43.0 4.5 %collective-permute-start.10 = (bf16[512,128]{1,0:T(8,128)(2,1)S(1)}, bf16[512,128]{1,0:T(8,128)(2,1)S(1)}, u32[]{:S(2)}, u32[]{:S(2)}) collective-permute-start(bf16[512,128]{1,0:T(8,128)(2,1)S(1)} %add_convert_fusion.1), channel_id=1, source_target_pairs={{0,16},{1,17},{2,18},{3,19},{4,20},{5,21},{6,22},{7,23},{8,10},{9,... | collective-permute-start | bytes 393224 | tf_op jit(solution)/shard_map/ppermute | solution.py:392
  47.6 6.6 %collective-permute-start.14 = (bf16[512,128]{1,0:T(8,128)(2,1)S(1)}, bf16[512,128]{1,0:T(8,128)(2,1)S(1)}, u32[]{:S(2)}, u32[]{:S(2)}) collective-permute-start(bf16[512,128]{1,0:T(8,128)(2,1)S(1)} %add_convert_fusion.lat0), channel_id=1, source_target_pairs={{0,65},{1,64},{2,67},{3,66},{4,69},{5,68},{6,71},{7,70},{8,73},{9,... | collective-permute-start | bytes 393224 | tf_op jit(solution)/shard_map/ppermute | solution.py:392
  50.2 7.5 %collective-permute-start.13 = (bf16[512,128]{1,0:T(8,128)(2,1)S(1)}, bf16[512,128]{1,0:T(8,128)(2,1)S(1)}, u32[]{:S(2)}, u32[]{:S(2)}) collective-permute-start(bf16[512,128]{1,0:T(8,128)(2,1)S(1)} %add_convert_fusion.lat0), channel_id=1, source_target_pairs={{0,8},{1,9},{2,10},{3,11},{4,12},{5,13},{6,14},{7,15},{8,0},{9,1},... | collective-permute-start | bytes 393224 | tf_op jit(solution)/shard_map/ppermute | solution.py:392
  54.2 4.4 %collective-permute-start.15 = (bf16[512,128]{1,0:T(8,128)(2,1)S(1)}, bf16[512,128]{1,0:T(8,128)(2,1)S(1)}, u32[]{:S(2)}, u32[]{:S(2)}) collective-permute-start(bf16[512,128]{1,0:T(8,128)(2,1)S(1)} %collective-permute-done.14.lat2), channel_id=1, source_target_pairs={{0,8},{1,9},{2,10},{3,11},{4,12},{5,13},{6,14},{7,15},{8,0},{9,1},... | collective-permute-start | bytes 393224 | tf_op jit(solution)/shard_map/ppermute | solution.py:392

commit v7 on v4

--- a/solution.py
+++ b/solution.py
@@ -49,7 +49,7 @@
 def pack_kernel(q_ref, k_ref, v_ref, *outs):
     z = (lax.axis_index("seq") >> 1) & 3
     for shift, out in enumerate(outs):
-        head = (z + shift) & 3
+        head = z ^ shift
         columns = pl.ds(pl.multiple_of(head * HD, HD), HD)
         out[:, 0:HD] = q_ref[:, columns]
         out[:, HD : 2 * HD] = k_ref[:, columns]
@@ -139,7 +139,7 @@
 def low_kernel(pos, p0, p1, p2, p3, kv0, kv1, kv2, kv3, w2, hl, out, q_s, part_s):
     z = pos[1]
     for shift, piece in enumerate((p0, p1, p2, p3)):
-        q_s[lax.rem(z + 4 - shift, 4)] = piece[:, 0:HD]
+        q_s[lax.bitwise_xor(z, shift)] = piece[:, 0:HD]
     for half in range(2):
         q = q_s[2 * half : 2 * half + 2].reshape(2 * TOK, HD)
         blocks = (kv0, kv1, kv2, kv3)
@@ -284,7 +284,16 @@
 
     lax.fori_loop(0, KEYS // BLOCK, step, 0, unroll=2)
 
-    @pl.when(jnp.logical_not(jnp.min(acc_s[:, :, HD:]) > TINY))
+    def finish():
+        for head in range(4):
+            mixed = (acc_s[head, :, :HD] / acc_s[head, :, HD:]).astype(BF)
+            columns = slice(head * HD, (head + 1) * HD)
+            attn_out[:, columns] = dot(mixed, wv[:, columns]).astype(BF)
+
+    weakest = jnp.min(acc_s[:, :, HD:])
+    finish()
+
+    @pl.when(jnp.logical_not(weakest > TINY))
     def _():
         def careful_head(head, carry):
             acc_s[head] = jnp.zeros((4 * TOK, 2 * HD), F32)
@@ -303,11 +312,7 @@
             return lax.fori_loop(0, KEYS // 512, careful, carry)
 
         lax.fori_loop(0, 4, careful_head, 0)
-
-    for head in range(4):
-        mixed = (acc_s[head, :, :HD] / acc_s[head, :, HD:]).astype(BF)
-        columns = slice(head * HD, (head + 1) * HD)
-        attn_out[:, columns] = dot(mixed, wv[:, columns]).astype(BF)
+        finish()
 
 
 def hi_attention(pos, lats, conv_first, bias_first, conv_second, bias_second, gq, gk, m, value_weight):
@@ -343,8 +348,8 @@
     )(pos, *args)
 
 
-def z_shift(step):
-    return [(i, (i & 9) | ((((i >> 1) + step) & 3) << 1)) for i in range(16)]
+def z_swap(bits):
+    return [(i, i ^ (bits << 1)) for i in range(16)]
 
 
 def trade(value, partner):
@@ -407,7 +412,7 @@
     pos = jnp.stack([seq // 8, (seq // 2) % 4, seq % 2, head]).astype(jnp.int32)
     pieces = pack(query_low, key_low, value_low)
     pieces = [pieces[0]] + [
-        lax.ppermute(pieces[step], "seq", z_shift(step)) for step in (1, 2, 3)
+        lax.ppermute(pieces[step], "seq", z_swap(step)) for step in (1, 2, 3)
     ]
     w2, hl, m, gq, gk = prep(
         pos, out_weight, latent_weight, hidden_low, query_weight, key_weight, query_gain, key_gain

time: 169 us -> 169 us (level)
  waiting for transfers between devices: 17.3 us -> 20.8 us
  starting transfers between devices: 32 us -> 29.1 us
    ppermute x3, waiting for transfers between devices: 3.27 us -> 6.71 us  [local(): lax.ppermute(pieces[step], 'seq', z_swap(step))]
    ppermute x13, starting transfers between devices: 25.4 us -> 23.2 us  [trade(): return lax.ppermute(value, ('seq', 'head'), pairs)]
  transfers between devices with their start and end apart: 16 -> 16, of which waited for: 11 -> 9; matrix products, arithmetic and copies ran while one was open for 0% -> 0% of each run, Pallas kernels for 3% -> 3%
where the time goes in v7:
time: 169 us
  Pallas kernels  118 us (70%)
  starting transfers between devices  29.1 us (17%)
  waiting for transfers between devices  20.8 us (12%)
    pallas_call x1, Pallas kernels, hi_attention(): pl.pallas_call(hi_kernel, grid_spec=pltpu.PrefetchScalarGridSpec(num_scal...  110 us
    ppermute x13, starting transfers between devices, trade(): return lax.ppermute(value, ('seq', 'head'), pairs)  23.2 us
    ppermute x13, waiting for transfers between devices, trade(): return lax.ppermute(value, ('seq', 'head'), pairs)  14.1 us
    ppermute x3, waiting for transfers between devices, local(): lax.ppermute(pieces[step], 'seq', z_swap(step))  6.71 us
    ppermute x3, starting transfers between devices, local(): lax.ppermute(pieces[step], 'seq', z_swap(step))  5.85 us
    pallas_call x1, Pallas kernels, prep(): pl.pallas_call(prep_kernel, grid_spec=pltpu.PrefetchScalarGridSpec(num_sc...  4.46 us
  transfers between devices with their start and end apart: 16, of which 9 were waited for; matrix products, arithmetic and copies ran while one was open for 0% of the time, Pallas kernels for 3%

profile of v7, /device:TPU:1, one launch (start us, length us, event | category | flops | bytes accessed | tf_op | source)
XLA Modules:
  0.0 169.2 jit_solution(7570515603316864258)
XLA Ops:
  0.6 1.1 pack.1
  1.7 2.5 %collective-permute-start = (bf16[128,384]{1,0:T(8,128)(2,1)S(1)}, bf16[128,384]{1,0:T(8,128)(2,1)S(1)}, u32[]{:S(2)}, u32[]{:S(2)}) collective-permute-start(bf16[128,384]{1,0:T(8,128)(2,1)S(1)} %get-tuple-element.18), channel_id=1, source_target_pairs={{0,16},{8,24},{16,0},{24,8},{32,48},{40,56},{48,32},{56,40},{64,80... | collective-permute-start | bytes 294920 | tf_op jit(solution)/shard_map/ppermute | solution.py:415
  4.3 3.3 %collective-permute-start.1 = (bf16[128,384]{1,0:T(8,128)(2,1)S(1)}, bf16[128,384]{1,0:T(8,128)(2,1)S(1)}, u32[]{:S(2)}, u32[]{:S(2)}) collective-permute-start(bf16[128,384]{1,0:T(8,128)(2,1)S(1)} %get-tuple-element.19), channel_id=1, source_target_pairs={{0,32},{8,40},{16,48},{24,56},{32,0},{40,8},{48,16},{56,24},{64,96... | collective-permute-start | bytes 294920 | tf_op jit(solution)/shard_map/ppermute | solution.py:415
  7.6 0.0 collective-permute-start.2
  7.6 0.0 collective-permute-done.p1
  7.6 4.0 %collective-permute-done.1.p2 = bf16[128,384]{1,0:T(8,128)(2,1)S(1)} collective-permute-done((bf16[128,384]{1,0:T(8,128)(2,1)S(1)}, bf16[128,384]{1,0:T(8,128)(2,1)S(1)}, u32[]{:S(2)}, u32[]{:S(2)}) %collective-permute-start.1) | collective-permute-done | bytes 98336 | tf_op jit(solution)/shard_map/ppermute | solution.py:415
  11.6 2.7 %collective-permute-done.2.p3 = bf16[128,384]{1,0:T(8,128)(2,1)S(1)} collective-permute-done((bf16[128,384]{1,0:T(8,128)(2,1)S(1)}, bf16[128,384]{1,0:T(8,128)(2,1)S(1)}, u32[]{:S(2)}, u32[]{:S(2)}) %collective-permute-start.2) | collective-permute-done | bytes 98336 | tf_op jit(solution)/shard_map/ppermute | solution.py:415
  14.4 2.8 %collective-permute-start.4 = (bf16[512,256]{1,0:T(8,128)(2,1)S(1)}, bf16[512,256]{1,0:T(8,128)(2,1)S(1)}, u32[]{:S(2)}, u32[]{:S(2)}) collective-permute-start(bf16[512,256]{1,0:T(8,128)(2,1)S(1)} %pad_maximum_fusion.kv0), channel_id=1, source_target_pairs={{0,64},{1,65},{2,66},{3,67},{4,68},{5,69},{6,70},{7,71},{8,72},{9,... | collective-permute-start | bytes 786440 | tf_op jit(solution)/shard_map/ppermute | solution.py:363
  17.2 0.1 pad_add_fusion.pos
  17.3 0.0 copy-start
  17.3 0.0 copy-start.1
  17.3 0.0 copy-start.2
  17.3 0.0 copy-start.3
  17.3 0.0 copy-start.4
  17.3 4.5 %prep.1 = (bf16[128,256]{1,0:T(8,128)(2,1)S(1)}, f32[16,128]{1,0:T(8,128)S(1)}, bf16[4,128,256]{2,1,0:T(8,128)(2,1)S(1)}, bf16[128,256]{1,0:T(8,128)(2,1)S(1)}, bf16[128,256]{1,0:T(8,128)(2,1)S(1)}) custom-call(s32[4]{0:T(128)S(1)} %pad_add_fusion.pos, bf16[512,4096]{1,0:T(8,128)(2,1)} %ow.1, bf16[4096,128]{1,0:T(8,128)(2,1)} %lw.1, bf16[128,4096]{1,0:T(8,128)(2,1)} %hid.1, ...), custom_call_target="tpu_custom_call" | custom-call | flops 900000000 | bytes 5000000 | tf_op jit(solution)/shard_map/prep/pallas_call | solution.py:86
  21.8 1.3 collective-permute-start.3
  23.0 0.0 collective-permute-done.4.kv2
  23.0 1.6 collective-permute-start.5
  24.7 0.0 collective-permute-done.3.kv1
  24.7 1.2 collective-permute-done.5.kv3
  25.8 2.8 %low.1 = bf16[512,128]{1,0:T(8,128)(2,1)S(1)} custom-call(s32[4]{0:T(128)S(1)} %pad_add_fusion.pos, bf16[128,384]{1,0:T(8,128)(2,1)S(1)} %get-tuple-element.17.p0, bf16[128,384]{1,0:T(8,128)(2,1)S(1)} %collective-permute-done.p1, bf16[128,384]{1,0:T(8,128)(2,1)S(1)} %collective-permute-done.1.p2, bf16[128,384]{1,0:T(8,128)(2,1)S(1)} %collective-permute-done.2.p3, ...), custom_call_target="tpu_custom_call" | custom-call | tf_op jit(solution)/shard_map/low/pallas_call | solution.py:164
  28.6 1.3 collective-permute-start.6
  29.9 3.5 %collective-permute-done.6 = bf16[512,128]{1,0:T(8,128)(2,1)S(1)} collective-permute-done((bf16[512,128]{1,0:T(8,128)(2,1)S(1)}, bf16[512,128]{1,0:T(8,128)(2,1)S(1)}, u32[]{:S(2)}, u32[]{:S(2)}) %collective-permute-start.6) | collective-permute-done | bytes 131104 | tf_op jit(solution)/shard_map/ppermute | solution.py:363
  33.5 0.1 collective-permute-start.9
  33.5 0.9 collective-permute-start.8
  34.4 1.8 %collective-permute-start.7 = (bf16[512,128]{1,0:T(8,128)(2,1)S(1)}, bf16[512,128]{1,0:T(8,128)(2,1)S(1)}, u32[]{:S(2)}, u32[]{:S(2)}) collective-permute-start(bf16[512,128]{1,0:T(8,128)(2,1)S(1)} %add_convert_fusion.2), channel_id=1, source_target_pairs={{0,2},{1,3},{2,0},{3,1},{4,6},{5,7},{6,4},{7,5},{8,24},{9,25},{10,... | collective-permute-start | bytes 393224 | tf_op jit(solution)/shard_map/ppermute | solution.py:363
  36.2 2.8 %collective-permute-done.9 = bf16[512,128]{1,0:T(8,128)(2,1)S(1)} collective-permute-done((bf16[512,128]{1,0:T(8,128)(2,1)S(1)}, bf16[512,128]{1,0:T(8,128)(2,1)S(1)}, u32[]{:S(2)}, u32[]{:S(2)}) %collective-permute-start.9) | collective-permute-done | bytes 131104 | tf_op jit(solution)/shard_map/ppermute | solution.py:363
  39.0 1.4 collective-permute-done.8
  40.4 0.0 collective-permute-done.7
  40.4 0.1 add_convert_fusion.1
  40.4 2.8 %collective-permute-start.12 = (bf16[512,128]{1,0:T(8,128)(2,1)S(1)}, bf16[512,128]{1,0:T(8,128)(2,1)S(1)}, u32[]{:S(2)}, u32[]{:S(2)}) collective-permute-start(bf16[512,128]{1,0:T(8,128)(2,1)S(1)} %add_convert_fusion.1), channel_id=1, source_target_pairs={{0,32},{1,33},{2,34},{3,35},{4,36},{5,37},{6,38},{7,39},{8,12},{9,... | collective-permute-start | bytes 393224 | tf_op jit(solution)/shard_map/ppermute | solution.py:363
  43.3 0.8 collective-permute-start.11
  44.0 0.0 collective-permute-start.10
  44.0 2.2 %collective-permute-done.12 = bf16[512,128]{1,0:T(8,128)(2,1)S(1)} collective-permute-done((bf16[512,128]{1,0:T(8,128)(2,1)S(1)}, bf16[512,128]{1,0:T(8,128)(2,1)S(1)}, u32[]{:S(2)}, u32[]{:S(2)}) %collective-permute-start.12) | collective-permute-done | bytes 131104 | tf_op jit(solution)/shard_map/ppermute | solution.py:363
  46.3 2.0 %collective-permute-done.11 = bf16[512,128]{1,0:T(8,128)(2,1)S(1)} collective-permute-done((bf16[512,128]{1,0:T(8,128)(2,1)S(1)}, bf16[512,128]{1,0:T(8,128)(2,1)S(1)}, u32[]{:S(2)}, u32[]{:S(2)}) %collective-permute-start.11) | collective-permute-done | bytes 131104 | tf_op jit(solution)/shard_map/ppermute | solution.py:363
  48.3 0.0 collective-permute-done.10
  48.3 0.1 add_convert_fusion.lat0
  48.4 2.6 %collective-permute-start.14 = (bf16[512,128]{1,0:T(8,128)(2,1)S(1)}, bf16[512,128]{1,0:T(8,128)(2,1)S(1)}, u32[]{:S(2)}, u32[]{:S(2)}) collective-permute-start(bf16[512,128]{1,0:T(8,128)(2,1)S(1)} %add_convert_fusion.lat0), channel_id=1, source_target_pairs={{0,65},{1,64},{2,67},{3,66},{4,69},{5,68},{6,71},{7,70},{8,73},{9,... | collective-permute-start | bytes 393224 | tf_op jit(solution)/shard_map/ppermute | solution.py:363
  50.9 3.9 %collective-permute-start.13 = (bf16[512,128]{1,0:T(8,128)(2,1)S(1)}, bf16[512,128]{1,0:T(8,128)(2,1)S(1)}, u32[]{:S(2)}, u32[]{:S(2)}) collective-permute-start(bf16[512,128]{1,0:T(8,128)(2,1)S(1)} %add_convert_fusion.lat0), channel_id=1, source_target_pairs={{0,8},{1,9},{2,10},{3,11},{4,12},{5,13},{6,14},{7,15},{8,0},{9,1},... | collective-permute-start | bytes 393224 | tf_op jit(solution)/shard_map/ppermute | solution.py:363
  54.9 0.0 collective-permute-done.14.lat2
  54.9 3.4 %collective-permute-start.15 = (bf16[512,128]{1,0:T(8,128)(2,1)S(1)}, bf16[512,128]{1,0:T(8,128)(2,1)S(1)}, u32[]{:S(2)}, u32[]{:S(2)}) collective-permute-start(bf16[512,128]{1,0:T(8,128)(2,1)S(1)} %collective-permute-done.14.lat2), channel_id=1, source_target_pairs={{0,8},{1,9},{2,10},{3,11},{4,12},{5,13},{6,14},{7,15},{8,0},{9,1},... | collective-permute-start | bytes 393224 | tf_op jit(solution)/shard_map/ppermute | solution.py:363
  58.3 0.0 collective-permute-done.13.lat1
  58.3 1.0 collective-permute-done.15.lat3
  59.3 0.0 copy-done
  59.3 0.0 copy-done.1
  59.3 0.0 copy-done.2
  59.3 0.0 copy-done.3
  59.3 0.0 copy-done.4
  59.3 109.9 %hi.1 = (bf16[512,512]{1,0:T(8,128)(2,1)}, bf16[64,128]{1,0:T(8,128)(2,1)}) custom-call(s32[4]{0:T(128)S(1)} %pad_add_fusion.pos, bf16[512,128]{1,0:T(8,128)(2,1)S(1)} %add_convert_fusion.lat0, bf16[512,128]{1,0:T(8,128)(2,1)S(1)} %collective-permute-done.13.lat1, bf16[512,128]{1,0:T(8,128)(2,1)S(1)} %collective-permute-done.14.lat2, ...), custom_call_target="tpu_custom_call" | custom-call | tf_op jit(solution)/shard_map/hi/pallas_call | solution.py:324
  (6 shorter events, 0.1 us)
Async XLA Ops:
  1.7 5.9 %collective-permute-start = (bf16[128,384]{1,0:T(8,128)(2,1)S(1)}, bf16[128,384]{1,0:T(8,128)(2,1)S(1)}, u32[]{:S(2)}, u32[]{:S(2)}) collective-permute-start(bf16[128,384]{1,0:T(8,128)(2,1)S(1)} %get-tuple-element.18), channel_id=1, source_target_pairs={{0,16},{8,24},{16,0},{24,8},{32,48},{40,56},{48,32},{56,40},{64,80... | collective-permute-start | bytes 294920 | tf_op jit(solution)/shard_map/ppermute | solution.py:415
  4.3 7.3 %collective-permute-start.1 = (bf16[128,384]{1,0:T(8,128)(2,1)S(1)}, bf16[128,384]{1,0:T(8,128)(2,1)S(1)}, u32[]{:S(2)}, u32[]{:S(2)}) collective-permute-start(bf16[128,384]{1,0:T(8,128)(2,1)S(1)} %get-tuple-element.19), channel_id=1, source_target_pairs={{0,32},{8,40},{16,48},{24,56},{32,0},{40,8},{48,16},{56,24},{64,96... | collective-permute-start | bytes 294920 | tf_op jit(solution)/shard_map/ppermute | solution.py:415
  7.6 6.8 %collective-permute-start.2 = (bf16[128,384]{1,0:T(8,128)(2,1)S(1)}, bf16[128,384]{1,0:T(8,128)(2,1)S(1)}, u32[]{:S(2)}, u32[]{:S(2)}) collective-permute-start(bf16[128,384]{1,0:T(8,128)(2,1)S(1)} %get-tuple-element.20), channel_id=1, source_target_pairs={{0,48},{8,56},{16,32},{24,40},{32,16},{40,24},{48,0},{56,8},{64,11... | collective-permute-start | bytes 294920 | tf_op jit(solution)/shard_map/ppermute | solution.py:415
  14.4 8.7 %collective-permute-start.4 = (bf16[512,256]{1,0:T(8,128)(2,1)S(1)}, bf16[512,256]{1,0:T(8,128)(2,1)S(1)}, u32[]{:S(2)}, u32[]{:S(2)}) collective-permute-start(bf16[512,256]{1,0:T(8,128)(2,1)S(1)} %pad_maximum_fusion.kv0), channel_id=1, source_target_pairs={{0,64},{1,65},{2,66},{3,67},{4,68},{5,69},{6,70},{7,71},{8,72},{9,... | collective-permute-start | bytes 786440 | tf_op jit(solution)/shard_map/ppermute | solution.py:363
  17.3 42.0 %copy-start = (bf16[3,3,3,128,512]{4,3,2,1,0:T(8,128)(2,1)S(1)}, bf16[3,3,3,128,512]{4,3,2,1,0:T(8,128)(2,1)}, u32[]{:S(2)}) copy-start(bf16[3,3,3,128,512]{4,3,2,1,0:T(8,128)(2,1)} %param.21) | copy-start | bytes 10616836
  17.3 42.0 %copy-start.1 = (bf16[128,4096]{1,0:T(8,128)(2,1)S(1)}, bf16[128,4096]{1,0:T(8,128)(2,1)}, u32[]{:S(2)}) copy-start(bf16[128,4096]{1,0:T(8,128)(2,1)} %wv.1) | copy-start | bytes 3145732
  17.3 42.0 %copy-start.2 = (bf16[512,512]{1,0:T(8,128)(2,1)S(1)}, bf16[512,512]{1,0:T(8,128)(2,1)}, u32[]{:S(2)}) copy-start(bf16[512,512]{1,0:T(8,128)(2,1)} %second.1) | copy-start | bytes 1572868
  17.3 42.0 %copy-start.3 = (f32[512]{0:T(512)S(1)}, f32[512]{0:T(512)}, u32[]{:S(2)}) copy-start(f32[512]{0:T(512)} %param.22) | copy-start | bytes 6148
  17.3 42.0 %copy-start.4 = (f32[512]{0:T(512)S(1)}, f32[512]{0:T(512)}, u32[]{:S(2)}) copy-start(f32[512]{0:T(512)} %param.24) | copy-start | bytes 6148
  21.8 2.9 %collective-permute-start.3 = (bf16[512,256]{1,0:T(8,128)(2,1)S(1)}, bf16[512,256]{1,0:T(8,128)(2,1)S(1)}, u32[]{:S(2)}, u32[]{:S(2)}) collective-permute-start(bf16[512,256]{1,0:T(8,128)(2,1)S(1)} %pad_maximum_fusion.kv0), channel_id=1, source_target_pairs={{0,8},{1,9},{2,10},{3,11},{4,12},{5,13},{6,14},{7,15},{8,0},{9,1},... | collective-permute-start | bytes 786440 | tf_op jit(solution)/shard_map/ppermute | solution.py:363
  23.0 2.8 %collective-permute-start.5 = (bf16[512,256]{1,0:T(8,128)(2,1)S(1)}, bf16[512,256]{1,0:T(8,128)(2,1)S(1)}, u32[]{:S(2)}, u32[]{:S(2)}) collective-permute-start(bf16[512,256]{1,0:T(8,128)(2,1)S(1)} %collective-permute-done.4.kv2), channel_id=1, source_target_pairs={{0,8},{1,9},{2,10},{3,11},{4,12},{5,13},{6,14},{7,15},{8,0},{9,1},... | collective-permute-start | bytes 786440 | tf_op jit(solution)/shard_map/ppermute | solution.py:363
  28.6 4.8 %collective-permute-start.6 = (bf16[512,128]{1,0:T(8,128)(2,1)S(1)}, bf16[512,128]{1,0:T(8,128)(2,1)S(1)}, u32[]{:S(2)}, u32[]{:S(2)}) collective-permute-start(bf16[512,128]{1,0:T(8,128)(2,1)S(1)} %low.1), channel_id=1, source_target_pairs={{0,1},{1,0},{2,3},{3,2},{4,5},{5,4},{6,7},{7,6},{8,9},{9,8},{10,11... | collective-permute-start | bytes 393224 | tf_op jit(solution)/shard_map/ppermute | solution.py:363
  33.5 5.5 %collective-permute-start.9 = (bf16[512,128]{1,0:T(8,128)(2,1)S(1)}, bf16[512,128]{1,0:T(8,128)(2,1)S(1)}, u32[]{:S(2)}, u32[]{:S(2)}) collective-permute-start(bf16[512,128]{1,0:T(8,128)(2,1)S(1)} %add_convert_fusion.2), channel_id=1, source_target_pairs={{0,4},{1,5},{2,6},{3,7},{4,0},{5,1},{6,2},{7,3},{8,40},{9,41},{10,... | collective-permute-start | bytes 393224 | tf_op jit(solution)/shard_map/ppermute | solution.py:363
  33.5 6.8 %collective-permute-start.8 = (bf16[512,128]{1,0:T(8,128)(2,1)S(1)}, bf16[512,128]{1,0:T(8,128)(2,1)S(1)}, u32[]{:S(2)}, u32[]{:S(2)}) collective-permute-start(bf16[512,128]{1,0:T(8,128)(2,1)S(1)} %add_convert_fusion.2), channel_id=1, source_target_pairs={{0,6},{1,7},{2,4},{3,5},{4,2},{5,3},{6,0},{7,1},{8,56},{9,57},{10,... | collective-permute-start | bytes 393224 | tf_op jit(solution)/shard_map/ppermute | solution.py:363
  34.4 6.0 %collective-permute-start.7 = (bf16[512,128]{1,0:T(8,128)(2,1)S(1)}, bf16[512,128]{1,0:T(8,128)(2,1)S(1)}, u32[]{:S(2)}, u32[]{:S(2)}) collective-permute-start(bf16[512,128]{1,0:T(8,128)(2,1)S(1)} %add_convert_fusion.2), channel_id=1, source_target_pairs={{0,2},{1,3},{2,0},{3,1},{4,6},{5,7},{6,4},{7,5},{8,24},{9,25},{10,... | collective-permute-start | bytes 393224 | tf_op jit(solution)/shard_map/ppermute | solution.py:363
  40.4 5.9 %collective-permute-start.12 = (bf16[512,128]{1,0:T(8,128)(2,1)S(1)}, bf16[512,128]{1,0:T(8,128)(2,1)S(1)}, u32[]{:S(2)}, u32[]{:S(2)}) collective-permute-start(bf16[512,128]{1,0:T(8,128)(2,1)S(1)} %add_convert_fusion.1), channel_id=1, source_target_pairs={{0,32},{1,33},{2,34},{3,35},{4,36},{5,37},{6,38},{7,39},{8,12},{9,... | collective-permute-start | bytes 393224 | tf_op jit(solution)/shard_map/ppermute | solution.py:363
  43.3 5.0 %collective-permute-start.11 = (bf16[512,128]{1,0:T(8,128)(2,1)S(1)}, bf16[512,128]{1,0:T(8,128)(2,1)S(1)}, u32[]{:S(2)}, u32[]{:S(2)}) collective-permute-start(bf16[512,128]{1,0:T(8,128)(2,1)S(1)} %add_convert_fusion.1), channel_id=1, source_target_pairs={{0,48},{1,49},{2,50},{3,51},{4,52},{5,53},{6,54},{7,55},{8,14},{9,... | collective-permute-start | bytes 393224 | tf_op jit(solution)/shard_map/ppermute | solution.py:363
  44.0 4.3 %collective-permute-start.10 = (bf16[512,128]{1,0:T(8,128)(2,1)S(1)}, bf16[512,128]{1,0:T(8,128)(2,1)S(1)}, u32[]{:S(2)}, u32[]{:S(2)}) collective-permute-start(bf16[512,128]{1,0:T(8,128)(2,1)S(1)} %add_convert_fusion.1), channel_id=1, source_target_pairs={{0,16},{1,17},{2,18},{3,19},{4,20},{5,21},{6,22},{7,23},{8,10},{9,... | collective-permute-start | bytes 393224 | tf_op jit(solution)/shard_map/ppermute | solution.py:363
  48.4 6.5 %collective-permute-start.14 = (bf16[512,128]{1,0:T(8,128)(2,1)S(1)}, bf16[512,128]{1,0:T(8,128)(2,1)S(1)}, u32[]{:S(2)}, u32[]{:S(2)}) collective-permute-start(bf16[512,128]{1,0:T(8,128)(2,1)S(1)} %add_convert_fusion.lat0), channel_id=1, source_target_pairs={{0,65},{1,64},{2,67},{3,66},{4,69},{5,68},{6,71},{7,70},{8,73},{9,... | collective-permute-start | bytes 393224 | tf_op jit(solution)/shard_map/ppermute | solution.py:363
  50.9 7.3 %collective-permute-start.13 = (bf16[512,128]{1,0:T(8,128)(2,1)S(1)}, bf16[512,128]{1,0:T(8,128)(2,1)S(1)}, u32[]{:S(2)}, u32[]{:S(2)}) collective-permute-start(bf16[512,128]{1,0:T(8,128)(2,1)S(1)} %add_convert_fusion.lat0), channel_id=1, source_target_pairs={{0,8},{1,9},{2,10},{3,11},{4,12},{5,13},{6,14},{7,15},{8,0},{9,1},... | collective-permute-start | bytes 393224 | tf_op jit(solution)/shard_map/ppermute | solution.py:363
  54.9 4.4 %collective-permute-start.15 = (bf16[512,128]{1,0:T(8,128)(2,1)S(1)}, bf16[512,128]{1,0:T(8,128)(2,1)S(1)}, u32[]{:S(2)}, u32[]{:S(2)}) collective-permute-start(bf16[512,128]{1,0:T(8,128)(2,1)S(1)} %collective-permute-done.14.lat2), channel_id=1, source_target_pairs={{0,8},{1,9},{2,10},{3,11},{4,12},{5,13},{6,14},{7,15},{8,0},{9,1},... | collective-permute-start | bytes 393224 | tf_op jit(solution)/shard_map/ppermute | solution.py:363

commit v8 on v7

--- a/solution.py
+++ b/solution.py
@@ -49,7 +49,7 @@
 def pack_kernel(q_ref, k_ref, v_ref, *outs):
     z = (lax.axis_index("seq") >> 1) & 3
     for shift, out in enumerate(outs):
-        head = z ^ shift
+        head = (z + shift) & 3
         columns = pl.ds(pl.multiple_of(head * HD, HD), HD)
         out[:, 0:HD] = q_ref[:, columns]
         out[:, HD : 2 * HD] = k_ref[:, columns]
@@ -139,7 +139,7 @@
 def low_kernel(pos, p0, p1, p2, p3, kv0, kv1, kv2, kv3, w2, hl, out, q_s, part_s):
     z = pos[1]
     for shift, piece in enumerate((p0, p1, p2, p3)):
-        q_s[lax.bitwise_xor(z, shift)] = piece[:, 0:HD]
+        q_s[lax.rem(z + 4 - shift, 4)] = piece[:, 0:HD]
     for half in range(2):
         q = q_s[2 * half : 2 * half + 2].reshape(2 * TOK, HD)
         blocks = (kv0, kv1, kv2, kv3)
@@ -348,8 +348,8 @@
     )(pos, *args)
 
 
-def z_swap(bits):
-    return [(i, i ^ (bits << 1)) for i in range(16)]
+def z_shift(step):
+    return [(i, (i & 9) | ((((i >> 1) + step) & 3) << 1)) for i in range(16)]
 
 
 def trade(value, partner):
@@ -412,7 +412,7 @@
     pos = jnp.stack([seq // 8, (seq // 2) % 4, seq % 2, head]).astype(jnp.int32)
     pieces = pack(query_low, key_low, value_low)
     pieces = [pieces[0]] + [
-        lax.ppermute(pieces[step], "seq", z_swap(step)) for step in (1, 2, 3)
+        lax.ppermute(pieces[step], "seq", z_shift(step)) for step in (1, 2, 3)
     ]
     w2, hl, m, gq, gk = prep(
         pos, out_weight, latent_weight, hidden_low, query_weight, key_weight, query_gain, key_gain

time: 169 us -> 169 us (level)
  waiting for transfers between devices: 20.8 us -> 17.3 us
  starting transfers between devices: 29.1 us -> 32 us
    ppermute x3, waiting for transfers between devices: 6.71 us -> 3.27 us  [local(): lax.ppermute(pieces[step], 'seq', z_shift(step))]
    ppermute x13, starting transfers between devices: 23.2 us -> 25.4 us  [trade(): return lax.ppermute(value, ('seq', 'head'), pairs)]
  transfers between devices with their start and end apart: 16 -> 16, of which waited for: 9 -> 11; matrix products, arithmetic and copies ran while one was open for 0% -> 0% of each run, Pallas kernels for 3% -> 3%
where the time goes in v8:
time: 169 us
  Pallas kernels  118 us (70%)
  starting transfers between devices  32 us (19%)
  waiting for transfers between devices  17.3 us (10%)
    pallas_call x1, Pallas kernels, hi_attention(): pl.pallas_call(hi_kernel, grid_spec=pltpu.PrefetchScalarGridSpec(num_scal...  110 us
    ppermute x13, starting transfers between devices, trade(): return lax.ppermute(value, ('seq', 'head'), pairs)  25.4 us
    ppermute x13, waiting for transfers between devices, trade(): return lax.ppermute(value, ('seq', 'head'), pairs)  14 us
    ppermute x3, starting transfers between devices, local(): lax.ppermute(pieces[step], 'seq', z_shift(step))  6.57 us
    pallas_call x1, Pallas kernels, prep(): pl.pallas_call(prep_kernel, grid_spec=pltpu.PrefetchScalarGridSpec(num_sc...  4.47 us
  transfers between devices with their start and end apart: 16, of which 11 were waited for; matrix products, arithmetic and copies ran while one was open for 0% of the time, Pallas kernels for 3%

profile of v8, /device:TPU:1, one launch (start us, length us, event | category | flops | bytes accessed | tf_op | source)
XLA Modules:
  0.0 168.5 jit_solution(12271134377022110625)
XLA Ops:
  0.6 1.1 pack.1
  1.7 2.5 %collective-permute-start = (bf16[128,384]{1,0:T(8,128)(2,1)S(1)}, bf16[128,384]{1,0:T(8,128)(2,1)S(1)}, u32[]{:S(2)}, u32[]{:S(2)}) collective-permute-start(bf16[128,384]{1,0:T(8,128)(2,1)S(1)} %get-tuple-element.18), channel_id=1, source_target_pairs={{0,16},{8,24},{16,32},{24,40},{32,48},{40,56},{48,0},{56,8},{64,80... | collective-permute-start | bytes 294920 | tf_op jit(solution)/shard_map/ppermute | solution.py:415
  4.3 3.3 %collective-permute-start.1 = (bf16[128,384]{1,0:T(8,128)(2,1)S(1)}, bf16[128,384]{1,0:T(8,128)(2,1)S(1)}, u32[]{:S(2)}, u32[]{:S(2)}) collective-permute-start(bf16[128,384]{1,0:T(8,128)(2,1)S(1)} %get-tuple-element.19), channel_id=1, source_target_pairs={{0,32},{8,40},{16,48},{24,56},{32,0},{40,8},{48,16},{56,24},{64,96... | collective-permute-start | bytes 294920 | tf_op jit(solution)/shard_map/ppermute | solution.py:415
  7.6 0.7 collective-permute-start.2
  8.3 0.6 collective-permute-done.p1
  8.9 2.7 %collective-permute-done.1.p2 = bf16[128,384]{1,0:T(8,128)(2,1)S(1)} collective-permute-done((bf16[128,384]{1,0:T(8,128)(2,1)S(1)}, bf16[128,384]{1,0:T(8,128)(2,1)S(1)}, u32[]{:S(2)}, u32[]{:S(2)}) %collective-permute-start.1) | collective-permute-done | bytes 98336 | tf_op jit(solution)/shard_map/ppermute | solution.py:415
  11.6 0.0 collective-permute-done.2.p3
  11.6 2.8 %collective-permute-start.4 = (bf16[512,256]{1,0:T(8,128)(2,1)S(1)}, bf16[512,256]{1,0:T(8,128)(2,1)S(1)}, u32[]{:S(2)}, u32[]{:S(2)}) collective-permute-start(bf16[512,256]{1,0:T(8,128)(2,1)S(1)} %pad_maximum_fusion.kv0), channel_id=1, source_target_pairs={{0,64},{1,65},{2,66},{3,67},{4,68},{5,69},{6,70},{7,71},{8,72},{9,... | collective-permute-start | bytes 786440 | tf_op jit(solution)/shard_map/ppermute | solution.py:363
  14.5 0.1 pad_add_fusion.pos
  14.5 0.0 copy-start
  14.5 0.0 copy-start.1
  14.5 0.0 copy-start.2
  14.5 0.0 copy-start.3
  14.6 0.0 copy-start.4
  14.6 4.5 %prep.1 = (bf16[128,256]{1,0:T(8,128)(2,1)S(1)}, f32[16,128]{1,0:T(8,128)S(1)}, bf16[4,128,256]{2,1,0:T(8,128)(2,1)S(1)}, bf16[128,256]{1,0:T(8,128)(2,1)S(1)}, bf16[128,256]{1,0:T(8,128)(2,1)S(1)}) custom-call(s32[4]{0:T(128)S(1)} %pad_add_fusion.pos, bf16[512,4096]{1,0:T(8,128)(2,1)} %ow.1, bf16[4096,128]{1,0:T(8,128)(2,1)} %lw.1, bf16[128,4096]{1,0:T(8,128)(2,1)} %hid.1, ...), custom_call_target="tpu_custom_call" | custom-call | flops 900000000 | bytes 5000000 | tf_op jit(solution)/shard_map/prep/pallas_call | solution.py:86
  19.0 2.2 %collective-permute-start.3 = (bf16[512,256]{1,0:T(8,128)(2,1)S(1)}, bf16[512,256]{1,0:T(8,128)(2,1)S(1)}, u32[]{:S(2)}, u32[]{:S(2)}) collective-permute-start(bf16[512,256]{1,0:T(8,128)(2,1)S(1)} %pad_maximum_fusion.kv0), channel_id=1, source_target_pairs={{0,8},{1,9},{2,10},{3,11},{4,12},{5,13},{6,14},{7,15},{8,0},{9,1},... | collective-permute-start | bytes 786440 | tf_op jit(solution)/shard_map/ppermute | solution.py:363
  21.2 0.0 collective-permute-done.4.kv2
  21.2 0.7 collective-permute-start.5
  21.9 0.5 collective-permute-done.3.kv1
  22.4 0.7 collective-permute-done.5.kv3
  23.1 2.8 %low.1 = bf16[512,128]{1,0:T(8,128)(2,1)S(1)} custom-call(s32[4]{0:T(128)S(1)} %pad_add_fusion.pos, bf16[128,384]{1,0:T(8,128)(2,1)S(1)} %get-tuple-element.17.p0, bf16[128,384]{1,0:T(8,128)(2,1)S(1)} %collective-permute-done.p1, bf16[128,384]{1,0:T(8,128)(2,1)S(1)} %collective-permute-done.1.p2, bf16[128,384]{1,0:T(8,128)(2,1)S(1)} %collective-permute-done.2.p3, ...), custom_call_target="tpu_custom_call" | custom-call | tf_op jit(solution)/shard_map/low/pallas_call | solution.py:164
  25.9 1.3 collective-permute-start.6
  27.2 3.5 %collective-permute-done.6 = bf16[512,128]{1,0:T(8,128)(2,1)S(1)} collective-permute-done((bf16[512,128]{1,0:T(8,128)(2,1)S(1)}, bf16[512,128]{1,0:T(8,128)(2,1)S(1)}, u32[]{:S(2)}, u32[]{:S(2)}) %collective-permute-start.6) | collective-permute-done | bytes 131104 | tf_op jit(solution)/shard_map/ppermute | solution.py:363
  30.7 2.1 %collective-permute-start.9 = (bf16[512,128]{1,0:T(8,128)(2,1)S(1)}, bf16[512,128]{1,0:T(8,128)(2,1)S(1)}, u32[]{:S(2)}, u32[]{:S(2)}) collective-permute-start(bf16[512,128]{1,0:T(8,128)(2,1)S(1)} %add_convert_fusion.2), channel_id=1, source_target_pairs={{0,4},{1,5},{2,6},{3,7},{4,0},{5,1},{6,2},{7,3},{8,40},{9,41},{10,... | collective-permute-start | bytes 393224 | tf_op jit(solution)/shard_map/ppermute | solution.py:363
  32.8 2.3 %collective-permute-start.8 = (bf16[512,128]{1,0:T(8,128)(2,1)S(1)}, bf16[512,128]{1,0:T(8,128)(2,1)S(1)}, u32[]{:S(2)}, u32[]{:S(2)}) collective-permute-start(bf16[512,128]{1,0:T(8,128)(2,1)S(1)} %add_convert_fusion.2), channel_id=1, source_target_pairs={{0,6},{1,7},{2,4},{3,5},{4,2},{5,3},{6,0},{7,1},{8,56},{9,57},{10,... | collective-permute-start | bytes 393224 | tf_op jit(solution)/shard_map/ppermute | solution.py:363
  35.1 0.0 collective-permute-start.7
  35.1 1.0 collective-permute-done.9
  36.1 2.0 %collective-permute-done.8 = bf16[512,128]{1,0:T(8,128)(2,1)S(1)} collective-permute-done((bf16[512,128]{1,0:T(8,128)(2,1)S(1)}, bf16[512,128]{1,0:T(8,128)(2,1)S(1)}, u32[]{:S(2)}, u32[]{:S(2)}) %collective-permute-start.8) | collective-permute-done | bytes 131104 | tf_op jit(solution)/shard_map/ppermute | solution.py:363
  38.1 0.8 collective-permute-done.7
  38.9 0.1 add_convert_fusion.1
  39.0 3.3 %collective-permute-start.12 = (bf16[512,128]{1,0:T(8,128)(2,1)S(1)}, bf16[512,128]{1,0:T(8,128)(2,1)S(1)}, u32[]{:S(2)}, u32[]{:S(2)}) collective-permute-start(bf16[512,128]{1,0:T(8,128)(2,1)S(1)} %add_convert_fusion.1), channel_id=1, source_target_pairs={{0,32},{1,33},{2,34},{3,35},{4,36},{5,37},{6,38},{7,39},{8,12},{9,... | collective-permute-start | bytes 393224 | tf_op jit(solution)/shard_map/ppermute | solution.py:363
  42.2 0.8 collective-permute-start.11
  43.0 0.0 collective-permute-start.10
  43.0 1.6 collective-permute-done.12
  44.6 3.0 %collective-permute-done.11 = bf16[512,128]{1,0:T(8,128)(2,1)S(1)} collective-permute-done((bf16[512,128]{1,0:T(8,128)(2,1)S(1)}, bf16[512,128]{1,0:T(8,128)(2,1)S(1)}, u32[]{:S(2)}, u32[]{:S(2)}) %collective-permute-start.11) | collective-permute-done | bytes 131104 | tf_op jit(solution)/shard_map/ppermute | solution.py:363
  47.6 0.0 collective-permute-done.10
  47.6 0.1 add_convert_fusion.lat0
  47.6 2.6 %collective-permute-start.14 = (bf16[512,128]{1,0:T(8,128)(2,1)S(1)}, bf16[512,128]{1,0:T(8,128)(2,1)S(1)}, u32[]{:S(2)}, u32[]{:S(2)}) collective-permute-start(bf16[512,128]{1,0:T(8,128)(2,1)S(1)} %add_convert_fusion.lat0), channel_id=1, source_target_pairs={{0,65},{1,64},{2,67},{3,66},{4,69},{5,68},{6,71},{7,70},{8,73},{9,... | collective-permute-start | bytes 393224 | tf_op jit(solution)/shard_map/ppermute | solution.py:363
  50.2 4.0 %collective-permute-start.13 = (bf16[512,128]{1,0:T(8,128)(2,1)S(1)}, bf16[512,128]{1,0:T(8,128)(2,1)S(1)}, u32[]{:S(2)}, u32[]{:S(2)}) collective-permute-start(bf16[512,128]{1,0:T(8,128)(2,1)S(1)} %add_convert_fusion.lat0), channel_id=1, source_target_pairs={{0,8},{1,9},{2,10},{3,11},{4,12},{5,13},{6,14},{7,15},{8,0},{9,1},... | collective-permute-start | bytes 393224 | tf_op jit(solution)/shard_map/ppermute | solution.py:363
  54.2 0.0 collective-permute-done.14.lat2
  54.2 3.4 %collective-permute-start.15 = (bf16[512,128]{1,0:T(8,128)(2,1)S(1)}, bf16[512,128]{1,0:T(8,128)(2,1)S(1)}, u32[]{:S(2)}, u32[]{:S(2)}) collective-permute-start(bf16[512,128]{1,0:T(8,128)(2,1)S(1)} %collective-permute-done.14.lat2), channel_id=1, source_target_pairs={{0,8},{1,9},{2,10},{3,11},{4,12},{5,13},{6,14},{7,15},{8,0},{9,1},... | collective-permute-start | bytes 393224 | tf_op jit(solution)/shard_map/ppermute | solution.py:363
  57.7 0.0 collective-permute-done.13.lat1
  57.7 1.0 collective-permute-done.15.lat3
  58.6 0.0 copy-done
  58.6 0.0 copy-done.1
  58.6 0.0 copy-done.2
  58.6 0.0 copy-done.3
  58.7 0.0 copy-done.4
  58.7 109.9 %hi.1 = (bf16[512,512]{1,0:T(8,128)(2,1)}, bf16[64,128]{1,0:T(8,128)(2,1)}) custom-call(s32[4]{0:T(128)S(1)} %pad_add_fusion.pos, bf16[512,128]{1,0:T(8,128)(2,1)S(1)} %add_convert_fusion.lat0, bf16[512,128]{1,0:T(8,128)(2,1)S(1)} %collective-permute-done.13.lat1, bf16[512,128]{1,0:T(8,128)(2,1)S(1)} %collective-permute-done.14.lat2, ...), custom_call_target="tpu_custom_call" | custom-call | tf_op jit(solution)/shard_map/hi/pallas_call | solution.py:324
  (6 shorter events, 0.1 us)
Async XLA Ops:
  1.7 7.2 %collective-permute-start = (bf16[128,384]{1,0:T(8,128)(2,1)S(1)}, bf16[128,384]{1,0:T(8,128)(2,1)S(1)}, u32[]{:S(2)}, u32[]{:S(2)}) collective-permute-start(bf16[128,384]{1,0:T(8,128)(2,1)S(1)} %get-tuple-element.18), channel_id=1, source_target_pairs={{0,16},{8,24},{16,32},{24,40},{32,48},{40,56},{48,0},{56,8},{64,80... | collective-permute-start | bytes 294920 | tf_op jit(solution)/shard_map/ppermute | solution.py:415
  4.3 7.3 %collective-permute-start.1 = (bf16[128,384]{1,0:T(8,128)(2,1)S(1)}, bf16[128,384]{1,0:T(8,128)(2,1)S(1)}, u32[]{:S(2)}, u32[]{:S(2)}) collective-permute-start(bf16[128,384]{1,0:T(8,128)(2,1)S(1)} %get-tuple-element.19), channel_id=1, source_target_pairs={{0,32},{8,40},{16,48},{24,56},{32,0},{40,8},{48,16},{56,24},{64,96... | collective-permute-start | bytes 294920 | tf_op jit(solution)/shard_map/ppermute | solution.py:415
  7.6 4.0 %collective-permute-start.2 = (bf16[128,384]{1,0:T(8,128)(2,1)S(1)}, bf16[128,384]{1,0:T(8,128)(2,1)S(1)}, u32[]{:S(2)}, u32[]{:S(2)}) collective-permute-start(bf16[128,384]{1,0:T(8,128)(2,1)S(1)} %get-tuple-element.20), channel_id=1, source_target_pairs={{0,48},{8,56},{16,0},{24,8},{32,16},{40,24},{48,32},{56,40},{64,11... | collective-permute-start | bytes 294920 | tf_op jit(solution)/shard_map/ppermute | solution.py:415
  11.6 9.6 %collective-permute-start.4 = (bf16[512,256]{1,0:T(8,128)(2,1)S(1)}, bf16[512,256]{1,0:T(8,128)(2,1)S(1)}, u32[]{:S(2)}, u32[]{:S(2)}) collective-permute-start(bf16[512,256]{1,0:T(8,128)(2,1)S(1)} %pad_maximum_fusion.kv0), channel_id=1, source_target_pairs={{0,64},{1,65},{2,66},{3,67},{4,68},{5,69},{6,70},{7,71},{8,72},{9,... | collective-permute-start | bytes 786440 | tf_op jit(solution)/shard_map/ppermute | solution.py:363
  14.5 44.1 %copy-start = (bf16[3,3,3,128,512]{4,3,2,1,0:T(8,128)(2,1)S(1)}, bf16[3,3,3,128,512]{4,3,2,1,0:T(8,128)(2,1)}, u32[]{:S(2)}) copy-start(bf16[3,3,3,128,512]{4,3,2,1,0:T(8,128)(2,1)} %param.21) | copy-start | bytes 10616836
  14.5 44.1 %copy-start.1 = (bf16[128,4096]{1,0:T(8,128)(2,1)S(1)}, bf16[128,4096]{1,0:T(8,128)(2,1)}, u32[]{:S(2)}) copy-start(bf16[128,4096]{1,0:T(8,128)(2,1)} %wv.1) | copy-start | bytes 3145732
  14.5 44.1 %copy-start.2 = (bf16[512,512]{1,0:T(8,128)(2,1)S(1)}, bf16[512,512]{1,0:T(8,128)(2,1)}, u32[]{:S(2)}) copy-start(bf16[512,512]{1,0:T(8,128)(2,1)} %second.1) | copy-start | bytes 1572868
  14.5 44.1 %copy-start.3 = (f32[512]{0:T(512)S(1)}, f32[512]{0:T(512)}, u32[]{:S(2)}) copy-start(f32[512]{0:T(512)} %param.22) | copy-start | bytes 6148
  14.6 44.1 %copy-start.4 = (f32[512]{0:T(512)S(1)}, f32[512]{0:T(512)}, u32[]{:S(2)}) copy-start(f32[512]{0:T(512)} %param.24) | copy-start | bytes 6148
  19.0 3.4 %collective-permute-start.3 = (bf16[512,256]{1,0:T(8,128)(2,1)S(1)}, bf16[512,256]{1,0:T(8,128)(2,1)S(1)}, u32[]{:S(2)}, u32[]{:S(2)}) collective-permute-start(bf16[512,256]{1,0:T(8,128)(2,1)S(1)} %pad_maximum_fusion.kv0), channel_id=1, source_target_pairs={{0,8},{1,9},{2,10},{3,11},{4,12},{5,13},{6,14},{7,15},{8,0},{9,1},... | collective-permute-start | bytes 786440 | tf_op jit(solution)/shard_map/ppermute | solution.py:363
  21.2 1.9 %collective-permute-start.5 = (bf16[512,256]{1,0:T(8,128)(2,1)S(1)}, bf16[512,256]{1,0:T(8,128)(2,1)S(1)}, u32[]{:S(2)}, u32[]{:S(2)}) collective-permute-start(bf16[512,256]{1,0:T(8,128)(2,1)S(1)} %collective-permute-done.4.kv2), channel_id=1, source_target_pairs={{0,8},{1,9},{2,10},{3,11},{4,12},{5,13},{6,14},{7,15},{8,0},{9,1},... | collective-permute-start | bytes 786440 | tf_op jit(solution)/shard_map/ppermute | solution.py:363
  25.9 4.8 %collective-permute-start.6 = (bf16[512,128]{1,0:T(8,128)(2,1)S(1)}, bf16[512,128]{1,0:T(8,128)(2,1)S(1)}, u32[]{:S(2)}, u32[]{:S(2)}) collective-permute-start(bf16[512,128]{1,0:T(8,128)(2,1)S(1)} %low.1), channel_id=1, source_target_pairs={{0,1},{1,0},{2,3},{3,2},{4,5},{5,4},{6,7},{7,6},{8,9},{9,8},{10,11... | collective-permute-start | bytes 393224 | tf_op jit(solution)/shard_map/ppermute | solution.py:363
  30.7 5.4 %collective-permute-start.9 = (bf16[512,128]{1,0:T(8,128)(2,1)S(1)}, bf16[512,128]{1,0:T(8,128)(2,1)S(1)}, u32[]{:S(2)}, u32[]{:S(2)}) collective-permute-start(bf16[512,128]{1,0:T(8,128)(2,1)S(1)} %add_convert_fusion.2), channel_id=1, source_target_pairs={{0,4},{1,5},{2,6},{3,7},{4,0},{5,1},{6,2},{7,3},{8,40},{9,41},{10,... | collective-permute-start | bytes 393224 | tf_op jit(solution)/shard_map/ppermute | solution.py:363
  32.8 5.3 %collective-permute-start.8 = (bf16[512,128]{1,0:T(8,128)(2,1)S(1)}, bf16[512,128]{1,0:T(8,128)(2,1)S(1)}, u32[]{:S(2)}, u32[]{:S(2)}) collective-permute-start(bf16[512,128]{1,0:T(8,128)(2,1)S(1)} %add_convert_fusion.2), channel_id=1, source_target_pairs={{0,6},{1,7},{2,4},{3,5},{4,2},{5,3},{6,0},{7,1},{8,56},{9,57},{10,... | collective-permute-start | bytes 393224 | tf_op jit(solution)/shard_map/ppermute | solution.py:363
  35.1 3.8 %collective-permute-start.7 = (bf16[512,128]{1,0:T(8,128)(2,1)S(1)}, bf16[512,128]{1,0:T(8,128)(2,1)S(1)}, u32[]{:S(2)}, u32[]{:S(2)}) collective-permute-start(bf16[512,128]{1,0:T(8,128)(2,1)S(1)} %add_convert_fusion.2), channel_id=1, source_target_pairs={{0,2},{1,3},{2,0},{3,1},{4,6},{5,7},{6,4},{7,5},{8,24},{9,25},{10,... | collective-permute-start | bytes 393224 | tf_op jit(solution)/shard_map/ppermute | solution.py:363
  39.0 5.6 %collective-permute-start.12 = (bf16[512,128]{1,0:T(8,128)(2,1)S(1)}, bf16[512,128]{1,0:T(8,128)(2,1)S(1)}, u32[]{:S(2)}, u32[]{:S(2)}) collective-permute-start(bf16[512,128]{1,0:T(8,128)(2,1)S(1)} %add_convert_fusion.1), channel_id=1, source_target_pairs={{0,32},{1,33},{2,34},{3,35},{4,36},{5,37},{6,38},{7,39},{8,12},{9,... | collective-permute-start | bytes 393224 | tf_op jit(solution)/shard_map/ppermute | solution.py:363
  42.2 5.3 %collective-permute-start.11 = (bf16[512,128]{1,0:T(8,128)(2,1)S(1)}, bf16[512,128]{1,0:T(8,128)(2,1)S(1)}, u32[]{:S(2)}, u32[]{:S(2)}) collective-permute-start(bf16[512,128]{1,0:T(8,128)(2,1)S(1)} %add_convert_fusion.1), channel_id=1, source_target_pairs={{0,48},{1,49},{2,50},{3,51},{4,52},{5,53},{6,54},{7,55},{8,14},{9,... | collective-permute-start | bytes 393224 | tf_op jit(solution)/shard_map/ppermute | solution.py:363
  43.0 4.5 %collective-permute-start.10 = (bf16[512,128]{1,0:T(8,128)(2,1)S(1)}, bf16[512,128]{1,0:T(8,128)(2,1)S(1)}, u32[]{:S(2)}, u32[]{:S(2)}) collective-permute-start(bf16[512,128]{1,0:T(8,128)(2,1)S(1)} %add_convert_fusion.1), channel_id=1, source_target_pairs={{0,16},{1,17},{2,18},{3,19},{4,20},{5,21},{6,22},{7,23},{8,10},{9,... | collective-permute-start | bytes 393224 | tf_op jit(solution)/shard_map/ppermute | solution.py:363
  47.6 6.6 %collective-permute-start.14 = (bf16[512,128]{1,0:T(8,128)(2,1)S(1)}, bf16[512,128]{1,0:T(8,128)(2,1)S(1)}, u32[]{:S(2)}, u32[]{:S(2)}) collective-permute-start(bf16[512,128]{1,0:T(8,128)(2,1)S(1)} %add_convert_fusion.lat0), channel_id=1, source_target_pairs={{0,65},{1,64},{2,67},{3,66},{4,69},{5,68},{6,71},{7,70},{8,73},{9,... | collective-permute-start | bytes 393224 | tf_op jit(solution)/shard_map/ppermute | solution.py:363
  50.2 7.5 %collective-permute-start.13 = (bf16[512,128]{1,0:T(8,128)(2,1)S(1)}, bf16[512,128]{1,0:T(8,128)(2,1)S(1)}, u32[]{:S(2)}, u32[]{:S(2)}) collective-permute-start(bf16[512,128]{1,0:T(8,128)(2,1)S(1)} %add_convert_fusion.lat0), channel_id=1, source_target_pairs={{0,8},{1,9},{2,10},{3,11},{4,12},{5,13},{6,14},{7,15},{8,0},{9,1},... | collective-permute-start | bytes 393224 | tf_op jit(solution)/shard_map/ppermute | solution.py:363
  54.2 4.4 %collective-permute-start.15 = (bf16[512,128]{1,0:T(8,128)(2,1)S(1)}, bf16[512,128]{1,0:T(8,128)(2,1)S(1)}, u32[]{:S(2)}, u32[]{:S(2)}) collective-permute-start(bf16[512,128]{1,0:T(8,128)(2,1)S(1)} %collective-permute-done.14.lat2), channel_id=1, source_target_pairs={{0,8},{1,9},{2,10},{3,11},{4,12},{5,13},{6,14},{7,15},{8,0},{9,1},... | collective-permute-start | bytes 393224 | tf_op jit(solution)/shard_map/ppermute | solution.py:363
